TPU v7x, 32 devices: a whole 2x2x4 slice. The times are simulated.
32 devices in a mesh: group: 2 (over x), lat: 16 (over z, y, core).
Axes of the slice: x: 2, y: 2, z: 4, core: 2. Of those that a mesh axis runs over, the one named last changes fastest.
Arguments:
- inputs: bfloat16 [64, 1440, 256], P(('group', 'lat')), parts along dimension 0, may hold values from -6 to 6
- cotangent: bfloat16 [64, 1440, 256], P(('group', 'lat')), parts along dimension 0, may hold values from -6 to 6
- weight: bfloat16 [9, 256, 256], replicated, may hold values from -0.125 to 0.125
- pat_rows: int32 [32, 9, 3], replicated, may hold values from -2 to 2, as said below
- pat_lons: int32 [32, 9, 3], replicated, may hold values from -12 to 12, as said below
- pat_vals: float32 [32, 9, 3], replicated, may hold values from 0.05 to 0.35
Outputs:
- mixed: bfloat16 [64, 1440, 256], P(('group', 'lat')), parts along dimension 0
- grad_input: bfloat16 [64, 1440, 256], P(('group', 'lat')), parts along dimension 0
- grad_weight: float32 [18, 256, 256], P('group'), parts along dimension 0
There are 2 independent parts, one for each index of `group`. A program takes and returns all parts, laid end to end along the dimension named above; an argument that names none is the same for every part. Nothing has to cross between parts.
Inputs may be any that keep to these rules, and one draw needn't show every extreme that they name: Every source row i + pat_rows lies in the grid. `pat_lons`: rows near either end of the grid reach farther in longitude.
All inputs are finite; a program needn't handle non-finite values.
Results may differ from a plain program's by a relative error of at most 0.005.
Values may be sent and summed in bfloat16 or wider, within the bound.
No kernel may reach another device: no remote copies, remote signals or barrier semaphores. Data moves between devices by JAX's collectives and lax.ppermute only.
A program may use at most 128 MiB of HBM per device.

v0:
```python
import math

import jax
import jax.numpy as jnp
from jax import lax
from jax.sharding import PartitionSpec as P

K = 9
H = 2
LMAX = 12


def extended(value, sides, width):
    for axis, dim in sides:
        size, length = (lax.axis_size(axis), value.shape[dim])
        up = [(i, (i + 1) % size) for i in range(size - 1)]
        down = [(j, i) for i, j in up]
        last = lax.slice_in_dim(value, length - width, length, axis=dim)
        leading = lax.slice_in_dim(value, 0, width, axis=dim)
        before = lax.ppermute(last, axis, up)
        after = lax.ppermute(leading, axis, down)
        value = jnp.concatenate([before, value, after], axis=dim)
    return value


def from_behind(block, axis, distance):
    devices = range(lax.axis_size(axis))
    route = [(i - distance, i) for i in devices if i - distance in devices]
    return lax.ppermute(block, axis, route)


def wrap_lons(field):
    return jnp.concatenate([field[..., -LMAX:, :], field, field[..., :LMAX, :]], axis=-2)


def flat_pattern(drows, dlons, values):
    count = drows.shape[0]
    return (
        jnp.moveaxis(drows, 1, 0).reshape(K * count, -1),
        jnp.moveaxis(dlons, 1, 0).reshape(K * count, -1),
        jnp.moveaxis(values, 1, 0).reshape(K * count, -1),
    )


def gather_terms(source, drows, dlons, values):
    count = drows.shape[0]
    width = source.shape[1]
    chan = source.shape[2]
    wide = wrap_lons(source)
    rows_flat, lons_flat, vals_flat = flat_pattern(drows, dlons, values)

    def per_item(items):
        slot, row_off, lon_off, weights = items
        line = slot % count + H
        total = jnp.zeros((width, chan), jnp.float32)
        for entry in range(row_off.shape[0]):
            piece = lax.dynamic_slice(
                wide, (line + row_off[entry], LMAX + lon_off[entry], 0), (1, width, chan)
            )[0]
            total = total + weights[entry] * piece.astype(jnp.float32)
        return total.astype(jnp.bfloat16)

    slots = jnp.arange(K * count, dtype=jnp.int32)
    basis = lax.map(per_item, (slots, rows_flat, lons_flat, vals_flat))
    return basis.reshape(K, count, width, chan)


def spread_terms(dbasis, drows, dlons, values, rows_out):
    width = dbasis.shape[2]
    chan = dbasis.shape[3]
    count = dbasis.shape[1]
    wide = wrap_lons(dbasis)
    entries = drows.shape[2]

    def per_source(line, accum):
        for basis_id in range(K):
            for entry in range(entries):
                target = line + H + drows[line, basis_id, entry]
                piece = lax.dynamic_slice(
                    wide,
                    (basis_id, line, LMAX - dlons[line, basis_id, entry], 0),
                    (1, 1, width, chan),
                )[0, 0]
                current = lax.dynamic_slice(accum, (target, 0, 0), (1, width, chan))[0]
                updated = current + values[line, basis_id, entry] * piece.astype(jnp.float32)
                accum = lax.dynamic_update_slice(accum, updated[None], (target, 0, 0))
        return accum

    start = jnp.zeros((rows_out, width, chan), jnp.float32)
    return lax.fori_loop(0, count, per_source, start)


def per_device(inputs, cotangent, weight, pat_rows, pat_lons, pat_vals):
    rows = inputs.shape[0]
    width = inputs.shape[1]
    first = lax.axis_index("lat") * rows
    margin = ((H, H), (0, 0), (0, 0))
    rows_all = jnp.pad(pat_rows, margin)
    lons_all = jnp.pad(pat_lons, margin)
    vals_all = jnp.pad(pat_vals, margin)
    own_rows = lax.dynamic_slice_in_dim(rows_all, first + H, rows, 0)
    own_lons = lax.dynamic_slice_in_dim(lons_all, first + H, rows, 0)
    own_vals = lax.dynamic_slice_in_dim(vals_all, first + H, rows, 0)
    source = extended(inputs, (("lat", 0),), H)
    basis = gather_terms(source, own_rows, own_lons, own_vals)
    mixed = jnp.einsum("krjc,kcd->rjd", basis, weight, preferred_element_type=jnp.float32).astype(
        jnp.bfloat16
    )
    partial_w = jnp.einsum("krjc,rjd->kcd", basis, cotangent, preferred_element_type=jnp.float32)
    total_w = lax.psum(partial_w, "lat")
    grad_weight = total_w * (1.0 / math.sqrt(pat_rows.shape[0] * width))
    dbasis = jnp.einsum(
        "rjd,kcd->krjc", cotangent, weight, preferred_element_type=jnp.float32
    ).astype(jnp.bfloat16)
    spread = spread_terms(dbasis, own_rows, own_lons, own_vals, rows + 2 * H)
    from_below = from_behind(spread[:H], "lat", -1)
    from_above = from_behind(spread[rows + H :], "lat", 1)
    grad = spread[H : H + rows]
    grad = grad.at[:H].add(from_above)
    grad = grad.at[rows - H :].add(from_below)
    return (mixed, grad.astype(jnp.bfloat16), grad_weight)


def solution(mesh):
    return jax.shard_map(
        per_device,
        mesh=mesh,
        in_specs=(
            P(("group", "lat"), None, None),
            P(("group", "lat"), None, None),
            P(),
            P(),
            P(),
            P(),
        ),
        out_specs=(
            P(("group", "lat"), None, None),
            P(("group", "lat"), None, None),
            P("group", None, None),
        ),
        check_vma=False,
    )
```

profile of v0, /device:TPU:0, one launch (start us, length us, event | category | flops | bytes accessed | tf_op | source)
XLA Modules:
  0.0 825.8 jit_solution(6824118883111189193)
XLA Ops:
  7.2 3.6 collective-permute-start
  14.6 8.0 fusion.28
  23.7 62.7 %concatenate.15 = bf16[9,2,1464,256]{3,2,1,0:T(8,128)(2,1)} concatenate(bf16[9,2,12,256]{3,2,1,0:T(8,128)(2,1)S(1)} %get-tuple-element.518, bf16[9,2,1440,256]{3,2,1,0:T(8,128)(2,1)} %fusion.28, bf16[9,2,12,256]{3,2,1,0:T(8,128)(2,1)S(1)} %get-tuple-element.517), dimensions={2} | concatenate | bytes 26984448 | tf_op jit(solution)/shard_map/concatenate | solution.py:33
  86.4 4.2 broadcast_in_dim.90
  90.5 297.4 %while.34 = (s32[]{:T(128)}, f32[6,1440,256]{2,1,0:T(8,128)}, s32[2,9,3]{1,0,2:T(2,128)S(1)}, f32[2,9,3]{1,0,2:T(2,128)S(1)}, s32[2,9,3]{1,0,2:T(2,128)S(1)}, /*...) while((s32[]{:T(128)}, f32[6,1440,256]{2,1,0:T(8,128)}, ...), condition=%wide.region_3.4_spmd, body=%wide.region_2.3_spmd.sunk | while | flops 29859972 | bytes 99563856 | solution.py:90
  94.0 3.6 fusion.78
  104.8 3.6 fusion.80
  110.3 3.6 fusion.81
  115.9 3.6 fusion.82
  126.6 3.6 fusion.84
  132.1 3.6 fusion.85
  137.6 3.6 fusion.86
  143.1 3.6 fusion.87
  159.5 3.6 fusion.90
  170.3 3.6 fusion.92
  192.0 3.6 fusion.96
  208.4 3.6 fusion.99
  213.9 3.6 fusion.100
  224.8 3.6 fusion.102
  242.7 3.6 fusion.78
  253.5 3.6 fusion.80
  259.0 3.6 fusion.81
  264.5 3.6 fusion.82
  275.2 3.6 fusion.84
  280.7 3.6 fusion.85
  286.3 3.6 fusion.86
  291.7 3.6 fusion.87
  297.2 3.6 fusion.88
  308.2 3.6 fusion.90
  318.8 3.6 fusion.92
  329.7 3.6 fusion.94
  335.1 3.6 fusion.95
  340.6 3.6 fusion.96
  351.4 3.6 fusion.98
  357.0 3.6 fusion.99
  362.6 3.6 fusion.100
  368.0 3.6 fusion.101
  373.5 3.6 fusion.102
  387.9 5.6 fusion.38
  393.5 5.9 collective-permute-start.2
  406.8 22.6 %concatenate.14 = bf16[6,1464,256]{2,1,0:T(8,128)(2,1)} concatenate(bf16[6,12,256]{2,1,0:T(8,128)(2,1)S(1)} %get-tuple-element.522, bf16[6,1440,256]{2,1,0:T(8,128)(2,1)} %copy-done.1, bf16[6,12,256]{2,1,0:T(8,128)(2,1)S(1)} %get-tuple-element.521), dimensions={1} | concatenate | bytes 8994816 | tf_op jit(solution)/shard_map/concatenate | solution.py:33
  429.4 270.4 %while.33 = (s32[]{:T(128)}, bf16[18,1440,256]{2,1,0:T(8,128)(2,1)}, f32[18,3]{1,0:T(8,128)S(1)}, s32[18]{0:T(128)S(1)}, s32[18,3]{1,0:T(8,128)S(1)}, /*index=5*...) while((s32[]{:T(128)}, ...), condition=%wide.region_1.2_spmd, body=%wide.region_0.1_spmd.sunk | while | flops 3317798 | bytes 2951878 | solution.py:64
  439.4 5.1 fusion.77
  454.5 5.2 fusion.77
  469.6 5.2 fusion.77
  484.7 5.1 fusion.77
  499.8 5.2 fusion.77
  514.9 5.0 fusion.77
  529.8 5.0 fusion.77
  544.8 5.1 fusion.77
  559.9 5.0 fusion.77
  574.8 5.1 fusion.77
  589.9 5.1 fusion.77
  605.0 5.0 fusion.77
  620.0 5.0 fusion.77
  634.9 5.0 fusion.77
  649.9 5.0 fusion.77
  664.8 5.0 fusion.77
  679.8 5.0 fusion.77
  694.7 5.1 fusion.77
  699.8 8.5 %convolution_bitcast_fusion.1 = f32[9,256,256]{2,1,0:T(8,128)} fusion(bf16[9,2,1440,256]{3,2,1,0:T(8,128)(2,1)} %bitcast.576, bf16[2,1440,256]{2,1,0:T(8,128)(2,1)S(1)} %copy-done), kind=kOutput, calls=%fused_computation.145 | convolution fusion | flops 3397386240 | bytes 17104896 | tf_op jit(solution)/shard_map/krjc,rjd->kcd/dot_general | solution.py:109
  709.6 9.5 %fusion.29 = bf16[2,1440,256]{2,1,0:T(8,128)(2,1)} fusion(bf16[9,2,1440,256]{3,2,1,0:T(8,128)(2,1)} %bitcast.577, bf16[9,256,256]{2,1,0:T(8,128)(2,1)S(1)} %copy-done.2), kind=kOutput, calls=%fused_computation.143 | convolution fusion | flops 3398123520 | bytes 15925248 | tf_op jit(solution)/shard_map/krjc,kcd->rjd/dot_general | solution.py:106
  719.1 91.5 %all-reduce.5.cloned.1.call-done = f32[9,256,256]{2,1,0:T(8,128)} async-done(((f32[9,256,256]{2,1,0:T(8,128)}), f32[9,256,256]{2,1,0:T(8,128)}) %all-reduce.5.cloned.1.call-update) | async-done | bytes 2359312 | tf_op jit(solution)/shard_map/psum | solution.py:110
  813.8 5.2 add_convert_fusion.1
  (173 shorter events, 136.5 us)
Async XLA Ops:
  7.2 7.4 copy-start
  7.2 803.3 %all-reduce.5.cloned.1.call-start = ((), (), s32[]{:S(2)}) async-start(), calls=%async_computation | async-start | bytes 4718592 | tf_op jit(solution)/shard_map/psum | solution.py:110
  7.2 394.0 %collective-permute-start = (bf16[2,1440,256]{2,1,0:T(8,128)(2,1)}, bf16[2,1440,256]{2,1,0:T(8,128)(2,1)}, u32[]{:S(2)}, u32[]{:S(2)}) collective-permute-start(bf16[2,1440,256]{2,1,0:T(8,128)(2,1)} %param.18), channel_id=1, source_target_pairs={{0,1},{1,2},{2,3},{3,4},{4,5},{5,6},{6,7},{7,8},{8,9},{9,10},{10,1... | collective-permute-start | bytes 4423688 | tf_op jit(solution)/shard_map/ppermute | solution.py:20
  10.9 392.3 %collective-permute-start.1 = (bf16[2,1440,256]{2,1,0:T(8,128)(2,1)}, bf16[2,1440,256]{2,1,0:T(8,128)(2,1)}, u32[]{:S(2)}, u32[]{:S(2)}) collective-permute-start(bf16[2,1440,256]{2,1,0:T(8,128)(2,1)} %param.18), channel_id=1, source_target_pairs={{1,0},{2,1},{3,2},{4,3},{5,4},{6,5},{7,6},{8,7},{9,8},{10,9},{11,1... | collective-permute-start | bytes 4423688 | tf_op jit(solution)/shard_map/ppermute | solution.py:21
  14.6 9.0 %copy-start.4 = (f32[32,9,3]{1,0,2:T(8,128)}, f32[32,9,3]{1,0,2:T(8,128)S(1)}, u32[]{:S(2)}) copy-start(f32[32,9,3]{1,0,2:T(8,128)S(1)} %copy.19) | copy-start | bytes 10372
  387.9 13.2 %copy-start.5 = (f32[32,9,3]{1,0,2:T(8,128)S(1)}, f32[32,9,3]{1,0,2:T(8,128)}, u32[]{:S(2)}) copy-start(f32[32,9,3]{1,0,2:T(8,128)} %copy-done.4) | copy-start | bytes 10372
  393.5 420.3 %collective-permute-start.2 = (f32[2,1440,256]{2,1,0:T(8,128)}, f32[2,1440,256]{2,1,0:T(8,128)}, u32[]{:S(2)}, u32[]{:S(2)}) collective-permute-start(f32[2,1440,256]{2,1,0:T(8,128)} %get-tuple-element.519), channel_id=1, source_target_pairs={{0,1},{1,2},{2,3},{3,4},{4,5},{5,6},{6,7},{7,8},{8,9},{9,10},{10,1... | collective-permute-start | bytes 8847368 | tf_op jit(solution)/shard_map/ppermute | solution.py:29
  399.4 414.4 %collective-permute-start.3 = (f32[2,1440,256]{2,1,0:T(8,128)}, f32[2,1440,256]{2,1,0:T(8,128)}, u32[]{:S(2)}, u32[]{:S(2)}) collective-permute-start(f32[2,1440,256]{2,1,0:T(8,128)} %get-tuple-element.520), channel_id=1, source_target_pairs={{1,0},{2,1},{3,2},{4,3},{5,4},{6,5},{7,6},{8,7},{9,8},{10,9},{11,1... | collective-permute-start | bytes 8847368 | tf_op jit(solution)/shard_map/ppermute | solution.py:29
  401.2 1.8 copy-start.3
  404.6 2.1 copy-start.1
  708.3 1.3 copy-start.2
Sparse Core Ops, SparseCore 0:
  708.4 102.0 all-reduce.4
where the time goes:
time: 835 us; the launch traced here: 826 us
  other arithmetic  293 us (35%)
  loops' own time  238 us (29%)
  local copies, waits for them, and re-layouts  151 us (18%)
  waiting for transfers between devices  91.5 us (11%)
  matrix products  26 us (3%)
  between operations  14.2 us (2%)
  starting transfers between devices  12.3 us (1%)
    dynamic_update_slice x54, other arithmetic, per_source(): accum = lax.dynamic_update_slice(accum, updated[None], (target, 0, 0))  193 us
    another operation x1, loops' own time, gather_terms(): basis = lax.map(per_item, (slots, rows_flat, lons_flat, vals_flat))  137 us
    another operation x1, loops' own time, spread_terms(): return lax.fori_loop(0, count, per_source, start)  101 us
    psum x1, waiting for transfers between devices, per_device(): total_w = lax.psum(partial_w, 'lat')  91.5 us
    dynamic_update_slice x18, other arithmetic, gather_terms(): basis = lax.map(per_item, (slots, rows_flat, lons_flat, vals_flat))  91.3 us
    concatenate x2, local copies, waits for them, and re-layouts, wrap_lons(): jnp.concatenate([field[..., -LMAX:, :], field, field[..., :LMAX, :]], axi...  85.3 us
  transfers between devices with their start and end apart: 5, of which 1 were waited for; matrix products, arithmetic and copies ran while one was open for 56% of the time, Pallas kernels for 0%

commit v1 on v0

v1 whole, which is shorter than its diff:
```python
import math

import jax
import jax.numpy as jnp
from jax import lax
from jax.experimental import pallas as pl
from jax.experimental.pallas import tpu as pltpu
from jax.sharding import PartitionSpec as P

H = 2
PAD = 16
GROUP = 4


def fwd_kernel(prow, plon, pval, own, above, below, cot, weight, mixed, gw, xf, basis, cott):
    rows, width, chan = own.shape
    nk = weight.shape[0]
    ne = prow.shape[0] // (rows * nk)
    half = 128
    nh = chan // half

    def widen(src, r, dst):
        for h in range(nh):
            cols = slice(h * half, (h + 1) * half)
            xf[dst, h, PAD : PAD + width] = src[r, :, cols].astype(jnp.float32)
            xf[dst, h, 0:PAD] = src[r, width - PAD : width, cols].astype(jnp.float32)
            xf[dst, h, PAD + width :] = src[r, 0:PAD, cols].astype(jnp.float32)

    for r in range(H):
        widen(above, r, r)
        widen(below, r, H + rows + r)
    for r in range(rows):
        widen(own, r, H + r)
    wall = weight[...].reshape(nk * chan, chan)
    for i in range(rows):
        cott[...] = cot[i].T

        def per_k(k, carry):
            vs = [pval[(i * nk + k) * ne + e] for e in range(ne)]
            rs = [i + H + prow[(i * nk + k) * ne + e] for e in range(ne)]
            os = [PAD + plon[(i * nk + k) * ne + e] for e in range(ne)]
            for h in range(nh):
                t = vs[0] * xf[rs[0], h, pl.ds(os[0], width), :]
                for e in range(1, ne):
                    t = t + vs[e] * xf[rs[e], h, pl.ds(os[e], width), :]
                basis[k, :, h * half : (h + 1) * half] = t.astype(jnp.bfloat16)
            return carry

        lax.fori_loop(0, nk, per_k, 0)
        tile = width // 3
        for t in range(3):
            sl = slice(t * tile, (t + 1) * tile)
            acc = jnp.dot(basis[0, sl], weight[0], preferred_element_type=jnp.float32)
            for k in range(1, nk):
                acc = acc + jnp.dot(basis[k, sl], weight[k], preferred_element_type=jnp.float32)
            mixed[i, sl] = acc.astype(jnp.bfloat16)
        for k in range(nk):
            p = jnp.dot(cott[...], basis[k], preferred_element_type=jnp.float32)
            if i == 0:
                gw[k] = p
            else:
                gw[k] = gw[k] + p
    for k in range(nk):
        gw[k] = gw[k].T


def forward(prow, plon, pval, own, above, below, cot, weight):
    rows, width, chan = own.shape
    nk = weight.shape[0]
    smem = pl.BlockSpec(memory_space=pltpu.SMEM)
    vmem = pl.BlockSpec(memory_space=pltpu.VMEM)
    return pl.pallas_call(
        fwd_kernel,
        in_specs=[smem] * 3 + [vmem] * 5,
        out_specs=[vmem] * 2,
        out_shape=[
            jax.ShapeDtypeStruct((rows, width, chan), jnp.bfloat16),
            jax.ShapeDtypeStruct((nk, chan, chan), jnp.float32),
        ],
        scratch_shapes=[
            pltpu.VMEM((rows + 2 * H, chan // 128, width + 2 * PAD, 128), jnp.float32),
            pltpu.VMEM((nk, width, chan), jnp.bfloat16),
            pltpu.VMEM((chan, width), jnp.bfloat16),
        ],
        compiler_params=pltpu.CompilerParams(vmem_limit_bytes=56 * 2**20),
        name="forward",
    )(prow, plon, pval, own, above, below, cot, weight)


def bwd_kernel(prow, plon, pval, cot, weight, own, above, below, db, acc, cnt, lst_n, lst_o, lst_v):
    rows, width, chan = cot.shape
    nk = weight.shape[0]
    ne = prow.shape[0] // (rows * nk)
    half = 128
    nh = chan // half
    lines = rows + 2 * H
    cap = rows * nk * ne + GROUP

    for t in range(lines):
        cnt[t] = 0

    def bin_one(n, carry):
        i = n // nk
        k = n - i * nk
        for e in range(ne):
            t = i + H + prow[(i * nk + k) * ne + e]
            c = cnt[t]
            lst_n[t * cap + c] = n
            lst_o[t * cap + c] = PAD - plon[(i * nk + k) * ne + e]
            lst_v[t * cap + c] = pval[(i * nk + k) * ne + e]
            cnt[t] = c + 1
        return carry

    lax.fori_loop(0, rows * nk, bin_one, 0)
    for t in range(lines):
        c = cnt[t]
        for g in range(GROUP - 1):
            lst_n[t * cap + c + g] = 0
            lst_o[t * cap + c + g] = PAD
            lst_v[t * cap + c + g] = 0.0

    for i in range(rows):
        def per_k(k, carry):
            n = i * nk + k
            d = lax.dot_general(cot[i], weight[k], (((1,), (1,)), ((), ())), preferred_element_type=jnp.float32)
            for h in range(nh):
                cols = slice(h * half, (h + 1) * half)
                db[n, h, PAD : PAD + width] = d[:, cols]
                db[n, h, 0:PAD] = d[width - PAD :, cols]
                db[n, h, PAD + width :] = d[0:PAD, cols]
            return carry

        lax.fori_loop(0, nk, per_k, 0)

    for t in range(lines):
        for h in range(nh):
            acc[h] = jnp.zeros((width, half), jnp.float32)

        def group(g, carry):
            at = t * cap + g * GROUP
            ns = [lst_n[at + j] for j in range(GROUP)]
            os = [lst_o[at + j] for j in range(GROUP)]
            vs = [lst_v[at + j] for j in range(GROUP)]
            for h in range(nh):
                s = vs[0] * db[ns[0], h, pl.ds(os[0], width), :]
                for j in range(1, GROUP):
                    s = s + vs[j] * db[ns[j], h, pl.ds(os[j], width), :]
                acc[h] = acc[h] + s
            return carry

        lax.fori_loop(0, (cnt[t] + GROUP - 1) // GROUP, group, 0)
        dst = above if t < H else (own if t < H + rows else below)
        r = t if t < H else (t - H if t < H + rows else t - H - rows)
        for h in range(nh):
            dst[r, :, h * half : (h + 1) * half] = acc[h].astype(dst.dtype)


def backward(prow, plon, pval, cot, weight):
    rows, width, chan = cot.shape
    nk = weight.shape[0]
    ne = prow.shape[0] // (rows * nk)
    smem = pl.BlockSpec(memory_space=pltpu.SMEM)
    vmem = pl.BlockSpec(memory_space=pltpu.VMEM)
    lines = rows + 2 * H
    cap = rows * nk * ne + GROUP
    return pl.pallas_call(
        bwd_kernel,
        in_specs=[smem] * 3 + [vmem] * 2,
        out_specs=[vmem] * 3,
        out_shape=[
            jax.ShapeDtypeStruct((rows, width, chan), jnp.float32),
            jax.ShapeDtypeStruct((H, width, chan), jnp.bfloat16),
            jax.ShapeDtypeStruct((H, width, chan), jnp.bfloat16),
        ],
        scratch_shapes=[
            pltpu.VMEM((rows * nk, chan // 128, width + 2 * PAD, 128), jnp.float32),
            pltpu.VMEM((chan // 128, width, 128), jnp.float32),
            pltpu.SMEM((lines,), jnp.int32),
            pltpu.SMEM((lines * cap,), jnp.int32),
            pltpu.SMEM((lines * cap,), jnp.int32),
            pltpu.SMEM((lines * cap,), jnp.float32),
        ],
        compiler_params=pltpu.CompilerParams(vmem_limit_bytes=56 * 2**20),
        name="backward",
    )(prow, plon, pval, cot, weight)


def sum_over_lat(value):
    size = lax.axis_size("lat")
    shape = value.shape
    value = value.reshape(-1, shape[-1])
    if size & (size - 1) or value.shape[0] % size:
        return lax.psum(value, "lat").reshape(shape)
    index = lax.axis_index("lat")
    bits = [1 << b for b in range(size.bit_length() - 1)]
    for bit in bits:
        side = (index // bit) % 2
        count = value.shape[0] // 2
        keep = lax.dynamic_slice_in_dim(value, side * count, count, 0)
        send = lax.dynamic_slice_in_dim(value, (1 - side) * count, count, 0).astype(jnp.bfloat16)
        got = lax.ppermute(send, "lat", [(i, i ^ bit) for i in range(size)])
        value = keep + got.astype(jnp.float32)
    value = value.astype(jnp.bfloat16)
    for bit in reversed(bits):
        side = (index // bit) % 2
        got = lax.ppermute(value, "lat", [(i, i ^ bit) for i in range(size)])
        value = jnp.where(
            side == 0, jnp.concatenate([value, got]), jnp.concatenate([got, value])
        )
    return value.reshape(shape)


def per_device(inputs, cotangent, weight, pat_rows, pat_lons, pat_vals):
    rows = inputs.shape[0]
    width = inputs.shape[1]
    size = lax.axis_size("lat")
    up = [(i, i + 1) for i in range(size - 1)]
    down = [(i + 1, i) for i in range(size - 1)]
    first = lax.axis_index("lat") * rows
    pattern = [
        lax.dynamic_slice_in_dim(table, first, rows, 0).reshape(-1)
        for table in (pat_rows, pat_lons, pat_vals)
    ]
    above = lax.ppermute(inputs[rows - H :], "lat", up)
    below = lax.ppermute(inputs[:H], "lat", down)
    grad, to_above, to_below = backward(*pattern, cotangent, weight)
    from_above = lax.ppermute(to_below, "lat", up)
    from_below = lax.ppermute(to_above, "lat", down)
    above, below, to_below, to_above = lax.optimization_barrier((above, below, to_below, to_above))
    mixed, partial_w = forward(*pattern, inputs, above, below, cotangent, weight)
    total_w = sum_over_lat(partial_w)
    grad_weight = total_w.astype(jnp.float32) * (1.0 / math.sqrt(pat_rows.shape[0] * width))
    grad = grad.at[:H].add(from_above.astype(jnp.float32))
    grad = grad.at[rows - H :].add(from_below.astype(jnp.float32))
    return (mixed, grad.astype(jnp.bfloat16), grad_weight)


def solution(mesh):
    return jax.shard_map(
        per_device,
        mesh=mesh,
        in_specs=(
            P(("group", "lat"), None, None),
            P(("group", "lat"), None, None),
            P(),
            P(),
            P(),
            P(),
        ),
        out_specs=(
            P(("group", "lat"), None, None),
            P(("group", "lat"), None, None),
            P("group", None, None),
        ),
        check_vma=False,
    )
```

time: 835 us -> 134 us (0.16); the launches traced: 826 us -> 133 us
  other arithmetic: 293 us -> 10.4 us
  loops' own time: 238 us -> 0 us
  local copies, waits for them, and re-layouts: 151 us -> 7.24 us
  waiting for transfers between devices: 91.5 us -> 47.2 us
  Pallas kernels: 0 us -> 42.8 us
  matrix products: 26 us -> 0 us
  between operations: 14.2 us -> 0.88 us
  starting transfers between devices: 12.3 us -> 24.7 us
    dynamic_update_slice x72 -> x0, other arithmetic: 284 us -> none  [the longest x54 193 us: per_source(): accum = lax.dynamic_update_slice(accum, updated[None], (target, 0, 0))]
    another operation x2 -> x0, loops' own time: 238 us -> none  [the longest x1 137 us: gather_terms(): basis = lax.map(per_item, (slots, rows_flat, lons_flat, vals_flat))]
    psum x1 -> x0, waiting for transfers between devices: 91.5 us -> none  [per_device(): total_w = lax.psum(partial_w, 'lat')]
    concatenate x3 -> x0, local copies, waits for them, and re-layouts: 86.8 us -> none  [the longest x2 85.3 us: wrap_lons(): jnp.concatenate([field[..., -LMAX:, :], field, field[..., :LMAX, :]], axi...]
    ppermute x4 -> x12, waiting for transfers between devices: 0.01 us -> 47.2 us  [the longest x4 29.4 us: sum_over_lat(): got = lax.ppermute(send, 'lat', [(i, i ^ bit) for i in range(size)])]
    pallas_call x0 -> x2, Pallas kernels: none -> 42.8 us  [the longest x1 22.7 us: backward(): pl.pallas_call(bwd_kernel, in_specs=[smem] * 3 + [vmem] * 2, out_specs=[v...]
    slice x57 -> x0, local copies, waits for them, and re-layouts: 38.1 us -> none  [the longest x18 10.5 us: per_item(): total = total + weights[entry] * piece.astype(jnp.float32)]
    dot_general x3 -> x0, matrix products: 26 us -> none  [the longest x1 9.5 us: per_device(): jnp.einsum('krjc,kcd->rjd', basis, weight, preferred_element_type=jnp.flo...]
  transfers between devices with their start and end apart: 5 -> 12, of which waited for: 1 -> 7; matrix products, arithmetic and copies ran while one was open for 56% -> 8% of each run, Pallas kernels for 0% -> 17%
where the time goes in v1:
time: 134 us; the launch traced here: 133 us
  waiting for transfers between devices  47.2 us (35%)
  Pallas kernels  42.8 us (32%)
  starting transfers between devices  24.7 us (18%)
  other arithmetic  10.4 us (8%)
  local copies, waits for them, and re-layouts  7.24 us (5%)
    ppermute x4, waiting for transfers between devices, sum_over_lat(): got = lax.ppermute(send, 'lat', [(i, i ^ bit) for i in range(size)])  29.4 us
    pallas_call x1, Pallas kernels, backward(): pl.pallas_call(bwd_kernel, in_specs=[smem] * 3 + [vmem] * 2, out_specs=[v...  22.7 us
    pallas_call x1, Pallas kernels, forward(): pl.pallas_call(fwd_kernel, in_specs=[smem] * 3 + [vmem] * 5, out_specs=[v...  20.2 us
    ppermute x4, waiting for transfers between devices, sum_over_lat(): got = lax.ppermute(value, 'lat', [(i, i ^ bit) for i in range(size)])  17.8 us
    ppermute x4, starting transfers between devices, sum_over_lat(): got = lax.ppermute(send, 'lat', [(i, i ^ bit) for i in range(size)])  16.9 us
    convert_element_type x1, other arithmetic, per_device(): return (mixed, grad.astype(jnp.bfloat16), grad_weight)  3.55 us
    add x3, other arithmetic, sum_over_lat(): value = keep + got.astype(jnp.float32)  2.72 us
  transfers between devices with their start and end apart: 12, of which 7 were waited for; matrix products, arithmetic and copies ran while one was open for 8% of the time, Pallas kernels for 17%

profile of v1, /device:TPU:0, one launch (start us, length us, event | category | flops | bytes accessed | tf_op | source)
XLA Modules:
  0.0 133.3 jit_solution(17776708157875671118)
XLA Ops:
  0.6 0.0 copy-start
  0.6 2.5 %collective-permute-start = (bf16[2,1440,256]{2,1,0:T(8,128)(2,1)}, bf16[2,1440,256]{2,1,0:T(8,128)(2,1)S(1)}, u32[]{:S(2)}, u32[]{:S(2)}) collective-permute-start(bf16[2,1440,256]{2,1,0:T(8,128)(2,1)} %own.1), channel_id=1, source_target_pairs={{0,1},{1,2},{2,3},{3,4},{4,5},{5,6},{6,7},{7,8},{8,9},{9,10},{10,1... | collective-permute-start | bytes 4423688 | tf_op jit(solution)/shard_map/ppermute | solution.py:224
  3.1 1.3 collective-permute-start.1
  4.4 0.8 constant_dynamic-slice_fusion.1
  5.2 0.2 copy.12
  5.4 0.6 reshape.90.prow
  6.0 0.2 copy.13
  6.2 0.7 reshape.91.plon
  6.9 0.0 copy-done
  6.9 0.1 constant_dynamic-slice_fusion
  7.0 0.2 copy.14
  7.1 0.7 reshape.92.pval
  7.8 22.7 %backward.1 = (f32[2,1440,256]{2,1,0:T(8,128)}, bf16[2,1440,256]{2,1,0:T(8,128)(2,1)}, bf16[2,1440,256]{2,1,0:T(8,128)(2,1)}) custom-call(s32[54]{0:T(128)} %reshape.90.prow, s32[54]{0:T(128)} %reshape.91.plon, f32[54]{0:T(128)} %reshape.92.pval, bf16[2,1440,256]{2,1,0:T(8,128)(2,1)} %cot.3, bf16[9,256,256]{2,1,0:T(8,128)(2,1)} %weight.3), custom_call_target="tpu_custom_call" | custom-call | tf_op jit(solution)/shard_map/backward/pallas_call | solution.py:166
  30.5 0.0 collective-permute-done.above
  30.5 0.0 copy-start.3
  30.5 0.0 collective-permute-done.1.below
  30.5 0.0 copy-start.4
  30.5 1.1 copy-done.3
  31.6 0.5 copy-done.4
  32.1 20.2 %forward.1 = (bf16[2,1440,256]{2,1,0:T(8,128)(2,1)}, f32[9,256,256]{2,1,0:T(8,128)}) custom-call(s32[54]{0:T(128)} %reshape.90.prow, s32[54]{0:T(128)} %reshape.91.plon, f32[54]{0:T(128)} %reshape.92.pval, bf16[2,1440,256]{2,1,0:T(8,128)(2,1)} %own.1, bf16[2,1440,256]{2,1,0:T(8,128)(2,1)} %copy-done.3, bf16[2,1440,256]{2,1,0:T(8,128)(2,1)} %copy-done.4, ...), custom_call_target="tpu_custom_call" | custom-call | tf_op jit(solution)/shard_map/forward/pallas_call | solution.py:72
  52.3 1.3 dynamic-slice_convert_fusion
  53.6 7.5 %collective-permute-start.4 = (bf16[1152,256]{1,0:T(8,128)(2,1)S(1)}, bf16[1152,256]{1,0:T(8,128)(2,1)S(1)}, u32[]{:S(2)}, u32[]{:S(2)}) collective-permute-start(bf16[1152,256]{1,0:T(8,128)(2,1)S(1)} %dynamic-slice_convert_fusion), channel_id=1, source_target_pairs={{0,1},{1,0},{2,3},{3,2},{4,5},{5,4},{6,7},{7,6},{8,9},{9,8},{10,11... | collective-permute-start | bytes 1769480 | tf_op jit(solution)/shard_map/ppermute | solution.py:201
  61.1 1.6 %collective-permute-done.4 = bf16[1152,256]{1,0:T(8,128)(2,1)S(1)} collective-permute-done((bf16[1152,256]{1,0:T(8,128)(2,1)S(1)}, bf16[1152,256]{1,0:T(8,128)(2,1)S(1)}, u32[]{:S(2)}, u32[]{:S(2)}) %collective-permute-start.4) | collective-permute-done | bytes 589856 | tf_op jit(solution)/shard_map/ppermute | solution.py:201
  62.8 1.4 %convert_add_fusion = f32[1152,256]{1,0:T(8,128)S(1)} fusion(bf16[1152,256]{1,0:T(8,128)(2,1)S(1)} %collective-permute-done.4, f32[2304,256]{1,0:T(8,128)} %bitcast.4, s32[]{:T(128)S(6)} %select_n.117), kind=kLoop, calls=%fused_computation.3 | loop fusion | flops 589824 | bytes 2949124 | tf_op jit(solution)/shard_map/add | solution.py:202
  64.2 2.9 %collective-permute-start.5 = (bf16[576,256]{1,0:T(8,128)(2,1)S(1)}, bf16[576,256]{1,0:T(8,128)(2,1)S(1)}, u32[]{:S(2)}, u32[]{:S(2)}) collective-permute-start(bf16[576,256]{1,0:T(8,128)(2,1)S(1)} %dynamic-slice_convert_fusion.1), channel_id=1, source_target_pairs={{0,2},{1,3},{2,0},{3,1},{4,6},{5,7},{6,4},{7,5},{8,10},{9,11},{10,... | collective-permute-start | bytes 884744 | tf_op jit(solution)/shard_map/ppermute | solution.py:201
  67.1 7.3 %collective-permute-done.5 = bf16[576,256]{1,0:T(8,128)(2,1)S(1)} collective-permute-done((bf16[576,256]{1,0:T(8,128)(2,1)S(1)}, bf16[576,256]{1,0:T(8,128)(2,1)S(1)}, u32[]{:S(2)}, u32[]{:S(2)}) %collective-permute-start.5) | collective-permute-done | bytes 294944 | tf_op jit(solution)/shard_map/ppermute | solution.py:201
  74.4 0.1 convert_add_fusion.1
  74.5 0.0 copy-start.2
  74.5 0.8 copy-done.2
  75.3 1.1 collective-permute-start.6
  76.4 2.5 %collective-permute-start.2 = (bf16[2,1440,256]{2,1,0:T(8,128)(2,1)}, bf16[2,1440,256]{2,1,0:T(8,128)(2,1)}, u32[]{:S(2)}, u32[]{:S(2)}) collective-permute-start(bf16[2,1440,256]{2,1,0:T(8,128)(2,1)} %get-tuple-element.50), channel_id=1, source_target_pairs={{0,1},{1,2},{2,3},{3,4},{4,5},{5,6},{6,7},{7,8},{8,9},{9,10},{10,1... | collective-permute-start | bytes 4423688 | tf_op jit(solution)/shard_map/ppermute | solution.py:227
  79.0 1.3 collective-permute-start.3
  80.3 0.0 copy-start.1
  80.3 0.5 collective-permute-done.6
  80.8 1.2 convert_add_fusion.2
  82.1 5.4 %collective-permute-start.7 = (bf16[144,256]{1,0:T(8,128)(2,1)S(1)}, bf16[144,256]{1,0:T(8,128)(2,1)S(1)}, u32[]{:S(2)}, u32[]{:S(2)}) collective-permute-start(bf16[144,256]{1,0:T(8,128)(2,1)S(1)} %dynamic-slice_convert_fusion.3), channel_id=1, source_target_pairs={{0,8},{1,9},{2,10},{3,11},{4,12},{5,13},{6,14},{7,15},{8,0},{9,1},... | collective-permute-start | bytes 221192 | tf_op jit(solution)/shard_map/ppermute | solution.py:201
  87.4 20.0 %collective-permute-done.7 = bf16[144,256]{1,0:T(8,128)(2,1)S(1)} collective-permute-done((bf16[144,256]{1,0:T(8,128)(2,1)S(1)}, bf16[144,256]{1,0:T(8,128)(2,1)S(1)}, u32[]{:S(2)}, u32[]{:S(2)}) %collective-permute-start.7) | collective-permute-done | bytes 73760 | tf_op jit(solution)/shard_map/ppermute | solution.py:201
  107.4 0.1 collective-permute-start.8
  107.5 5.8 %collective-permute-done.8 = bf16[144,256]{1,0:T(8,128)(2,1)S(1)} collective-permute-done((bf16[144,256]{1,0:T(8,128)(2,1)S(1)}, bf16[144,256]{1,0:T(8,128)(2,1)S(1)}, u32[]{:S(2)}, u32[]{:S(2)}) %collective-permute-start.8) | collective-permute-done | bytes 73760 | tf_op jit(solution)/shard_map/ppermute | solution.py:206
  113.3 0.1 collective-permute-start.9
  113.4 5.2 %collective-permute-done.9 = bf16[288,256]{1,0:T(8,128)(2,1)} collective-permute-done((bf16[288,256]{1,0:T(8,128)(2,1)S(1)}, bf16[288,256]{1,0:T(8,128)(2,1)}, u32[]{:S(2)}, u32[]{:S(2)}) %collective-permute-start.9) | collective-permute-done | bytes 147488 | tf_op jit(solution)/shard_map/ppermute | solution.py:206
  118.6 1.1 maximum_select_fusion.2
  119.7 0.1 collective-permute-start.10
  119.8 6.8 %collective-permute-done.10 = bf16[576,256]{1,0:T(8,128)(2,1)} collective-permute-done((bf16[576,256]{1,0:T(8,128)(2,1)S(1)}, bf16[576,256]{1,0:T(8,128)(2,1)}, u32[]{:S(2)}, u32[]{:S(2)}) %collective-permute-start.10) | collective-permute-done | bytes 294944 | tf_op jit(solution)/shard_map/ppermute | solution.py:206
  126.6 1.3 maximum_select_fusion.1
  127.9 0.1 collective-permute-start.11
  128.0 0.0 collective-permute-done.2
  128.0 0.0 collective-permute-done.3
  128.0 0.0 copy-done.1
  128.0 3.5 %add_convert_fusion = bf16[2,1440,256]{2,1,0:T(8,128)(2,1)} fusion(bf16[2,1440,256]{2,1,0:T(8,128)(2,1)} %collective-permute-done.3, f32[2,1440,256]{2,1,0:T(8,128)S(1)} %copy-done.1, bf16[2,1440,256]{2,1,0:T(8,128)(2,1)} %collective-permute-done.2), kind=kLoop, calls=%fused_computation | loop fusion | flops 3686400 | bytes 7372800 | tf_op jit(solution)/shard_map/convert_element_type | solution.py:235
  131.6 0.0 collective-permute-done.11
  131.6 1.7 %convert_multiply_fusion = f32[2304,256]{1,0:T(8,128)} fusion(bf16[1152,256]{1,0:T(8,128)(2,1)S(1)} %collective-permute-done.11, bf16[1152,256]{1,0:T(8,128)(2,1)S(1)} %maximum_select_fusion.1, pred[]{:T(512)S(6)} %eq.21), kind=kLoop, calls=%fused_computation.1 | loop fusion | flops 6488064 | bytes 3538945 | tf_op jit(solution)/shard_map/mul | solution.py:232
  (5 shorter events, 0.1 us)
Async XLA Ops:
  0.6 6.3 %copy-start = (f32[32,9,3]{0,2,1:T(4,128)S(1)}, f32[32,9,3]{0,2,1:T(4,128)}, u32[]{:S(2)}) copy-start(f32[32,9,3]{0,2,1:T(4,128)} %param.19) | copy-start | bytes 10372
  0.6 29.9 %collective-permute-start = (bf16[2,1440,256]{2,1,0:T(8,128)(2,1)}, bf16[2,1440,256]{2,1,0:T(8,128)(2,1)S(1)}, u32[]{:S(2)}, u32[]{:S(2)}) collective-permute-start(bf16[2,1440,256]{2,1,0:T(8,128)(2,1)} %own.1), channel_id=1, source_target_pairs={{0,1},{1,2},{2,3},{3,4},{4,5},{5,6},{6,7},{7,8},{8,9},{9,10},{10,1... | collective-permute-start | bytes 4423688 | tf_op jit(solution)/shard_map/ppermute | solution.py:224
  3.1 27.4 %collective-permute-start.1 = (bf16[2,1440,256]{2,1,0:T(8,128)(2,1)}, bf16[2,1440,256]{2,1,0:T(8,128)(2,1)S(1)}, u32[]{:S(2)}, u32[]{:S(2)}) collective-permute-start(bf16[2,1440,256]{2,1,0:T(8,128)(2,1)} %own.1), channel_id=1, source_target_pairs={{1,0},{2,1},{3,2},{4,3},{5,4},{6,5},{7,6},{8,7},{9,8},{10,9},{11,1... | collective-permute-start | bytes 4423688 | tf_op jit(solution)/shard_map/ppermute | solution.py:225
  30.5 1.1 copy-start.3
  30.5 1.6 %copy-start.4 = (bf16[2,1440,256]{2,1,0:T(8,128)(2,1)}, bf16[2,1440,256]{2,1,0:T(8,128)(2,1)S(1)}, u32[]{:S(2)}) copy-start(bf16[2,1440,256]{2,1,0:T(8,128)(2,1)S(1)} %collective-permute-done.1.below) | copy-start | bytes 4423684
  53.6 9.1 %collective-permute-start.4 = (bf16[1152,256]{1,0:T(8,128)(2,1)S(1)}, bf16[1152,256]{1,0:T(8,128)(2,1)S(1)}, u32[]{:S(2)}, u32[]{:S(2)}) collective-permute-start(bf16[1152,256]{1,0:T(8,128)(2,1)S(1)} %dynamic-slice_convert_fusion), channel_id=1, source_target_pairs={{0,1},{1,0},{2,3},{3,2},{4,5},{5,4},{6,7},{7,6},{8,9},{9,8},{10,11... | collective-permute-start | bytes 1769480 | tf_op jit(solution)/shard_map/ppermute | solution.py:201
  64.2 10.2 %collective-permute-start.5 = (bf16[576,256]{1,0:T(8,128)(2,1)S(1)}, bf16[576,256]{1,0:T(8,128)(2,1)S(1)}, u32[]{:S(2)}, u32[]{:S(2)}) collective-permute-start(bf16[576,256]{1,0:T(8,128)(2,1)S(1)} %dynamic-slice_convert_fusion.1), channel_id=1, source_target_pairs={{0,2},{1,3},{2,0},{3,1},{4,6},{5,7},{6,4},{7,5},{8,10},{9,11},{10,... | collective-permute-start | bytes 884744 | tf_op jit(solution)/shard_map/ppermute | solution.py:201
  74.5 0.8 copy-start.2
  75.3 5.4 %collective-permute-start.6 = (bf16[288,256]{1,0:T(8,128)(2,1)S(1)}, bf16[288,256]{1,0:T(8,128)(2,1)S(1)}, u32[]{:S(2)}, u32[]{:S(2)}) collective-permute-start(bf16[288,256]{1,0:T(8,128)(2,1)S(1)} %dynamic-slice_convert_fusion.2), channel_id=1, source_target_pairs={{0,4},{1,5},{2,6},{3,7},{4,0},{5,1},{6,2},{7,3},{8,12},{9,13},{10,... | collective-permute-start | bytes 442376 | tf_op jit(solution)/shard_map/ppermute | solution.py:201
  76.4 51.6 %collective-permute-start.2 = (bf16[2,1440,256]{2,1,0:T(8,128)(2,1)}, bf16[2,1440,256]{2,1,0:T(8,128)(2,1)}, u32[]{:S(2)}, u32[]{:S(2)}) collective-permute-start(bf16[2,1440,256]{2,1,0:T(8,128)(2,1)} %get-tuple-element.50), channel_id=1, source_target_pairs={{0,1},{1,2},{2,3},{3,4},{4,5},{5,6},{6,7},{7,8},{8,9},{9,10},{10,1... | collective-permute-start | bytes 4423688 | tf_op jit(solution)/shard_map/ppermute | solution.py:227
  79.0 49.1 %collective-permute-start.3 = (bf16[2,1440,256]{2,1,0:T(8,128)(2,1)}, bf16[2,1440,256]{2,1,0:T(8,128)(2,1)}, u32[]{:S(2)}, u32[]{:S(2)}) collective-permute-start(bf16[2,1440,256]{2,1,0:T(8,128)(2,1)} %get-tuple-element.51), channel_id=1, source_target_pairs={{1,0},{2,1},{3,2},{4,3},{5,4},{6,5},{7,6},{8,7},{9,8},{10,9},{11,1... | collective-permute-start | bytes 4423688 | tf_op jit(solution)/shard_map/ppermute | solution.py:228
  80.3 47.7 %copy-start.1 = (f32[2,1440,256]{2,1,0:T(8,128)S(1)}, f32[2,1440,256]{2,1,0:T(8,128)}, u32[]{:S(2)}) copy-start(f32[2,1440,256]{2,1,0:T(8,128)} %get-tuple-element.55) | copy-start | bytes 8847364
  82.1 25.3 %collective-permute-start.7 = (bf16[144,256]{1,0:T(8,128)(2,1)S(1)}, bf16[144,256]{1,0:T(8,128)(2,1)S(1)}, u32[]{:S(2)}, u32[]{:S(2)}) collective-permute-start(bf16[144,256]{1,0:T(8,128)(2,1)S(1)} %dynamic-slice_convert_fusion.3), channel_id=1, source_target_pairs={{0,8},{1,9},{2,10},{3,11},{4,12},{5,13},{6,14},{7,15},{8,0},{9,1},... | collective-permute-start | bytes 221192 | tf_op jit(solution)/shard_map/ppermute | solution.py:201
  107.4 5.9 %collective-permute-start.8 = (bf16[144,256]{1,0:T(8,128)(2,1)S(1)}, bf16[144,256]{1,0:T(8,128)(2,1)S(1)}, u32[]{:S(2)}, u32[]{:S(2)}) collective-permute-start(bf16[144,256]{1,0:T(8,128)(2,1)S(1)} %add_convert_fusion.1), channel_id=1, source_target_pairs={{0,8},{1,9},{2,10},{3,11},{4,12},{5,13},{6,14},{7,15},{8,0},{9,1},... | collective-permute-start | bytes 221192 | tf_op jit(solution)/shard_map/ppermute | solution.py:206
  113.3 5.3 %collective-permute-start.9 = (bf16[288,256]{1,0:T(8,128)(2,1)S(1)}, bf16[288,256]{1,0:T(8,128)(2,1)}, u32[]{:S(2)}, u32[]{:S(2)}) collective-permute-start(bf16[288,256]{1,0:T(8,128)(2,1)S(1)} %maximum_select_fusion.3), channel_id=1, source_target_pairs={{0,4},{1,5},{2,6},{3,7},{4,0},{5,1},{6,2},{7,3},{8,12},{9,13},{10,... | collective-permute-start | bytes 442376 | tf_op jit(solution)/shard_map/ppermute | solution.py:206
  119.7 6.9 %collective-permute-start.10 = (bf16[576,256]{1,0:T(8,128)(2,1)S(1)}, bf16[576,256]{1,0:T(8,128)(2,1)}, u32[]{:S(2)}, u32[]{:S(2)}) collective-permute-start(bf16[576,256]{1,0:T(8,128)(2,1)S(1)} %maximum_select_fusion.2), channel_id=1, source_target_pairs={{0,2},{1,3},{2,0},{3,1},{4,6},{5,7},{6,4},{7,5},{8,10},{9,11},{10,... | collective-permute-start | bytes 884744 | tf_op jit(solution)/shard_map/ppermute | solution.py:206
  127.9 3.7 %collective-permute-start.11 = (bf16[1152,256]{1,0:T(8,128)(2,1)S(1)}, bf16[1152,256]{1,0:T(8,128)(2,1)S(1)}, u32[]{:S(2)}, u32[]{:S(2)}) collective-permute-start(bf16[1152,256]{1,0:T(8,128)(2,1)S(1)} %maximum_select_fusion.1), channel_id=1, source_target_pairs={{0,1},{1,0},{2,3},{3,2},{4,5},{5,4},{6,7},{7,6},{8,9},{9,8},{10,11... | collective-permute-start | bytes 1769480 | tf_op jit(solution)/shard_map/ppermute | solution.py:206

commit v2 on v0

v2 whole, which is shorter than its diff:
```python
import math

import jax
import jax.numpy as jnp
from jax import lax
from jax.experimental import pallas as pl
from jax.experimental.pallas import tpu as pltpu
from jax.sharding import PartitionSpec as P

H = 2
PAD = 16
GROUP = 4
HALF = 128


def entry(table, i, k, e, ne):
    return (
        table[i, k, e].astype(jnp.int32),
        table[i, k, ne + e].astype(jnp.int32),
        table[i, k, 2 * ne + e],
    )


def fwd_kernel(last, table, *refs):
    if last:
        own, slow, fast, cot, weight, earlier, mixed, keep, send, xf, basis, cott = refs
    else:
        own, slow, fast, cot, weight, mixed, keep, send, xf, basis, cott = refs
    rows, width, _ = own.shape
    chan = cot.shape[2]
    nk = weight.shape[0]
    ne = table.shape[2] // 3
    odd = table[0, 0, 3 * ne] > 0.5

    def widen(src, r, dst):
        def part(at, to):
            xf[dst, to] = src[r, at].astype(jnp.float32)

        part(slice(0, width), slice(PAD, PAD + width))
        part(slice(width - PAD, width), slice(0, PAD))
        part(slice(0, PAD), slice(PAD + width, 2 * PAD + width))

    for r in range(H):
        widen(slow, r, jnp.where(odd, H + rows, 0) + r)
        widen(fast, r, jnp.where(odd, 0, H + rows) + r)
    for r in range(rows):
        widen(own, r, H + r)
        cott[:, r * width : (r + 1) * width] = cot[r].T
    for i in range(rows):

        def per_k(k, carry):
            t = None
            for e in range(ne):
                line, lon, value = entry(table, i, k, e, ne)
                term = value * xf[i + H + line, pl.ds(PAD + lon, width), :]
                t = term if t is None else t + term
            cols = pl.ds(pl.multiple_of(k * HALF, HALF), HALF)
            basis[i * width : (i + 1) * width, cols] = t.astype(jnp.bfloat16)
            return carry

        lax.fori_loop(0, nk, per_k, 0)
    wflat = weight[...].reshape(nk * HALF, chan)
    parts = 3 * rows
    tile = rows * width // parts
    for p in range(parts):
        i, at = divmod(p * tile, width)
        acc = jnp.dot(basis[p * tile : (p + 1) * tile], wflat, preferred_element_type=jnp.float32)
        if last:
            mixed[i, at : at + tile] = (earlier[i, at : at + tile] + acc).astype(jnp.bfloat16)
        else:
            mixed[i, at : at + tile] = acc
    gwt = jnp.dot(cott[...], basis[...], preferred_element_type=jnp.float32)
    dhalf = chan // 2
    for k in range(nk):
        mat = gwt[:, k * HALF : (k + 1) * HALF].T
        low, high = mat[:, :dhalf], mat[:, dhalf:]
        keep[k] = jnp.where(odd, high, low)
        send[k] = jnp.where(odd, low, high).astype(jnp.bfloat16)


def forward(table, own, slow, fast, cot, weight, h, earlier=None):
    rows, width, chan = cot.shape
    nk = weight.shape[0]
    smem = pl.BlockSpec(memory_space=pltpu.SMEM)
    vmem = pl.BlockSpec(memory_space=pltpu.VMEM)
    last = earlier is not None
    half = pl.BlockSpec((rows, width, HALF), lambda g: (0, 0, h))
    side = pl.BlockSpec((H, width, HALF), lambda g: (0, 0, h))
    wide = pl.BlockSpec((rows, width, chan), lambda g: (0, 0, 0))
    edge = pl.BlockSpec((H, width, HALF), lambda g: (0, 0, 0))
    part = pl.BlockSpec((nk, HALF, chan // 2), lambda g: (0, 0, 0))
    return pl.pallas_call(
        lambda *refs: fwd_kernel(last, *refs),
        grid=(1,),
        in_specs=[smem]
        + [half, edge, side, wide, pl.BlockSpec((nk, HALF, chan), lambda g: (0, h, 0))]
        + [wide] * last,
        out_specs=[wide, part, part],
        out_shape=[
            jax.ShapeDtypeStruct((rows, width, chan), jnp.bfloat16 if last else jnp.float32),
            jax.ShapeDtypeStruct((nk, HALF, chan // 2), jnp.float32),
            jax.ShapeDtypeStruct((nk, HALF, chan // 2), jnp.bfloat16),
        ],
        scratch_shapes=[
            pltpu.VMEM((rows + 2 * H, width + 2 * PAD, HALF), jnp.float32),
            pltpu.VMEM((rows * width, nk * HALF), jnp.bfloat16),
            pltpu.VMEM((chan, rows * width), jnp.bfloat16),
        ],
        compiler_params=pltpu.CompilerParams(vmem_limit_bytes=48 * 2**20),
        cost_estimate=pl.CostEstimate(
            flops=0, bytes_accessed=0, transcendentals=0
        ),
        name="forward",
    )(table, own, slow, fast, cot, weight, *([earlier] if last else []))


def bwd_kernel(table, cin, win, own, *rest):
    edges, scratch = rest[:2], rest[2:]
    db, acc, narrow, cnt, lst_n, lst_o, lst_v, out_sems = scratch
    rows, width, chan = cin.shape
    nk = win.shape[0]
    ne = table.shape[2] // 3
    odd = table[0, 0, 3 * ne] > 0.5
    nh = chan // HALF
    lines = rows + 2 * H
    cap = rows * nk * ne + GROUP
    for line in range(lines):
        cnt[line] = 0

    for i in range(rows):

        def bin_one(k, carry):
            for e in range(ne):
                row, lon, value = entry(table, i, k, e, ne)
                line = i + H + row
                c = cnt[line]
                lst_n[line * cap + c] = i * nk + k
                lst_o[line * cap + c] = PAD - lon
                lst_v[line * cap + c] = value
                cnt[line] = c + 1
            return carry

        lax.fori_loop(0, nk, bin_one, 0)
    for line in range(lines):
        c = cnt[line]
        for g in range(GROUP):
            lst_n[line * cap + c + g] = 0
            lst_o[line * cap + c + g] = PAD
            lst_v[line * cap + c + g] = 0.0
    for i in range(rows):
        for k in range(nk):
            n = i * nk + k
            d = lax.dot_general(
                cin[i], win[k], (((1,), (1,)), ((), ())), preferred_element_type=jnp.float32
            )
            for h in range(nh):
                cols = slice(h * HALF, (h + 1) * HALF)
                db[n, h, PAD : PAD + width] = d[:, cols]
                db[n, h, 0:PAD] = d[width - PAD :, cols]
                db[n, h, PAD + width :] = d[0:PAD, cols]

    def terms(t, g, h):
        s = None
        for j in range(GROUP):
            at = t * cap + g * GROUP + j
            x = lst_v[at] * db[lst_n[at], h, pl.ds(lst_o[at], width), :]
            s = x if s is None else s + x
        return s

    def line_sum(t, slot):
        for h in range(nh):
            acc[slot, :, h * HALF : (h + 1) * HALF] = terms(t, 0, h)

        def group(g, carry):
            for h in range(nh):
                cols = slice(h * HALF, (h + 1) * HALF)
                acc[slot, :, cols] = acc[slot, :, cols] + terms(t, g, h)
            return carry

        lax.fori_loop(1, (cnt[t] + GROUP - 1) // GROUP, group, 0)

    def edge(s, carry):
        top = (s < H) != odd
        line_sum(jnp.where(top, 0, H + rows) + s % H, rows)
        narrow[s] = acc[rows].astype(narrow.dtype)
        return carry

    lax.fori_loop(0, 2 * H, edge, 0)
    writes = [
        pltpu.make_async_copy(narrow.at[0:H], edges[0], out_sems.at[0]),
        pltpu.make_async_copy(narrow.at[H:], edges[1], out_sems.at[1]),
    ]
    writes.append(pltpu.make_async_copy(acc.at[0:rows], own, out_sems.at[2]))
    for write in writes[:2]:
        write.start()

    def inner(s, carry):
        line_sum(s + H, s)
        return carry

    lax.fori_loop(0, rows, inner, 0)
    writes[2].start()
    for write in writes:
        write.wait()


def backward(table, cot, weight):
    rows, width, chan = cot.shape
    nk = weight.shape[0]
    ne = table.shape[2] // 3
    smem = pl.BlockSpec(memory_space=pltpu.SMEM)
    anym = pl.BlockSpec(memory_space=pl.ANY)
    lines = rows + 2 * H
    cap = rows * nk * ne + GROUP
    return pl.pallas_call(
        bwd_kernel,
        in_specs=[smem] + [pl.BlockSpec(memory_space=pltpu.VMEM)] * 2,
        out_specs=[anym] * 3,
        out_shape=[
            jax.ShapeDtypeStruct((rows, width, chan), jnp.float32),
        ]
        + [jax.ShapeDtypeStruct((H, width, chan), jnp.bfloat16)] * 2,
        scratch_shapes=[
            pltpu.VMEM((rows * nk, chan // HALF, width + 2 * PAD, HALF), jnp.float32),
            pltpu.VMEM((rows + 1, width, chan), jnp.float32),
            pltpu.VMEM((2 * H, width, chan), jnp.bfloat16),
            pltpu.SMEM((lines,), jnp.int32),
            pltpu.SMEM((lines * cap,), jnp.int32),
            pltpu.SMEM((lines * cap,), jnp.int32),
            pltpu.SMEM((lines * cap,), jnp.float32),
            pltpu.SemaphoreType.DMA((3,)),
        ],
        compiler_params=pltpu.CompilerParams(vmem_limit_bytes=56 * 2**20),
        cost_estimate=pl.CostEstimate(
            flops=2 * rows * width * nk * chan * chan, bytes_accessed=12 * 2**20, transcendentals=0
        ),
        name="backward",
    )(table, cot, weight)


def swap(value, bit, size):
    return lax.ppermute(value, "lat", [(i, i ^ bit) for i in range(size)])


def sums_over_lat(keeps, sends, between):
    size = lax.axis_size("lat")
    shape = keeps[0].shape
    index = lax.axis_index("lat")
    values = []
    for keep, send in zip(keeps, sends):
        got = swap(send.reshape(-1, shape[-1]), 1, size)
        values.append(keep.reshape(-1, shape[-1]) + got.astype(jnp.float32))
    bits = [1 << b for b in range(1, size.bit_length() - 1)]
    halved = bits[1:]
    for bit in halved:
        values = between(bit, values)
        side = (index // bit) % 2
        count = values[0].shape[0] // 2
        for j, value in enumerate(values):
            kept = lax.dynamic_slice_in_dim(value, side * count, count, 0)
            sent = lax.dynamic_slice_in_dim(value, (1 - side) * count, count, 0)
            got = swap(sent.astype(jnp.bfloat16), bit, size)
            values[j] = kept + got.astype(jnp.float32)
    for bit in bits[:1]:
        values = between(bit, values)
        for j, value in enumerate(values):
            sent = value.astype(jnp.bfloat16)
            values[j] = sent.astype(jnp.float32) + swap(sent, bit, size).astype(jnp.float32)
    values = [value.astype(jnp.bfloat16) for value in values]
    for bit in reversed(halved):
        values = between(-bit, values)
        side = (index // bit) % 2
        for j, value in enumerate(values):
            got = swap(value, bit, size)
            values[j] = jnp.where(
                side == 0, jnp.concatenate([value, got]), jnp.concatenate([got, value])
            )
    for j, value in enumerate(values):
        got = swap(value, 1, size)
        first = jnp.where(index % 2 == 0, value, got)
        second = jnp.where(index % 2 == 0, got, value)
        values[j] = jnp.concatenate([first.reshape(shape), second.reshape(shape)], axis=-1)
    return values


def per_device(inputs, cotangent, weight, pat_rows, pat_lons, pat_vals):
    rows = inputs.shape[0]
    width = inputs.shape[1]
    size = lax.axis_size("lat")
    index = lax.axis_index("lat")
    odd = index % 2 == 1
    fast_pairs = [(i, i ^ 1) for i in range(size)]
    slow_pairs = [(i, i + 1 if i % 2 else i - 1) for i in range(1, size - 1)]
    near_pairs = [pair for pair in slow_pairs if min(pair) % 4 == 1]
    far_pairs = [pair for pair in slow_pairs if min(pair) % 4 == 3]
    if rows == H:
        to_slow = to_fast = inputs
    else:
        head, tail = inputs[:H], inputs[rows - H :]
        to_slow, to_fast = jnp.where(odd, tail, head), jnp.where(odd, head, tail)
    slow = [
        lax.ppermute(to_slow[:, :, h * HALF : (h + 1) * HALF], "lat", slow_pairs) for h in range(2)
    ]
    fast = lax.ppermute(to_fast, "lat", fast_pairs)
    side = jnp.full((rows, pat_rows.shape[1], 1), odd, jnp.float32)
    table = [
        lax.dynamic_slice_in_dim(part, index * rows, rows, 0).astype(jnp.float32)
        for part in (pat_rows, pat_lons, pat_vals)
    ]
    table = jnp.concatenate([*table, side], axis=-1)
    grad, edge_slow, edge_fast = backward(table, cotangent, weight)
    slow[0], fast, edge_slow, edge_fast = lax.optimization_barrier(
        (slow[0], fast, edge_slow, edge_fast)
    )
    mixed, keep0, send0 = forward(table, inputs, slow[0], fast, cotangent, weight, 0)
    mixed, edge_slow, edge_fast = lax.optimization_barrier((mixed, edge_slow, edge_fast))
    got_far = lax.ppermute(edge_slow, "lat", far_pairs)
    got_near = lax.ppermute(edge_slow, "lat", near_pairs)
    got_fast = lax.ppermute(edge_fast, "lat", fast_pairs)
    mixed, keep1, send1 = forward(table, inputs, slow[1], fast, cotangent, weight, 1, mixed)
    scale = 1.0 / math.sqrt(pat_rows.shape[0] * width)
    waits = {4: 0, 2: 1}
    got = [got_far, got_near]

    def between(bit, values):
        if bit in waits:
            at = waits[bit]
            values, got[at] = lax.optimization_barrier((values, got[at]))
        return list(values)

    sums = sums_over_lat([keep0, keep1], [send0, send1], between)
    grad_weight = jnp.concatenate(sums, axis=1).astype(jnp.float32) * scale
    from_slow = got[0].astype(jnp.float32) + got[1].astype(jnp.float32)
    from_fast = got_fast.astype(jnp.float32)
    if rows == H:
        grad = grad + from_slow + from_fast
    else:
        grad = grad.at[:H].add(jnp.where(odd, from_fast, from_slow))
        grad = grad.at[rows - H :].add(jnp.where(odd, from_slow, from_fast))
    return (mixed, grad.astype(jnp.bfloat16), grad_weight)


def solution(mesh):
    return jax.shard_map(
        per_device,
        mesh=mesh,
        in_specs=(
            P(("group", "lat"), None, None),
            P(("group", "lat"), None, None),
            P(),
            P(),
            P(),
            P(),
        ),
        out_specs=(
            P(("group", "lat"), None, None),
            P(("group", "lat"), None, None),
            P("group", None, None),
        ),
        check_vma=False,
    )
```

time: 835 us -> 106 us (0.13); the launches traced: 826 us -> 106 us
  other arithmetic: 293 us -> 11 us
  loops' own time: 238 us -> 0 us
  local copies, waits for them, and re-layouts: 151 us -> 4.45 us
  waiting for transfers between devices: 91.5 us -> 19.4 us
  Pallas kernels: 0 us -> 39.3 us
  matrix products: 26 us -> 0 us
  starting transfers between devices: 12.3 us -> 30.9 us
  between operations: 14.2 us -> 0.93 us
    dynamic_update_slice x72 -> x0, other arithmetic: 284 us -> none  [the longest x54 193 us: per_source(): accum = lax.dynamic_update_slice(accum, updated[None], (target, 0, 0))]
    another operation x2 -> x0, loops' own time: 238 us -> none  [the longest x1 137 us: gather_terms(): basis = lax.map(per_item, (slots, rows_flat, lons_flat, vals_flat))]
    psum x1 -> x0, waiting for transfers between devices: 91.5 us -> none  [per_device(): total_w = lax.psum(partial_w, 'lat')]
    concatenate x3 -> x1, local copies, waits for them, and re-layouts: 86.8 us -> 0.08 us  [per_device(): table = jnp.concatenate([*table, side], axis=-1)]
    pallas_call x0 -> x3, Pallas kernels: none -> 39.3 us  [the longest x2 22.4 us: forward(): pl.pallas_call(lambda *refs: fwd_kernel(last, *refs), grid=(1,), in_specs...]
    slice x57 -> x1, local copies, waits for them, and re-layouts: 38.1 us -> 2.61 us  [per_device(): to_slow[:, :, h * HALF:(h + 1) * HALF]]
    dot_general x3 -> x0, matrix products: 26 us -> none  [the longest x1 9.5 us: per_device(): jnp.einsum('krjc,kcd->rjd', basis, weight, preferred_element_type=jnp.flo...]
    ppermute x4 -> x20, waiting for transfers between devices: 0.01 us -> 19.4 us  [the longest x14 19.4 us: swap(): return lax.ppermute(value, 'lat', [(i, i ^ bit) for i in range(size)])]
  transfers between devices with their start and end apart: 5 -> 20, of which waited for: 1 -> 9; matrix products, arithmetic and copies ran while one was open for 56% -> 13% of each run, Pallas kernels for 0% -> 37%
where the time goes in v2:
time: 106 us
  Pallas kernels  39.3 us (37%)
  starting transfers between devices  30.9 us (29%)
  waiting for transfers between devices  19.4 us (18%)
  other arithmetic  11 us (10%)
  local copies, waits for them, and re-layouts  4.45 us (4%)
    ppermute x14, starting transfers between devices, swap(): return lax.ppermute(value, 'lat', [(i, i ^ bit) for i in range(size)])  25.4 us
    pallas_call x2, Pallas kernels, forward(): pl.pallas_call(lambda *refs: fwd_kernel(last, *refs), grid=(1,), in_specs...  22.4 us
    ppermute x14, waiting for transfers between devices, swap(): return lax.ppermute(value, 'lat', [(i, i ^ bit) for i in range(size)])  19.4 us
    pallas_call x1, Pallas kernels, backward(): pl.pallas_call(bwd_kernel, in_specs=[smem] + [pl.BlockSpec(memory_space=p...  16.9 us
    convert_element_type x1, other arithmetic, per_device(): return (mixed, grad.astype(jnp.bfloat16), grad_weight)  4.21 us
    slice x1, local copies, waits for them, and re-layouts, per_device(): to_slow[:, :, h * HALF:(h + 1) * HALF]  2.61 us
  transfers between devices with their start and end apart: 20, of which 9 were waited for; matrix products, arithmetic and copies ran while one was open for 13% of the time, Pallas kernels for 37%

profile of v2, /device:TPU:0, one launch (start us, length us, event | category | flops | bytes accessed | tf_op | source)
XLA Modules:
  0.0 105.9 jit_solution(6100166966627920057)
XLA Ops:
  0.6 0.0 copy-start
  0.7 0.5 collective-permute-start.2
  1.2 2.6 %fusion = (bf16[2,1440,128]{2,1,0:T(8,128)(2,1)}, bf16[2,1440,128]{2,1,0:T(8,128)(2,1)}) fusion(bf16[2,1440,256]{2,1,0:T(8,128)(2,1)} %refs_1_.3), kind=kLoop, calls=%fused_computation.26 | loop fusion | bytes 2949120 | tf_op jit(solution)/shard_map/slice | solution.py:302
  3.8 0.7 collective-permute-start.1
  4.5 0.7 collective-permute-start
  5.2 0.0 copy-done.7
  5.2 0.0 copy-done.8
  5.2 0.1 constant_dynamic-slice_fusion.1
  5.3 0.0 copy-done
  5.3 0.1 constant_dynamic-slice_fusion
  5.4 0.2 copy.12
  5.6 0.2 copy.13
  5.8 0.2 copy.14
  6.0 0.1 pad.23.clone
  6.0 0.7 maximum_maximum_fusion.table.refs_0_
  6.7 16.9 %backward.1 = (f32[2,1440,256]{2,1,0:T(8,128)}, bf16[2,1440,256]{2,1,0:T(8,128)(2,1)}, bf16[2,1440,256]{2,1,0:T(8,128)(2,1)}) custom-call(f32[2,9,10]{2,1,0:T(8,128)} %maximum_maximum_fusion.table.refs_0_, bf16[2,1440,256]{2,1,0:T(8,128)(2,1)} %refs_4_.3, bf16[9,256,256]{2,1,0:T(8,128)(2,1)} %refs_5_.3), custom_call_target="tpu_custom_call" | custom-call | flops 3397386240 | bytes 12582912 | tf_op jit(solution)/shard_map/backward/pallas_call | solution.py:215
  23.6 0.0 collective-permute-done.1.refs_2_
  23.6 0.0 collective-permute-done.2.refs_3_
  23.7 10.4 %forward.2 = (f32[2,1440,256]{2,1,0:T(8,128)}, f32[9,128,128]{2,1,0:T(8,128)S(1)}, bf16[9,128,128]{2,1,0:T(8,128)(2,1)S(1)}) custom-call(f32[2,9,10]{2,1,0:T(8,128)S(1)} %copy-done.4, bf16[2,1440,256]{2,1,0:T(8,128)(2,1)S(1)} %copy-done.1, bf16[2,1440,128]{2,1,0:T(8,128)(2,1)S(1)} %collective-permute-done.1.refs_2_, ...), custom_call_target="tpu_custom_call" | custom-call | tf_op jit(solution)/shard_map/forward/pallas_call | solution.py:92
  34.1 1.8 %collective-permute-start.5 = (bf16[2,1440,256]{2,1,0:T(8,128)(2,1)}, bf16[2,1440,256]{2,1,0:T(8,128)(2,1)}, u32[]{:S(2)}, u32[]{:S(2)}) collective-permute-start(bf16[2,1440,256]{2,1,0:T(8,128)(2,1)} %get-tuple-element.39), channel_id=1, source_target_pairs={{3,4},{4,3},{7,8},{8,7},{11,12},{12,11},{19,20},{20,19},{23,24},{2... | collective-permute-start | bytes 4423688 | tf_op jit(solution)/shard_map/ppermute | solution.py:317
  35.9 0.0 collective-permute-done.refs_2_
  35.9 12.0 %forward.3 = (bf16[2,1440,256]{2,1,0:T(8,128)(2,1)}, f32[9,128,128]{2,1,0:T(8,128)S(1)}, bf16[9,128,128]{2,1,0:T(8,128)(2,1)}) custom-call(f32[2,9,10]{2,1,0:T(8,128)S(1)} %copy-done.4, bf16[2,1440,256]{2,1,0:T(8,128)(2,1)S(1)} %copy-done.1, bf16[2,1440,128]{2,1,0:T(8,128)(2,1)S(1)} %collective-permute-done.refs_2_, ...), custom_call_target="tpu_custom_call" | custom-call | tf_op jit(solution)/shard_map/forward/pallas_call | solution.py:92
  47.9 9.3 %collective-permute-start.4 = (bf16[1152,128]{1,0:T(8,128)(2,1)}, bf16[1152,128]{1,0:T(8,128)(2,1)S(1)}, u32[]{:S(2)}, u32[]{:S(2)}) collective-permute-start(bf16[1152,128]{1,0:T(8,128)(2,1)} %bitcast.3), channel_id=1, source_target_pairs={{0,1},{1,0},{2,3},{3,2},{4,5},{5,4},{6,7},{7,6},{8,9},{9,8},{10,11... | collective-permute-start | bytes 884744 | tf_op jit(solution)/shard_map/ppermute | solution.py:242
  57.1 1.8 %collective-permute-start.10 = (bf16[2,1440,256]{2,1,0:T(8,128)(2,1)}, bf16[2,1440,256]{2,1,0:T(8,128)(2,1)}, u32[]{:S(2)}, u32[]{:S(2)}) collective-permute-start(bf16[2,1440,256]{2,1,0:T(8,128)(2,1)} %get-tuple-element.39), channel_id=1, source_target_pairs={{1,2},{2,1},{5,6},{6,5},{9,10},{10,9},{13,14},{14,13},{17,18},{18,... | collective-permute-start | bytes 4423688 | tf_op jit(solution)/shard_map/ppermute | solution.py:318
  58.9 2.7 %collective-permute-start.3 = (bf16[1152,128]{1,0:T(8,128)(2,1)S(1)}, bf16[1152,128]{1,0:T(8,128)(2,1)S(1)}, u32[]{:S(2)}, u32[]{:S(2)}) collective-permute-start(bf16[1152,128]{1,0:T(8,128)(2,1)S(1)} %bitcast.11), channel_id=1, source_target_pairs={{0,1},{1,0},{2,3},{3,2},{4,5},{5,4},{6,7},{7,6},{8,9},{9,8},{10,11... | collective-permute-start | bytes 884744 | tf_op jit(solution)/shard_map/ppermute | solution.py:242
  61.6 0.0 collective-permute-done.4
  61.6 0.1 bitcast_add_fusion
  61.7 1.1 %collective-permute-done.3 = bf16[1152,128]{1,0:T(8,128)(2,1)S(1)} collective-permute-done((bf16[1152,128]{1,0:T(8,128)(2,1)S(1)}, bf16[1152,128]{1,0:T(8,128)(2,1)S(1)}, u32[]{:S(2)}, u32[]{:S(2)}) %collective-permute-start.3) | collective-permute-done | bytes 294944 | tf_op jit(solution)/shard_map/ppermute | solution.py:242
  62.8 1.9 %bitcast_add_fusion.1 = f32[1152,128]{1,0:T(8,128)} fusion(f32[9,128,128]{2,1,0:T(8,128)} %copy-done.3, bf16[1152,128]{1,0:T(8,128)(2,1)S(1)} %collective-permute-done.3), kind=kLoop, calls=%fused_computation.3 | loop fusion | flops 294912 | bytes 1474560 | tf_op jit(solution)/shard_map/add | solution.py:252
  64.7 0.0 collective-permute-done.5
  64.8 1.1 %collective-permute-start.8 = (bf16[576,128]{1,0:T(8,128)(2,1)S(1)}, bf16[576,128]{1,0:T(8,128)(2,1)S(1)}, u32[]{:S(2)}, u32[]{:S(2)}) collective-permute-start(bf16[576,128]{1,0:T(8,128)(2,1)S(1)} %dynamic-slice_convert_fusion), channel_id=1, source_target_pairs={{0,4},{1,5},{2,6},{3,7},{4,0},{5,1},{6,2},{7,3},{8,12},{9,13},{10,... | collective-permute-start | bytes 442376 | tf_op jit(solution)/shard_map/ppermute | solution.py:242
  65.9 0.1 collective-permute-start.11
  66.0 1.0 dynamic-slice_convert_fusion.1
  67.0 1.0 collective-permute-start.6
  68.0 3.5 %collective-permute-done.8 = bf16[576,128]{1,0:T(8,128)(2,1)S(1)} collective-permute-done((bf16[576,128]{1,0:T(8,128)(2,1)S(1)}, bf16[576,128]{1,0:T(8,128)(2,1)S(1)}, u32[]{:S(2)}, u32[]{:S(2)}) %collective-permute-start.8) | collective-permute-done | bytes 147488 | tf_op jit(solution)/shard_map/ppermute | solution.py:242
  71.5 1.0 convert_add_fusion
  72.5 2.1 %collective-permute-start.9 = (bf16[288,128]{1,0:T(8,128)(2,1)S(1)}, bf16[288,128]{1,0:T(8,128)(2,1)S(1)}, u32[]{:S(2)}, u32[]{:S(2)}) collective-permute-start(bf16[288,128]{1,0:T(8,128)(2,1)S(1)} %dynamic-slice_convert_fusion.2), channel_id=1, source_target_pairs={{0,8},{1,9},{2,10},{3,11},{4,12},{5,13},{6,14},{7,15},{8,0},{9,1},... | collective-permute-start | bytes 221192 | tf_op jit(solution)/shard_map/ppermute | solution.py:242
  74.6 0.0 collective-permute-done.6
  74.6 1.0 convert_add_fusion.1
  75.6 1.6 %collective-permute-start.7 = (bf16[288,128]{1,0:T(8,128)(2,1)S(1)}, bf16[288,128]{1,0:T(8,128)(2,1)S(1)}, u32[]{:S(2)}, u32[]{:S(2)}) collective-permute-start(bf16[288,128]{1,0:T(8,128)(2,1)S(1)} %dynamic-slice_convert_fusion.3), channel_id=1, source_target_pairs={{0,8},{1,9},{2,10},{3,11},{4,12},{5,13},{6,14},{7,15},{8,0},{9,1},... | collective-permute-start | bytes 221192 | tf_op jit(solution)/shard_map/ppermute | solution.py:242
  77.2 2.4 %collective-permute-done.9 = bf16[288,128]{1,0:T(8,128)(2,1)S(1)} collective-permute-done((bf16[288,128]{1,0:T(8,128)(2,1)S(1)}, bf16[288,128]{1,0:T(8,128)(2,1)S(1)}, u32[]{:S(2)}, u32[]{:S(2)}) %collective-permute-start.9) | collective-permute-done | bytes 73760 | tf_op jit(solution)/shard_map/ppermute | solution.py:242
  79.6 2.2 %collective-permute-done.7 = bf16[288,128]{1,0:T(8,128)(2,1)S(1)} collective-permute-done((bf16[288,128]{1,0:T(8,128)(2,1)S(1)}, bf16[288,128]{1,0:T(8,128)(2,1)S(1)}, u32[]{:S(2)}, u32[]{:S(2)}) %collective-permute-start.7) | collective-permute-done | bytes 73760 | tf_op jit(solution)/shard_map/ppermute | solution.py:242
  81.8 0.0 collective-permute-done.10
  81.8 0.1 collective-permute-start.12
  81.9 2.0 %collective-permute-start.16 = (bf16[288,128]{1,0:T(8,128)(2,1)S(1)}, bf16[288,128]{1,0:T(8,128)(2,1)S(1)}, u32[]{:S(2)}, u32[]{:S(2)}) collective-permute-start(bf16[288,128]{1,0:T(8,128)(2,1)S(1)} %convert_add_fusion.2), channel_id=1, source_target_pairs={{0,2},{1,3},{2,0},{3,1},{4,6},{5,7},{6,4},{7,5},{8,10},{9,11},{10,... | collective-permute-start | bytes 221192 | tf_op jit(solution)/shard_map/ppermute | solution.py:242
  83.9 2.3 %collective-permute-done.12 = bf16[288,128]{1,0:T(8,128)(2,1)S(1)} collective-permute-done((bf16[288,128]{1,0:T(8,128)(2,1)S(1)}, bf16[288,128]{1,0:T(8,128)(2,1)S(1)}, u32[]{:S(2)}, u32[]{:S(2)}) %collective-permute-start.12) | collective-permute-done | bytes 73760 | tf_op jit(solution)/shard_map/ppermute | solution.py:242
  86.3 0.8 collective-permute-start.13
  87.1 0.0 collective-permute-done.16
  87.2 2.2 %collective-permute-start.17 = (bf16[288,128]{1,0:T(8,128)(2,1)S(1)}, bf16[288,128]{1,0:T(8,128)(2,1)S(1)}, u32[]{:S(2)}, u32[]{:S(2)}) collective-permute-start(bf16[288,128]{1,0:T(8,128)(2,1)S(1)} %add_convert_fusion.1), channel_id=1, source_target_pairs={{0,8},{1,9},{2,10},{3,11},{4,12},{5,13},{6,14},{7,15},{8,0},{9,1},... | collective-permute-start | bytes 221192 | tf_op jit(solution)/shard_map/ppermute | solution.py:242
  89.4 3.3 %collective-permute-done.13 = bf16[288,128]{1,0:T(8,128)(2,1)S(1)} collective-permute-done((bf16[288,128]{1,0:T(8,128)(2,1)S(1)}, bf16[288,128]{1,0:T(8,128)(2,1)S(1)}, u32[]{:S(2)}, u32[]{:S(2)}) %collective-permute-start.13) | collective-permute-done | bytes 73760 | tf_op jit(solution)/shard_map/ppermute | solution.py:242
  92.8 0.1 collective-permute-start.14
  92.9 0.8 collective-permute-done.17
  93.7 1.8 %collective-permute-start.18 = (bf16[576,128]{1,0:T(8,128)(2,1)S(1)}, bf16[576,128]{1,0:T(8,128)(2,1)S(1)}, u32[]{:S(2)}, u32[]{:S(2)}) collective-permute-start(bf16[576,128]{1,0:T(8,128)(2,1)S(1)} %maximum_select_fusion.3), channel_id=1, source_target_pairs={{0,4},{1,5},{2,6},{3,7},{4,0},{5,1},{6,2},{7,3},{8,12},{9,13},{10,... | collective-permute-start | bytes 442376 | tf_op jit(solution)/shard_map/ppermute | solution.py:242
  95.5 2.5 %collective-permute-done.14 = bf16[576,128]{1,0:T(8,128)(2,1)S(1)} collective-permute-done((bf16[576,128]{1,0:T(8,128)(2,1)S(1)}, bf16[576,128]{1,0:T(8,128)(2,1)S(1)}, u32[]{:S(2)}, u32[]{:S(2)}) %collective-permute-start.14) | collective-permute-done | bytes 147488 | tf_op jit(solution)/shard_map/ppermute | solution.py:242
  98.0 0.1 maximum_select_fusion
  98.1 0.1 collective-permute-start.15
  98.2 0.0 collective-permute-done.11
  98.2 4.2 %add_convert_fusion = bf16[2,1440,256]{2,1,0:T(8,128)(2,1)} fusion(bf16[2,1440,256]{2,1,0:T(8,128)(2,1)} %collective-permute-done.11, f32[2,1440,256]{2,1,0:T(8,128)S(1)} %copy-done.5, bf16[2,1440,256]{2,1,0:T(8,128)(2,1)} %collective-permute-done.10, bf16[2,1440,256]{2,1,0:T(8,128)(2,1)} %collective-permute-done.5), kind=kLoop, calls=%fused_computation | loop fusion | flops 5160960 | bytes 8847360 | tf_op jit(solution)/shard_map/convert_element_type | solution.py:340
  102.4 0.0 collective-permute-done.18
  102.4 0.1 maximum_select_fusion.1
  102.5 0.5 collective-permute-start.19
  103.0 0.0 collective-permute-done.15
  103.1 1.2 %collective-permute-done.19 = bf16[1152,128]{1,0:T(8,128)(2,1)S(1)} collective-permute-done((bf16[1152,128]{1,0:T(8,128)(2,1)S(1)}, bf16[1152,128]{1,0:T(8,128)(2,1)S(1)}, u32[]{:S(2)}, u32[]{:S(2)}) %collective-permute-start.19) | collective-permute-done | bytes 294944 | tf_op jit(solution)/shard_map/ppermute | solution.py:242
  104.3 1.6 %convert_multiply_fusion = f32[9,256,256]{2,1,0:T(8,128)} fusion(bf16[9,128,128]{2,1,0:T(8,128)(2,1)S(1)} %bitcast.15, bf16[9,128,128]{2,1,0:T(8,128)(2,1)S(1)} %bitcast.14, bf16[9,128,128]{2,1,0:T(8,128)(2,1)S(1)} %bitcast.13, bf16[9,128,128]{2,1,0:T(8,128)(2,1)S(1)} %bitcast.12), kind=kLoop, calls=%fused_computation.1 | loop fusion | flops 5308416 | bytes 3538944 | tf_op jit(solution)/shard_map/mul | solution.py:332
  (27 shorter events, 0.4 us)
Async XLA Ops:
  0.6 4.7 %copy-start = (f32[32,9,3]{0,2,1:T(4,128)S(1)}, f32[32,9,3]{0,2,1:T(4,128)}, u32[]{:S(2)}) copy-start(f32[32,9,3]{0,2,1:T(4,128)} %param.11) | copy-start | bytes 10372
  0.6 4.6 %copy-start.7 = (s32[32,9,3]{0,2,1:T(4,128)S(1)}, s32[32,9,3]{0,2,1:T(4,128)}, u32[]{:S(2)}) copy-start(s32[32,9,3]{0,2,1:T(4,128)} %param.10) | copy-start | bytes 10372
  0.7 4.6 %copy-start.8 = (s32[32,9,3]{0,2,1:T(4,128)S(1)}, s32[32,9,3]{0,2,1:T(4,128)}, u32[]{:S(2)}) copy-start(s32[32,9,3]{0,2,1:T(4,128)} %param.9) | copy-start | bytes 10372
  0.7 23.0 %collective-permute-start.2 = (bf16[2,1440,256]{2,1,0:T(8,128)(2,1)}, bf16[2,1440,256]{2,1,0:T(8,128)(2,1)S(1)}, u32[]{:S(2)}, u32[]{:S(2)}) collective-permute-start(bf16[2,1440,256]{2,1,0:T(8,128)(2,1)} %refs_1_.3), channel_id=1, source_target_pairs={{0,1},{1,0},{2,3},{3,2},{4,5},{5,4},{6,7},{7,6},{8,9},{9,8},{10,11... | collective-permute-start | bytes 4423688 | tf_op jit(solution)/shard_map/ppermute | solution.py:304
  3.8 19.8 %collective-permute-start.1 = (bf16[2,1440,128]{2,1,0:T(8,128)(2,1)}, bf16[2,1440,128]{2,1,0:T(8,128)(2,1)S(1)}, u32[]{:S(2)}, u32[]{:S(2)}) collective-permute-start(bf16[2,1440,128]{2,1,0:T(8,128)(2,1)} %get-tuple-element.47), channel_id=1, source_target_pairs={{1,2},{2,1},{3,4},{4,3},{5,6},{6,5},{7,8},{8,7},{9,10},{10,9},{11,... | collective-permute-start | bytes 2211848 | tf_op jit(solution)/shard_map/ppermute | solution.py:302
  4.5 31.4 %collective-permute-start = (bf16[2,1440,128]{2,1,0:T(8,128)(2,1)}, bf16[2,1440,128]{2,1,0:T(8,128)(2,1)S(1)}, u32[]{:S(2)}, u32[]{:S(2)}) collective-permute-start(bf16[2,1440,128]{2,1,0:T(8,128)(2,1)} %get-tuple-element.48), channel_id=1, source_target_pairs={{1,2},{2,1},{3,4},{4,3},{5,6},{6,5},{7,8},{8,7},{9,10},{10,9},{11,... | collective-permute-start | bytes 2211848 | tf_op jit(solution)/shard_map/ppermute | solution.py:302
  6.7 16.9 %copy-start.1 = (bf16[2,1440,256]{2,1,0:T(8,128)(2,1)S(1)}, bf16[2,1440,256]{2,1,0:T(8,128)(2,1)}, u32[]{:S(2)}) copy-start(bf16[2,1440,256]{2,1,0:T(8,128)(2,1)} %refs_1_.3) | copy-start | bytes 4423684
  6.7 16.9 %copy-start.2 = (bf16[9,256,256]{2,1,0:T(8,128)(2,1)S(1)}, bf16[9,256,256]{2,1,0:T(8,128)(2,1)}, u32[]{:S(2)}) copy-start(bf16[9,256,256]{2,1,0:T(8,128)(2,1)} %refs_5_.3) | copy-start | bytes 3538948
  6.7 16.9 %copy-start.4 = (f32[2,9,10]{2,1,0:T(8,128)S(1)}, f32[2,9,10]{2,1,0:T(8,128)}, u32[]{:S(2)}) copy-start(f32[2,9,10]{2,1,0:T(8,128)} %maximum_maximum_fusion.table.refs_0_) | copy-start | bytes 2164
  34.1 13.8 %copy-start.3 = (f32[9,128,128]{2,1,0:T(8,128)}, f32[9,128,128]{2,1,0:T(8,128)S(1)}, u32[]{:S(2)}) copy-start(f32[9,128,128]{2,1,0:T(8,128)S(1)} %get-tuple-element.35) | copy-start | bytes 1769476
  34.1 30.7 %collective-permute-start.5 = (bf16[2,1440,256]{2,1,0:T(8,128)(2,1)}, bf16[2,1440,256]{2,1,0:T(8,128)(2,1)}, u32[]{:S(2)}, u32[]{:S(2)}) collective-permute-start(bf16[2,1440,256]{2,1,0:T(8,128)(2,1)} %get-tuple-element.39), channel_id=1, source_target_pairs={{3,4},{4,3},{7,8},{8,7},{11,12},{12,11},{19,20},{20,19},{23,24},{2... | collective-permute-start | bytes 4423688 | tf_op jit(solution)/shard_map/ppermute | solution.py:317
  47.9 13.7 %collective-permute-start.4 = (bf16[1152,128]{1,0:T(8,128)(2,1)}, bf16[1152,128]{1,0:T(8,128)(2,1)S(1)}, u32[]{:S(2)}, u32[]{:S(2)}) collective-permute-start(bf16[1152,128]{1,0:T(8,128)(2,1)} %bitcast.3), channel_id=1, source_target_pairs={{0,1},{1,0},{2,3},{3,2},{4,5},{5,4},{6,7},{7,6},{8,9},{9,8},{10,11... | collective-permute-start | bytes 884744 | tf_op jit(solution)/shard_map/ppermute | solution.py:242
  57.1 24.7 %collective-permute-start.10 = (bf16[2,1440,256]{2,1,0:T(8,128)(2,1)}, bf16[2,1440,256]{2,1,0:T(8,128)(2,1)}, u32[]{:S(2)}, u32[]{:S(2)}) collective-permute-start(bf16[2,1440,256]{2,1,0:T(8,128)(2,1)} %get-tuple-element.39), channel_id=1, source_target_pairs={{1,2},{2,1},{5,6},{6,5},{9,10},{10,9},{13,14},{14,13},{17,18},{18,... | collective-permute-start | bytes 4423688 | tf_op jit(solution)/shard_map/ppermute | solution.py:318
  58.9 3.9 %collective-permute-start.3 = (bf16[1152,128]{1,0:T(8,128)(2,1)S(1)}, bf16[1152,128]{1,0:T(8,128)(2,1)S(1)}, u32[]{:S(2)}, u32[]{:S(2)}) collective-permute-start(bf16[1152,128]{1,0:T(8,128)(2,1)S(1)} %bitcast.11), channel_id=1, source_target_pairs={{0,1},{1,0},{2,3},{3,2},{4,5},{5,4},{6,7},{7,6},{8,9},{9,8},{10,11... | collective-permute-start | bytes 884744 | tf_op jit(solution)/shard_map/ppermute | solution.py:242
  61.6 3.1 %copy-start.6 = (f32[1152,128]{1,0:T(8,128)}, f32[1152,128]{1,0:T(8,128)S(1)}, u32[]{:S(2)}) copy-start(f32[1152,128]{1,0:T(8,128)S(1)} %bitcast_add_fusion) | copy-start | bytes 1769476
  64.7 33.4 %copy-start.5 = (f32[2,1440,256]{2,1,0:T(8,128)S(1)}, f32[2,1440,256]{2,1,0:T(8,128)}, u32[]{:S(2)}) copy-start(f32[2,1440,256]{2,1,0:T(8,128)} %get-tuple-element.34) | copy-start | bytes 8847364
  64.8 6.7 %collective-permute-start.8 = (bf16[576,128]{1,0:T(8,128)(2,1)S(1)}, bf16[576,128]{1,0:T(8,128)(2,1)S(1)}, u32[]{:S(2)}, u32[]{:S(2)}) collective-permute-start(bf16[576,128]{1,0:T(8,128)(2,1)S(1)} %dynamic-slice_convert_fusion), channel_id=1, source_target_pairs={{0,4},{1,5},{2,6},{3,7},{4,0},{5,1},{6,2},{7,3},{8,12},{9,13},{10,... | collective-permute-start | bytes 442376 | tf_op jit(solution)/shard_map/ppermute | solution.py:242
  65.9 32.2 %collective-permute-start.11 = (bf16[2,1440,256]{2,1,0:T(8,128)(2,1)}, bf16[2,1440,256]{2,1,0:T(8,128)(2,1)}, u32[]{:S(2)}, u32[]{:S(2)}) collective-permute-start(bf16[2,1440,256]{2,1,0:T(8,128)(2,1)} %get-tuple-element.44), channel_id=1, source_target_pairs={{0,1},{1,0},{2,3},{3,2},{4,5},{5,4},{6,7},{7,6},{8,9},{9,8},{10,11... | collective-permute-start | bytes 4423688 | tf_op jit(solution)/shard_map/ppermute | solution.py:319
  67.0 7.7 %collective-permute-start.6 = (bf16[576,128]{1,0:T(8,128)(2,1)S(1)}, bf16[576,128]{1,0:T(8,128)(2,1)S(1)}, u32[]{:S(2)}, u32[]{:S(2)}) collective-permute-start(bf16[576,128]{1,0:T(8,128)(2,1)S(1)} %dynamic-slice_convert_fusion.1), channel_id=1, source_target_pairs={{0,4},{1,5},{2,6},{3,7},{4,0},{5,1},{6,2},{7,3},{8,12},{9,13},{10,... | collective-permute-start | bytes 442376 | tf_op jit(solution)/shard_map/ppermute | solution.py:242
  72.5 7.1 %collective-permute-start.9 = (bf16[288,128]{1,0:T(8,128)(2,1)S(1)}, bf16[288,128]{1,0:T(8,128)(2,1)S(1)}, u32[]{:S(2)}, u32[]{:S(2)}) collective-permute-start(bf16[288,128]{1,0:T(8,128)(2,1)S(1)} %dynamic-slice_convert_fusion.2), channel_id=1, source_target_pairs={{0,8},{1,9},{2,10},{3,11},{4,12},{5,13},{6,14},{7,15},{8,0},{9,1},... | collective-permute-start | bytes 221192 | tf_op jit(solution)/shard_map/ppermute | solution.py:242
  75.6 6.2 %collective-permute-start.7 = (bf16[288,128]{1,0:T(8,128)(2,1)S(1)}, bf16[288,128]{1,0:T(8,128)(2,1)S(1)}, u32[]{:S(2)}, u32[]{:S(2)}) collective-permute-start(bf16[288,128]{1,0:T(8,128)(2,1)S(1)} %dynamic-slice_convert_fusion.3), channel_id=1, source_target_pairs={{0,8},{1,9},{2,10},{3,11},{4,12},{5,13},{6,14},{7,15},{8,0},{9,1},... | collective-permute-start | bytes 221192 | tf_op jit(solution)/shard_map/ppermute | solution.py:242
  81.8 4.4 %collective-permute-start.12 = (bf16[288,128]{1,0:T(8,128)(2,1)S(1)}, bf16[288,128]{1,0:T(8,128)(2,1)S(1)}, u32[]{:S(2)}, u32[]{:S(2)}) collective-permute-start(bf16[288,128]{1,0:T(8,128)(2,1)S(1)} %convert_add_fusion.3), channel_id=1, source_target_pairs={{0,2},{1,3},{2,0},{3,1},{4,6},{5,7},{6,4},{7,5},{8,10},{9,11},{10,... | collective-permute-start | bytes 221192 | tf_op jit(solution)/shard_map/ppermute | solution.py:242
  81.9 5.2 %collective-permute-start.16 = (bf16[288,128]{1,0:T(8,128)(2,1)S(1)}, bf16[288,128]{1,0:T(8,128)(2,1)S(1)}, u32[]{:S(2)}, u32[]{:S(2)}) collective-permute-start(bf16[288,128]{1,0:T(8,128)(2,1)S(1)} %convert_add_fusion.2), channel_id=1, source_target_pairs={{0,2},{1,3},{2,0},{3,1},{4,6},{5,7},{6,4},{7,5},{8,10},{9,11},{10,... | collective-permute-start | bytes 221192 | tf_op jit(solution)/shard_map/ppermute | solution.py:242
  86.3 6.4 %collective-permute-start.13 = (bf16[288,128]{1,0:T(8,128)(2,1)S(1)}, bf16[288,128]{1,0:T(8,128)(2,1)S(1)}, u32[]{:S(2)}, u32[]{:S(2)}) collective-permute-start(bf16[288,128]{1,0:T(8,128)(2,1)S(1)} %add_convert_fusion.2), channel_id=1, source_target_pairs={{0,8},{1,9},{2,10},{3,11},{4,12},{5,13},{6,14},{7,15},{8,0},{9,1},... | collective-permute-start | bytes 221192 | tf_op jit(solution)/shard_map/ppermute | solution.py:242
  87.2 6.5 %collective-permute-start.17 = (bf16[288,128]{1,0:T(8,128)(2,1)S(1)}, bf16[288,128]{1,0:T(8,128)(2,1)S(1)}, u32[]{:S(2)}, u32[]{:S(2)}) collective-permute-start(bf16[288,128]{1,0:T(8,128)(2,1)S(1)} %add_convert_fusion.1), channel_id=1, source_target_pairs={{0,8},{1,9},{2,10},{3,11},{4,12},{5,13},{6,14},{7,15},{8,0},{9,1},... | collective-permute-start | bytes 221192 | tf_op jit(solution)/shard_map/ppermute | solution.py:242
  92.8 5.2 %collective-permute-start.14 = (bf16[576,128]{1,0:T(8,128)(2,1)S(1)}, bf16[576,128]{1,0:T(8,128)(2,1)S(1)}, u32[]{:S(2)}, u32[]{:S(2)}) collective-permute-start(bf16[576,128]{1,0:T(8,128)(2,1)S(1)} %maximum_select_fusion.2), channel_id=1, source_target_pairs={{0,4},{1,5},{2,6},{3,7},{4,0},{5,1},{6,2},{7,3},{8,12},{9,13},{10,... | collective-permute-start | bytes 442376 | tf_op jit(solution)/shard_map/ppermute | solution.py:242
  93.7 8.6 %collective-permute-start.18 = (bf16[576,128]{1,0:T(8,128)(2,1)S(1)}, bf16[576,128]{1,0:T(8,128)(2,1)S(1)}, u32[]{:S(2)}, u32[]{:S(2)}) collective-permute-start(bf16[576,128]{1,0:T(8,128)(2,1)S(1)} %maximum_select_fusion.3), channel_id=1, source_target_pairs={{0,4},{1,5},{2,6},{3,7},{4,0},{5,1},{6,2},{7,3},{8,12},{9,13},{10,... | collective-permute-start | bytes 442376 | tf_op jit(solution)/shard_map/ppermute | solution.py:242
  98.1 5.0 %collective-permute-start.15 = (bf16[1152,128]{1,0:T(8,128)(2,1)S(1)}, bf16[1152,128]{1,0:T(8,128)(2,1)S(1)}, u32[]{:S(2)}, u32[]{:S(2)}) collective-permute-start(bf16[1152,128]{1,0:T(8,128)(2,1)S(1)} %maximum_select_fusion), channel_id=1, source_target_pairs={{0,1},{1,0},{2,3},{3,2},{4,5},{5,4},{6,7},{7,6},{8,9},{9,8},{10,11... | collective-permute-start | bytes 884744 | tf_op jit(solution)/shard_map/ppermute | solution.py:242
  102.5 1.8 %collective-permute-start.19 = (bf16[1152,128]{1,0:T(8,128)(2,1)S(1)}, bf16[1152,128]{1,0:T(8,128)(2,1)S(1)}, u32[]{:S(2)}, u32[]{:S(2)}) collective-permute-start(bf16[1152,128]{1,0:T(8,128)(2,1)S(1)} %maximum_select_fusion.1), channel_id=1, source_target_pairs={{0,1},{1,0},{2,3},{3,2},{4,5},{5,4},{6,7},{7,6},{8,9},{9,8},{10,11... | collective-permute-start | bytes 884744 | tf_op jit(solution)/shard_map/ppermute | solution.py:242

commit v3 on v2

--- a/solution.py
+++ b/solution.py
@@ -23,7 +23,7 @@
 
 def fwd_kernel(last, table, *refs):
     if last:
-        own, slow, fast, cot, weight, earlier, mixed, keep, send, xf, basis, cott = refs
+        own, slow, fast, cot, weight, earlier, keep_in, send_in, mixed, keep, send, xf, basis, cott = refs
     else:
         own, slow, fast, cot, weight, mixed, keep, send, xf, basis, cott = refs
     rows, width, _ = own.shape
@@ -71,35 +71,43 @@
             mixed[i, at : at + tile] = acc
     gwt = jnp.dot(cott[...], basis[...], preferred_element_type=jnp.float32)
     dhalf = chan // 2
+    at = nk if last else 0
+    if last:
+        keep[0:nk] = keep_in[...]
+        send[0:nk] = send_in[...]
     for k in range(nk):
         mat = gwt[:, k * HALF : (k + 1) * HALF].T
         low, high = mat[:, :dhalf], mat[:, dhalf:]
-        keep[k] = jnp.where(odd, high, low)
-        send[k] = jnp.where(odd, low, high).astype(jnp.bfloat16)
-
-
-def forward(table, own, slow, fast, cot, weight, h, earlier=None):
+        keep[at + k] = jnp.where(odd, high, low)
+        send[at + k] = jnp.where(odd, low, high).astype(jnp.bfloat16)
+
+
+def forward(table, own, slow, fast, cot, weight, h, earlier=()):
     rows, width, chan = cot.shape
     nk = weight.shape[0]
     smem = pl.BlockSpec(memory_space=pltpu.SMEM)
     vmem = pl.BlockSpec(memory_space=pltpu.VMEM)
-    last = earlier is not None
+    last = len(earlier) > 0
+    count = nk * (1 + last)
     half = pl.BlockSpec((rows, width, HALF), lambda g: (0, 0, h))
     side = pl.BlockSpec((H, width, HALF), lambda g: (0, 0, h))
     wide = pl.BlockSpec((rows, width, chan), lambda g: (0, 0, 0))
     edge = pl.BlockSpec((H, width, HALF), lambda g: (0, 0, 0))
-    part = pl.BlockSpec((nk, HALF, chan // 2), lambda g: (0, 0, 0))
+
+    def part(blocks):
+        return pl.BlockSpec((blocks, HALF, chan // 2), lambda g: (0, 0, 0))
+
     return pl.pallas_call(
         lambda *refs: fwd_kernel(last, *refs),
         grid=(1,),
         in_specs=[smem]
         + [half, edge, side, wide, pl.BlockSpec((nk, HALF, chan), lambda g: (0, h, 0))]
-        + [wide] * last,
-        out_specs=[wide, part, part],
+        + ([wide, part(nk), part(nk)] if last else []),
+        out_specs=[wide, part(count), part(count)],
         out_shape=[
             jax.ShapeDtypeStruct((rows, width, chan), jnp.bfloat16 if last else jnp.float32),
-            jax.ShapeDtypeStruct((nk, HALF, chan // 2), jnp.float32),
-            jax.ShapeDtypeStruct((nk, HALF, chan // 2), jnp.bfloat16),
+            jax.ShapeDtypeStruct((count, HALF, chan // 2), jnp.float32),
+            jax.ShapeDtypeStruct((count, HALF, chan // 2), jnp.bfloat16),
         ],
         scratch_shapes=[
             pltpu.VMEM((rows + 2 * H, width + 2 * PAD, HALF), jnp.float32),
@@ -111,7 +119,7 @@
             flops=0, bytes_accessed=0, transcendentals=0
         ),
         name="forward",
-    )(table, own, slow, fast, cot, weight, *([earlier] if last else []))
+    )(table, own, slow, fast, cot, weight, *earlier)
 
 
 def bwd_kernel(table, cin, win, own, *rest):
@@ -231,56 +239,65 @@
             pltpu.SemaphoreType.DMA((3,)),
         ],
         compiler_params=pltpu.CompilerParams(vmem_limit_bytes=56 * 2**20),
-        cost_estimate=pl.CostEstimate(
-            flops=2 * rows * width * nk * chan * chan, bytes_accessed=12 * 2**20, transcendentals=0
-        ),
+        cost_estimate=pl.CostEstimate(flops=0, bytes_accessed=0, transcendentals=0),
         name="backward",
     )(table, cot, weight)
 
 
+WAITS = (-1, 3)
+ADDED = 4
+TIED = True
+
+
 def swap(value, bit, size):
     return lax.ppermute(value, "lat", [(i, i ^ bit) for i in range(size)])
 
 
-def sums_over_lat(keeps, sends, between):
+def sum_over_lat(keep, send, between):
     size = lax.axis_size("lat")
-    shape = keeps[0].shape
+    shape = keep.shape
     index = lax.axis_index("lat")
-    values = []
-    for keep, send in zip(keeps, sends):
-        got = swap(send.reshape(-1, shape[-1]), 1, size)
-        values.append(keep.reshape(-1, shape[-1]) + got.astype(jnp.float32))
-    bits = [1 << b for b in range(1, size.bit_length() - 1)]
-    halved = bits[1:]
-    for bit in halved:
-        values = between(bit, values)
-        side = (index // bit) % 2
-        count = values[0].shape[0] // 2
-        for j, value in enumerate(values):
-            kept = lax.dynamic_slice_in_dim(value, side * count, count, 0)
-            sent = lax.dynamic_slice_in_dim(value, (1 - side) * count, count, 0)
+    whole = keep.reshape(-1, shape[-1])
+    whole = whole + swap(send.reshape(-1, shape[-1]), 1, size).astype(jnp.float32)
+    (whole,) = between(-1, [whole])
+    values = list(jnp.split(whole, 2))
+    rest = [1 << b for b in range(1, size.bit_length() - 1)]
+    orders = [rest[1:] + rest[:1], rest]
+    for step in range(len(rest) - 1):
+        values = between(step, values)
+        for j in range(2):
+            bit = orders[j][step]
+            side = (index // bit) % 2
+            count = values[j].shape[0] // 2
+            kept = lax.dynamic_slice_in_dim(values[j], side * count, count, 0)
+            sent = lax.dynamic_slice_in_dim(values[j], (1 - side) * count, count, 0)
             got = swap(sent.astype(jnp.bfloat16), bit, size)
             values[j] = kept + got.astype(jnp.float32)
-    for bit in bits[:1]:
-        values = between(bit, values)
-        for j, value in enumerate(values):
-            sent = value.astype(jnp.bfloat16)
-            values[j] = sent.astype(jnp.float32) + swap(sent, bit, size).astype(jnp.float32)
-    values = [value.astype(jnp.bfloat16) for value in values]
-    for bit in reversed(halved):
-        values = between(-bit, values)
-        side = (index // bit) % 2
-        for j, value in enumerate(values):
-            got = swap(value, bit, size)
+    values = between(len(rest) - 1, values)
+    for j in range(2):
+        sent = values[j].astype(jnp.bfloat16)
+        got = swap(sent, orders[j][-1], size)
+        values[j] = (sent.astype(jnp.float32) + got.astype(jnp.float32)).astype(jnp.bfloat16)
+    for step in reversed(range(len(rest) - 1)):
+        values = between(2 * len(rest) - 2 - step, values)
+        for j in range(2):
+            bit = orders[j][step]
+            side = (index // bit) % 2
+            got = swap(values[j], bit, size)
             values[j] = jnp.where(
-                side == 0, jnp.concatenate([value, got]), jnp.concatenate([got, value])
+                side == 0,
+                jnp.concatenate([values[j], got]),
+                jnp.concatenate([got, values[j]]),
             )
-    for j, value in enumerate(values):
+    values = between(2 * len(rest) - 1, values)
+    parts = []
+    for value in values:
         got = swap(value, 1, size)
         first = jnp.where(index % 2 == 0, value, got)
         second = jnp.where(index % 2 == 0, got, value)
-        values[j] = jnp.concatenate([first.reshape(shape), second.reshape(shape)], axis=-1)
-    return values
+        part = (shape[0] // 2, *shape[1:])
+        parts.append(jnp.concatenate([first.reshape(part), second.reshape(part)], axis=-1))
+    return jnp.concatenate(parts, axis=1)
 
 
 def per_device(inputs, cotangent, weight, pat_rows, pat_lons, pat_vals):
@@ -298,9 +315,10 @@
     else:
         head, tail = inputs[:H], inputs[rows - H :]
         to_slow, to_fast = jnp.where(odd, tail, head), jnp.where(odd, head, tail)
-    slow = [
-        lax.ppermute(to_slow[:, :, h * HALF : (h + 1) * HALF], "lat", slow_pairs) for h in range(2)
-    ]
+    part = to_slow[:, :, :HALF]
+    slow = [lax.ppermute(part, "lat", slow_pairs)]
+    rest, part = lax.optimization_barrier((to_slow, part))
+    slow.append(lax.ppermute(rest[:, :, HALF:], "lat", slow_pairs))
     fast = lax.ppermute(to_fast, "lat", fast_pairs)
     side = jnp.full((rows, pat_rows.shape[1], 1), odd, jnp.float32)
     table = [
@@ -312,32 +330,35 @@
     slow[0], fast, edge_slow, edge_fast = lax.optimization_barrier(
         (slow[0], fast, edge_slow, edge_fast)
     )
-    mixed, keep0, send0 = forward(table, inputs, slow[0], fast, cotangent, weight, 0)
-    mixed, edge_slow, edge_fast = lax.optimization_barrier((mixed, edge_slow, edge_fast))
+    partial, *earlier = forward(table, inputs, slow[0], fast, cotangent, weight, 0)
+    partial, edge_slow, edge_fast = lax.optimization_barrier((partial, edge_slow, edge_fast))
     got_far = lax.ppermute(edge_slow, "lat", far_pairs)
     got_near = lax.ppermute(edge_slow, "lat", near_pairs)
     got_fast = lax.ppermute(edge_fast, "lat", fast_pairs)
-    mixed, keep1, send1 = forward(table, inputs, slow[1], fast, cotangent, weight, 1, mixed)
+    mixed, keep, send = forward(table, inputs, slow[1], fast, cotangent, weight, 1, (partial, *earlier))
     scale = 1.0 / math.sqrt(pat_rows.shape[0] * width)
-    waits = {4: 0, 2: 1}
     got = [got_far, got_near]
 
-    def between(bit, values):
-        if bit in waits:
-            at = waits[bit]
-            values, got[at] = lax.optimization_barrier((values, got[at]))
+    def between(step, values):
+        nonlocal grad
+        for j in range(2):
+            if step == WAITS[j]:
+                values, got[j] = lax.optimization_barrier((values, got[j]))
+        if step == ADDED:
+            from_slow = got[0].astype(jnp.float32) + got[1].astype(jnp.float32)
+            from_fast = got_fast.astype(jnp.float32)
+            if rows == H:
+                grad = grad + from_slow + from_fast
+            else:
+                grad = grad.at[:H].add(jnp.where(odd, from_fast, from_slow))
+                grad = grad.at[rows - H :].add(jnp.where(odd, from_slow, from_fast))
+            grad = grad.astype(jnp.bfloat16)
+            if TIED:
+                values, grad = lax.optimization_barrier((values, grad))
         return list(values)
 
-    sums = sums_over_lat([keep0, keep1], [send0, send1], between)
-    grad_weight = jnp.concatenate(sums, axis=1).astype(jnp.float32) * scale
-    from_slow = got[0].astype(jnp.float32) + got[1].astype(jnp.float32)
-    from_fast = got_fast.astype(jnp.float32)
-    if rows == H:
-        grad = grad + from_slow + from_fast
-    else:
-        grad = grad.at[:H].add(jnp.where(odd, from_fast, from_slow))
-        grad = grad.at[rows - H :].add(jnp.where(odd, from_slow, from_fast))
-    return (mixed, grad.astype(jnp.bfloat16), grad_weight)
+    total = sum_over_lat(keep, send, between)
+    return (mixed, grad, total.astype(jnp.float32) * scale)
 
 
 def solution(mesh):

time: 106 us -> 104 us (0.981)
  other arithmetic: 11 us -> 7.57 us
    ppermute x1, starting transfers between devices: 0.08 us -> 2.69 us  [per_device(): got_fast = lax.ppermute(edge_fast, 'lat', fast_pairs)]
    add x6 -> x3, other arithmetic: 4.01 us -> 1.46 us  [the longest x1 1.4 us: sum_over_lat(): whole + swap(send.reshape(-1, shape[-1]), 1, size).astype(jnp.float32)]
    ppermute x14 -> x13, starting transfers between devices: 25.4 us -> 23.1 us  [swap(): return lax.ppermute(value, 'lat', [(i, i ^ bit) for i in range(size)])]
    convert_element_type x3 -> x5, other arithmetic: 4.25 us -> 3.4 us  [the longest x1 3.32 us: between(): grad = grad.astype(jnp.bfloat16)]
    slice x1 -> x2, local copies, waits for them, and re-layouts: 2.61 us -> 3.02 us  [the longest x1 2.1 us: per_device(): part = to_slow[:, :, :HALF]]
    ppermute x14 -> x13, waiting for transfers between devices: 19.4 us -> 19.6 us  [swap(): return lax.ppermute(value, 'lat', [(i, i ^ bit) for i in range(size)])]
  transfers between devices with their start and end apart: 20 -> 19, of which waited for: 9 -> 8; matrix products, arithmetic and copies ran while one was open for 13% -> 9% of each run, Pallas kernels for 37% -> 38%
where the time goes in v3:
time: 104 us
  Pallas kernels  39.7 us (38%)
  starting transfers between devices  31.2 us (30%)
  waiting for transfers between devices  19.6 us (19%)
  other arithmetic  7.57 us (7%)
  local copies, waits for them, and re-layouts  4.98 us (5%)
    ppermute x13, starting transfers between devices, swap(): return lax.ppermute(value, 'lat', [(i, i ^ bit) for i in range(size)])  23.1 us
    pallas_call x2, Pallas kernels, forward(): pl.pallas_call(lambda *refs: fwd_kernel(last, *refs), grid=(1,), in_specs...  22.5 us
    ppermute x13, waiting for transfers between devices, swap(): return lax.ppermute(value, 'lat', [(i, i ^ bit) for i in range(size)])  19.6 us
    pallas_call x1, Pallas kernels, backward(): pl.pallas_call(bwd_kernel, in_specs=[smem] + [pl.BlockSpec(memory_space=p...  17.1 us
    convert_element_type x1, other arithmetic, between(): grad = grad.astype(jnp.bfloat16)  3.32 us
    ppermute x1, starting transfers between devices, per_device(): got_fast = lax.ppermute(edge_fast, 'lat', fast_pairs)  2.69 us
    slice x1, local copies, waits for them, and re-layouts, per_device(): part = to_slow[:, :, :HALF]  2.1 us
  transfers between devices with their start and end apart: 19, of which 8 were waited for; matrix products, arithmetic and copies ran while one was open for 9% of the time, Pallas kernels for 38%

profile of v3, /device:TPU:0, one launch (start us, length us, event | category | flops | bytes accessed | tf_op | source)
XLA Modules:
  0.0 104.0 jit_solution(146870272298504274)
XLA Ops:
  0.6 0.0 copy-start
  0.6 0.0 copy-start.1
  0.7 0.0 copy-start.6
  0.7 0.0 copy-start.7
  0.7 0.5 collective-permute-start.2
  1.2 2.1 %slice.6 = bf16[2,1440,128]{2,1,0:T(8,128)(2,1)} slice(bf16[2,1440,256]{2,1,0:T(8,128)(2,1)} %refs_1_.3), slice={[0:2], [0:1440], [0:128]} | slice | bytes 1474560 | tf_op jit(solution)/shard_map/slice | solution.py:318
  3.3 0.7 collective-permute-start.1
  4.0 0.9 slice.7
  4.9 1.5 %collective-permute-start = (bf16[2,1440,128]{2,1,0:T(8,128)(2,1)}, bf16[2,1440,128]{2,1,0:T(8,128)(2,1)}, u32[]{:S(2)}, u32[]{:S(2)}) collective-permute-start(bf16[2,1440,128]{2,1,0:T(8,128)(2,1)} %slice.7), channel_id=1, source_target_pairs={{1,2},{2,1},{3,4},{4,3},{5,6},{6,5},{7,8},{8,7},{9,10},{10,9},{11,... | collective-permute-start | bytes 2211848 | tf_op jit(solution)/shard_map/ppermute | solution.py:321
  6.5 0.1 constant_dynamic-slice_fusion.1
  6.5 0.0 copy-start.2
  6.6 0.2 copy.12
  6.7 0.2 copy.13
  6.9 0.1 constant_dynamic-slice_fusion
  7.0 0.2 copy.14
  7.2 0.1 pad.23.clone
  7.3 0.7 maximum_maximum_fusion.table.refs_0_
  8.0 17.1 %backward.1 = (f32[2,1440,256]{2,1,0:T(8,128)}, bf16[2,1440,256]{2,1,0:T(8,128)(2,1)}, bf16[2,1440,256]{2,1,0:T(8,128)(2,1)}) custom-call(f32[2,9,10]{2,1,0:T(8,128)} %maximum_maximum_fusion.table.refs_0_, bf16[2,1440,256]{2,1,0:T(8,128)(2,1)} %refs_4_.3, bf16[9,256,256]{2,1,0:T(8,128)(2,1)} %refs_5_.3), custom_call_target="tpu_custom_call" | custom-call | tf_op jit(solution)/shard_map/backward/pallas_call | solution.py:223
  25.1 0.0 collective-permute-done.1.refs_2_
  25.1 0.0 collective-permute-done.2.refs_3_
  25.1 0.0 copy-done.2
  25.2 10.7 %forward.2 = (f32[2,1440,256]{2,1,0:T(8,128)}, f32[9,128,128]{2,1,0:T(8,128)S(1)}, bf16[9,128,128]{2,1,0:T(8,128)(2,1)S(1)}) custom-call(f32[2,9,10]{2,1,0:T(8,128)S(1)} %copy-done.4, bf16[2,1440,256]{2,1,0:T(8,128)(2,1)S(1)} %copy-done.1, bf16[2,1440,128]{2,1,0:T(8,128)(2,1)S(1)} %collective-permute-done.1.refs_2_, ...), custom_call_target="tpu_custom_call" | custom-call | tf_op jit(solution)/shard_map/forward/pallas_call | solution.py:100
  35.9 1.9 %collective-permute-start.4 = (bf16[2,1440,256]{2,1,0:T(8,128)(2,1)}, bf16[2,1440,256]{2,1,0:T(8,128)(2,1)}, u32[]{:S(2)}, u32[]{:S(2)}) collective-permute-start(bf16[2,1440,256]{2,1,0:T(8,128)(2,1)} %get-tuple-element.42), channel_id=1, source_target_pairs={{3,4},{4,3},{7,8},{8,7},{11,12},{12,11},{19,20},{20,19},{23,24},{2... | collective-permute-start | bytes 4423688 | tf_op jit(solution)/shard_map/ppermute | solution.py:335
  37.8 0.0 collective-permute-done.refs_2_
  37.8 11.8 %forward.3 = (bf16[2,1440,256]{2,1,0:T(8,128)(2,1)}, f32[18,128,128]{2,1,0:T(8,128)S(1)}, bf16[18,128,128]{2,1,0:T(8,128)(2,1)S(1)}) custom-call(f32[2,9,10]{2,1,0:T(8,128)S(1)} %copy-done.4, bf16[2,1440,256]{2,1,0:T(8,128)(2,1)S(1)} %copy-done.1, bf16[2,1440,128]{2,1,0:T(8,128)(2,1)} %collective-permute-done.refs_2_, ...), custom_call_target="tpu_custom_call" | custom-call | tf_op jit(solution)/shard_map/forward/pallas_call | solution.py:100
  49.6 1.0 copy-done.3
  50.6 6.9 %collective-permute-start.3 = (bf16[2304,128]{1,0:T(8,128)(2,1)S(1)}, bf16[2304,128]{1,0:T(8,128)(2,1)S(1)}, u32[]{:S(2)}, u32[]{:S(2)}) collective-permute-start(bf16[2304,128]{1,0:T(8,128)(2,1)S(1)} %bitcast.8), channel_id=1, source_target_pairs={{0,1},{1,0},{2,3},{3,2},{4,5},{5,4},{6,7},{7,6},{8,9},{9,8},{10,11... | collective-permute-start | bytes 1769480 | tf_op jit(solution)/shard_map/ppermute | solution.py:253
  57.5 1.6 %collective-permute-done.3 = bf16[2304,128]{1,0:T(8,128)(2,1)S(1)} collective-permute-done((bf16[2304,128]{1,0:T(8,128)(2,1)S(1)}, bf16[2304,128]{1,0:T(8,128)(2,1)S(1)}, u32[]{:S(2)}, u32[]{:S(2)}) %collective-permute-start.3) | collective-permute-done | bytes 589856 | tf_op jit(solution)/shard_map/ppermute | solution.py:253
  59.1 1.4 %bitcast_add_fusion = f32[2304,128]{1,0:T(8,128)S(1)} fusion(f32[18,128,128]{2,1,0:T(8,128)} %copy-done.3, bf16[2304,128]{1,0:T(8,128)(2,1)S(1)} %collective-permute-done.3), kind=kLoop, calls=%fused_computation.2 | loop fusion | flops 589824 | bytes 2949120 | tf_op jit(solution)/shard_map/add | solution.py:261
  60.6 0.0 copy-start.8
  60.6 0.0 collective-permute-done.4
  60.6 0.1 fusion
  60.7 2.5 %collective-permute-start.8 = (bf16[576,128]{1,0:T(8,128)(2,1)S(1)}, bf16[576,128]{1,0:T(8,128)(2,1)S(1)}, u32[]{:S(2)}, u32[]{:S(2)}) collective-permute-start(bf16[576,128]{1,0:T(8,128)(2,1)S(1)} %dynamic-slice_convert_fusion), channel_id=1, source_target_pairs={{0,2},{1,3},{2,0},{3,1},{4,6},{5,7},{6,4},{7,5},{8,10},{9,11},{10,... | collective-permute-start | bytes 442376 | tf_op jit(solution)/shard_map/ppermute | solution.py:253
  63.2 0.7 collective-permute-start.11
  63.9 2.7 %collective-permute-start.14 = (bf16[2,1440,256]{2,1,0:T(8,128)(2,1)S(1)}, bf16[2,1440,256]{2,1,0:T(8,128)(2,1)S(1)}, u32[]{:S(2)}, u32[]{:S(2)}) collective-permute-start(bf16[2,1440,256]{2,1,0:T(8,128)(2,1)S(1)} %copy-done.8), channel_id=1, source_target_pairs={{0,1},{1,0},{2,3},{3,2},{4,5},{5,4},{6,7},{7,6},{8,9},{9,8},{10,11... | collective-permute-start | bytes 4423688 | tf_op jit(solution)/shard_map/ppermute | solution.py:337
  66.6 1.5 %collective-permute-start.5 = (bf16[576,128]{1,0:T(8,128)(2,1)S(1)}, bf16[576,128]{1,0:T(8,128)(2,1)S(1)}, u32[]{:S(2)}, u32[]{:S(2)}) collective-permute-start(bf16[576,128]{1,0:T(8,128)(2,1)S(1)} %dynamic-slice_convert_fusion.1), channel_id=1, source_target_pairs={{0,4},{1,5},{2,6},{3,7},{4,0},{5,1},{6,2},{7,3},{8,12},{9,13},{10,... | collective-permute-start | bytes 442376 | tf_op jit(solution)/shard_map/ppermute | solution.py:253
  68.2 0.0 collective-permute-done.8
  68.2 2.2 %collective-permute-start.9 = (bf16[288,128]{1,0:T(8,128)(2,1)S(1)}, bf16[288,128]{1,0:T(8,128)(2,1)S(1)}, u32[]{:S(2)}, u32[]{:S(2)}) collective-permute-start(bf16[288,128]{1,0:T(8,128)(2,1)S(1)} %dynamic-slice_convert_fusion.2), channel_id=1, source_target_pairs={{0,4},{1,5},{2,6},{3,7},{4,0},{5,1},{6,2},{7,3},{8,12},{9,13},{10,... | collective-permute-start | bytes 221192 | tf_op jit(solution)/shard_map/ppermute | solution.py:253
  70.5 2.8 %collective-permute-done.5 = bf16[576,128]{1,0:T(8,128)(2,1)S(1)} collective-permute-done((bf16[576,128]{1,0:T(8,128)(2,1)S(1)}, bf16[576,128]{1,0:T(8,128)(2,1)S(1)}, u32[]{:S(2)}, u32[]{:S(2)}) %collective-permute-start.5) | collective-permute-done | bytes 147488 | tf_op jit(solution)/shard_map/ppermute | solution.py:253
  73.3 2.7 %collective-permute-start.6 = (bf16[288,128]{1,0:T(8,128)(2,1)S(1)}, bf16[288,128]{1,0:T(8,128)(2,1)S(1)}, u32[]{:S(2)}, u32[]{:S(2)}) collective-permute-start(bf16[288,128]{1,0:T(8,128)(2,1)S(1)} %dynamic-slice_convert_fusion.3), channel_id=1, source_target_pairs={{0,8},{1,9},{2,10},{3,11},{4,12},{5,13},{6,14},{7,15},{8,0},{9,1},... | collective-permute-start | bytes 221192 | tf_op jit(solution)/shard_map/ppermute | solution.py:253
  76.1 0.0 collective-permute-done.9
  76.1 0.7 collective-permute-start.10
  76.8 4.1 %collective-permute-done.6 = bf16[288,128]{1,0:T(8,128)(2,1)S(1)} collective-permute-done((bf16[288,128]{1,0:T(8,128)(2,1)S(1)}, bf16[288,128]{1,0:T(8,128)(2,1)S(1)}, u32[]{:S(2)}, u32[]{:S(2)}) %collective-permute-start.6) | collective-permute-done | bytes 73760 | tf_op jit(solution)/shard_map/ppermute | solution.py:253
  81.0 2.7 %collective-permute-start.7 = (bf16[288,128]{1,0:T(8,128)(2,1)S(1)}, bf16[288,128]{1,0:T(8,128)(2,1)S(1)}, u32[]{:S(2)}, u32[]{:S(2)}) collective-permute-start(bf16[288,128]{1,0:T(8,128)(2,1)S(1)} %add_convert_fusion.4), channel_id=1, source_target_pairs={{0,2},{1,3},{2,0},{3,1},{4,6},{5,7},{6,4},{7,5},{8,10},{9,11},{10,... | collective-permute-start | bytes 221192 | tf_op jit(solution)/shard_map/ppermute | solution.py:253
  83.6 0.0 collective-permute-done.10
  83.6 3.6 %collective-permute-done.7 = bf16[288,128]{1,0:T(8,128)(2,1)S(1)} collective-permute-done((bf16[288,128]{1,0:T(8,128)(2,1)S(1)}, bf16[288,128]{1,0:T(8,128)(2,1)S(1)}, u32[]{:S(2)}, u32[]{:S(2)}) %collective-permute-start.7) | collective-permute-done | bytes 73760 | tf_op jit(solution)/shard_map/ppermute | solution.py:253
  87.3 0.0 collective-permute-done.11
  87.3 1.5 %collective-permute-start.13 = (bf16[288,128]{1,0:T(8,128)(2,1)S(1)}, bf16[288,128]{1,0:T(8,128)(2,1)S(1)}, u32[]{:S(2)}, u32[]{:S(2)}) collective-permute-start(bf16[288,128]{1,0:T(8,128)(2,1)S(1)} %add_convert_fusion.1), channel_id=1, source_target_pairs={{0,4},{1,5},{2,6},{3,7},{4,0},{5,1},{6,2},{7,3},{8,12},{9,13},{10,... | collective-permute-start | bytes 221192 | tf_op jit(solution)/shard_map/ppermute | solution.py:253
  88.8 1.1 %collective-permute-start.12 = (bf16[288,128]{1,0:T(8,128)(2,1)S(1)}, bf16[288,128]{1,0:T(8,128)(2,1)S(1)}, u32[]{:S(2)}, u32[]{:S(2)}) collective-permute-start(bf16[288,128]{1,0:T(8,128)(2,1)S(1)} %add_convert_fusion.3), channel_id=1, source_target_pairs={{0,8},{1,9},{2,10},{3,11},{4,12},{5,13},{6,14},{7,15},{8,0},{9,1},... | collective-permute-start | bytes 221192 | tf_op jit(solution)/shard_map/ppermute | solution.py:253
  89.9 0.0 collective-permute-done.14
  89.9 3.3 %add_convert_fusion = bf16[2,1440,256]{2,1,0:T(8,128)(2,1)} fusion(bf16[2,1440,256]{2,1,0:T(8,128)(2,1)S(1)} %collective-permute-done.14, f32[2,1440,256]{2,1,0:T(8,128)S(1)} %copy-done.5, bf16[2,1440,256]{2,1,0:T(8,128)(2,1)S(1)} %collective-permute-done.11, bf16[2,1440,256]{2,1,0:T(8,128)(2,1)} %collective-permute-done.4), kind=kLoop, calls=%fused_computation | loop fusion | flops 5160960 | bytes 8847360 | tf_op jit(solution)/shard_map/convert_element_type | solution.py:355
  93.2 0.0 collective-permute-done.13
  93.3 1.6 %collective-permute-done.12 = bf16[288,128]{1,0:T(8,128)(2,1)S(1)} collective-permute-done((bf16[288,128]{1,0:T(8,128)(2,1)S(1)}, bf16[288,128]{1,0:T(8,128)(2,1)S(1)}, u32[]{:S(2)}, u32[]{:S(2)}) %collective-permute-start.12) | collective-permute-done | bytes 73760 | tf_op jit(solution)/shard_map/ppermute | solution.py:253
  94.9 0.1 collective-permute-start.15
  95.0 0.6 collective-permute-start.17
  95.6 4.6 %collective-permute-done.15 = bf16[576,128]{1,0:T(8,128)(2,1)S(1)} collective-permute-done((bf16[576,128]{1,0:T(8,128)(2,1)S(1)}, bf16[576,128]{1,0:T(8,128)(2,1)S(1)}, u32[]{:S(2)}, u32[]{:S(2)}) %collective-permute-start.15) | collective-permute-done | bytes 147488 | tf_op jit(solution)/shard_map/ppermute | solution.py:253
  100.1 0.1 maximum_select_fusion
  100.2 0.1 collective-permute-start.16
  100.3 0.0 collective-permute-done.17
  100.3 0.1 maximum_select_fusion.1
  100.4 0.5 collective-permute-start.18
  101.0 0.9 collective-permute-done.16
  101.9 0.4 collective-permute-done.18
  102.3 1.6 %convert_multiply_fusion = f32[9,256,256]{2,1,0:T(8,128)} fusion(bf16[9,128,128]{2,1,0:T(8,128)(2,1)S(1)} %bitcast.12, bf16[9,128,128]{2,1,0:T(8,128)(2,1)S(1)} %bitcast.11, bf16[9,128,128]{2,1,0:T(8,128)(2,1)S(1)} %bitcast.10, bf16[9,128,128]{2,1,0:T(8,128)(2,1)S(1)} %bitcast.9), kind=kLoop, calls=%fused_computation.1 | loop fusion | flops 5308416 | bytes 3538944 | tf_op jit(solution)/shard_map/mul | solution.py:361
  (26 shorter events, 0.4 us)
Async XLA Ops:
  0.6 6.3 %copy-start = (f32[32,9,3]{0,2,1:T(4,128)S(1)}, f32[32,9,3]{0,2,1:T(4,128)}, u32[]{:S(2)}) copy-start(f32[32,9,3]{0,2,1:T(4,128)} %param.11) | copy-start | bytes 10372
  0.6 3.4 %copy-start.1 = (bf16[2,1440,256]{2,1,0:T(8,128)(2,1)S(1)}, bf16[2,1440,256]{2,1,0:T(8,128)(2,1)}, u32[]{:S(2)}) copy-start(bf16[2,1440,256]{2,1,0:T(8,128)(2,1)} %refs_1_.3) | copy-start | bytes 4423684
  0.7 5.8 %copy-start.6 = (s32[32,9,3]{0,2,1:T(4,128)S(1)}, s32[32,9,3]{0,2,1:T(4,128)}, u32[]{:S(2)}) copy-start(s32[32,9,3]{0,2,1:T(4,128)} %param.10) | copy-start | bytes 10372
  0.7 5.8 %copy-start.7 = (s32[32,9,3]{0,2,1:T(4,128)S(1)}, s32[32,9,3]{0,2,1:T(4,128)}, u32[]{:S(2)}) copy-start(s32[32,9,3]{0,2,1:T(4,128)} %param.9) | copy-start | bytes 10372
  0.7 24.5 %collective-permute-start.2 = (bf16[2,1440,256]{2,1,0:T(8,128)(2,1)}, bf16[2,1440,256]{2,1,0:T(8,128)(2,1)}, u32[]{:S(2)}, u32[]{:S(2)}) collective-permute-start(bf16[2,1440,256]{2,1,0:T(8,128)(2,1)} %refs_1_.3), channel_id=1, source_target_pairs={{0,1},{1,0},{2,3},{3,2},{4,5},{5,4},{6,7},{7,6},{8,9},{9,8},{10,11... | collective-permute-start | bytes 4423688 | tf_op jit(solution)/shard_map/ppermute | solution.py:322
  3.3 21.8 %collective-permute-start.1 = (bf16[2,1440,128]{2,1,0:T(8,128)(2,1)}, bf16[2,1440,128]{2,1,0:T(8,128)(2,1)S(1)}, u32[]{:S(2)}, u32[]{:S(2)}) collective-permute-start(bf16[2,1440,128]{2,1,0:T(8,128)(2,1)} %slice.6), channel_id=1, source_target_pairs={{1,2},{2,1},{3,4},{4,3},{5,6},{6,5},{7,8},{8,7},{9,10},{10,9},{11,... | collective-permute-start | bytes 2211848 | tf_op jit(solution)/shard_map/ppermute | solution.py:319
  4.9 32.9 %collective-permute-start = (bf16[2,1440,128]{2,1,0:T(8,128)(2,1)}, bf16[2,1440,128]{2,1,0:T(8,128)(2,1)}, u32[]{:S(2)}, u32[]{:S(2)}) collective-permute-start(bf16[2,1440,128]{2,1,0:T(8,128)(2,1)} %slice.7), channel_id=1, source_target_pairs={{1,2},{2,1},{3,4},{4,3},{5,6},{6,5},{7,8},{8,7},{9,10},{10,9},{11,... | collective-permute-start | bytes 2211848 | tf_op jit(solution)/shard_map/ppermute | solution.py:321
  6.5 18.6 %copy-start.2 = (bf16[9,256,256]{2,1,0:T(8,128)(2,1)S(1)}, bf16[9,256,256]{2,1,0:T(8,128)(2,1)}, u32[]{:S(2)}) copy-start(bf16[9,256,256]{2,1,0:T(8,128)(2,1)} %refs_5_.3) | copy-start | bytes 3538948
  8.0 17.2 %copy-start.4 = (f32[2,9,10]{2,1,0:T(8,128)S(1)}, f32[2,9,10]{2,1,0:T(8,128)}, u32[]{:S(2)}) copy-start(f32[2,9,10]{2,1,0:T(8,128)} %maximum_maximum_fusion.table.refs_0_) | copy-start | bytes 2164
  35.9 24.7 %collective-permute-start.4 = (bf16[2,1440,256]{2,1,0:T(8,128)(2,1)}, bf16[2,1440,256]{2,1,0:T(8,128)(2,1)}, u32[]{:S(2)}, u32[]{:S(2)}) collective-permute-start(bf16[2,1440,256]{2,1,0:T(8,128)(2,1)} %get-tuple-element.42), channel_id=1, source_target_pairs={{3,4},{4,3},{7,8},{8,7},{11,12},{12,11},{19,20},{20,19},{23,24},{2... | collective-permute-start | bytes 4423688 | tf_op jit(solution)/shard_map/ppermute | solution.py:335
  49.6 1.0 copy-start.3
  50.6 8.6 %collective-permute-start.3 = (bf16[2304,128]{1,0:T(8,128)(2,1)S(1)}, bf16[2304,128]{1,0:T(8,128)(2,1)S(1)}, u32[]{:S(2)}, u32[]{:S(2)}) collective-permute-start(bf16[2304,128]{1,0:T(8,128)(2,1)S(1)} %bitcast.8), channel_id=1, source_target_pairs={{0,1},{1,0},{2,3},{3,2},{4,5},{5,4},{6,7},{7,6},{8,9},{9,8},{10,11... | collective-permute-start | bytes 1769480 | tf_op jit(solution)/shard_map/ppermute | solution.py:253
  60.6 3.4 %copy-start.8 = (bf16[2,1440,256]{2,1,0:T(8,128)(2,1)S(1)}, bf16[2,1440,256]{2,1,0:T(8,128)(2,1)}, u32[]{:S(2)}) copy-start(bf16[2,1440,256]{2,1,0:T(8,128)(2,1)} %get-tuple-element.49) | copy-start | bytes 4423684
  60.7 7.5 %collective-permute-start.8 = (bf16[576,128]{1,0:T(8,128)(2,1)S(1)}, bf16[576,128]{1,0:T(8,128)(2,1)S(1)}, u32[]{:S(2)}, u32[]{:S(2)}) collective-permute-start(bf16[576,128]{1,0:T(8,128)(2,1)S(1)} %dynamic-slice_convert_fusion), channel_id=1, source_target_pairs={{0,2},{1,3},{2,0},{3,1},{4,6},{5,7},{6,4},{7,5},{8,10},{9,11},{10,... | collective-permute-start | bytes 442376 | tf_op jit(solution)/shard_map/ppermute | solution.py:253
  63.2 24.1 %collective-permute-start.11 = (bf16[2,1440,256]{2,1,0:T(8,128)(2,1)}, bf16[2,1440,256]{2,1,0:T(8,128)(2,1)S(1)}, u32[]{:S(2)}, u32[]{:S(2)}) collective-permute-start(bf16[2,1440,256]{2,1,0:T(8,128)(2,1)} %get-tuple-element.42), channel_id=1, source_target_pairs={{1,2},{2,1},{5,6},{6,5},{9,10},{10,9},{13,14},{14,13},{17,18},{18,... | collective-permute-start | bytes 4423688 | tf_op jit(solution)/shard_map/ppermute | solution.py:336
  63.9 26.0 %collective-permute-start.14 = (bf16[2,1440,256]{2,1,0:T(8,128)(2,1)S(1)}, bf16[2,1440,256]{2,1,0:T(8,128)(2,1)S(1)}, u32[]{:S(2)}, u32[]{:S(2)}) collective-permute-start(bf16[2,1440,256]{2,1,0:T(8,128)(2,1)S(1)} %copy-done.8), channel_id=1, source_target_pairs={{0,1},{1,0},{2,3},{3,2},{4,5},{5,4},{6,7},{7,6},{8,9},{9,8},{10,11... | collective-permute-start | bytes 4423688 | tf_op jit(solution)/shard_map/ppermute | solution.py:337
  66.6 23.3 %copy-start.5 = (f32[2,1440,256]{2,1,0:T(8,128)S(1)}, f32[2,1440,256]{2,1,0:T(8,128)}, u32[]{:S(2)}) copy-start(f32[2,1440,256]{2,1,0:T(8,128)} %get-tuple-element.46) | copy-start | bytes 8847364
  66.6 6.6 %collective-permute-start.5 = (bf16[576,128]{1,0:T(8,128)(2,1)S(1)}, bf16[576,128]{1,0:T(8,128)(2,1)S(1)}, u32[]{:S(2)}, u32[]{:S(2)}) collective-permute-start(bf16[576,128]{1,0:T(8,128)(2,1)S(1)} %dynamic-slice_convert_fusion.1), channel_id=1, source_target_pairs={{0,4},{1,5},{2,6},{3,7},{4,0},{5,1},{6,2},{7,3},{8,12},{9,13},{10,... | collective-permute-start | bytes 442376 | tf_op jit(solution)/shard_map/ppermute | solution.py:253
  68.2 7.9 %collective-permute-start.9 = (bf16[288,128]{1,0:T(8,128)(2,1)S(1)}, bf16[288,128]{1,0:T(8,128)(2,1)S(1)}, u32[]{:S(2)}, u32[]{:S(2)}) collective-permute-start(bf16[288,128]{1,0:T(8,128)(2,1)S(1)} %dynamic-slice_convert_fusion.2), channel_id=1, source_target_pairs={{0,4},{1,5},{2,6},{3,7},{4,0},{5,1},{6,2},{7,3},{8,12},{9,13},{10,... | collective-permute-start | bytes 221192 | tf_op jit(solution)/shard_map/ppermute | solution.py:253
  73.3 7.6 %collective-permute-start.6 = (bf16[288,128]{1,0:T(8,128)(2,1)S(1)}, bf16[288,128]{1,0:T(8,128)(2,1)S(1)}, u32[]{:S(2)}, u32[]{:S(2)}) collective-permute-start(bf16[288,128]{1,0:T(8,128)(2,1)S(1)} %dynamic-slice_convert_fusion.3), channel_id=1, source_target_pairs={{0,8},{1,9},{2,10},{3,11},{4,12},{5,13},{6,14},{7,15},{8,0},{9,1},... | collective-permute-start | bytes 221192 | tf_op jit(solution)/shard_map/ppermute | solution.py:253
  76.1 7.5 %collective-permute-start.10 = (bf16[288,128]{1,0:T(8,128)(2,1)S(1)}, bf16[288,128]{1,0:T(8,128)(2,1)S(1)}, u32[]{:S(2)}, u32[]{:S(2)}) collective-permute-start(bf16[288,128]{1,0:T(8,128)(2,1)S(1)} %add_convert_fusion.2), channel_id=1, source_target_pairs={{0,8},{1,9},{2,10},{3,11},{4,12},{5,13},{6,14},{7,15},{8,0},{9,1},... | collective-permute-start | bytes 221192 | tf_op jit(solution)/shard_map/ppermute | solution.py:253
  81.0 6.3 %collective-permute-start.7 = (bf16[288,128]{1,0:T(8,128)(2,1)S(1)}, bf16[288,128]{1,0:T(8,128)(2,1)S(1)}, u32[]{:S(2)}, u32[]{:S(2)}) collective-permute-start(bf16[288,128]{1,0:T(8,128)(2,1)S(1)} %add_convert_fusion.4), channel_id=1, source_target_pairs={{0,2},{1,3},{2,0},{3,1},{4,6},{5,7},{6,4},{7,5},{8,10},{9,11},{10,... | collective-permute-start | bytes 221192 | tf_op jit(solution)/shard_map/ppermute | solution.py:253
  87.3 5.9 %collective-permute-start.13 = (bf16[288,128]{1,0:T(8,128)(2,1)S(1)}, bf16[288,128]{1,0:T(8,128)(2,1)S(1)}, u32[]{:S(2)}, u32[]{:S(2)}) collective-permute-start(bf16[288,128]{1,0:T(8,128)(2,1)S(1)} %add_convert_fusion.1), channel_id=1, source_target_pairs={{0,4},{1,5},{2,6},{3,7},{4,0},{5,1},{6,2},{7,3},{8,12},{9,13},{10,... | collective-permute-start | bytes 221192 | tf_op jit(solution)/shard_map/ppermute | solution.py:253
  88.8 6.0 %collective-permute-start.12 = (bf16[288,128]{1,0:T(8,128)(2,1)S(1)}, bf16[288,128]{1,0:T(8,128)(2,1)S(1)}, u32[]{:S(2)}, u32[]{:S(2)}) collective-permute-start(bf16[288,128]{1,0:T(8,128)(2,1)S(1)} %add_convert_fusion.3), channel_id=1, source_target_pairs={{0,8},{1,9},{2,10},{3,11},{4,12},{5,13},{6,14},{7,15},{8,0},{9,1},... | collective-permute-start | bytes 221192 | tf_op jit(solution)/shard_map/ppermute | solution.py:253
  94.9 5.2 %collective-permute-start.15 = (bf16[576,128]{1,0:T(8,128)(2,1)S(1)}, bf16[576,128]{1,0:T(8,128)(2,1)S(1)}, u32[]{:S(2)}, u32[]{:S(2)}) collective-permute-start(bf16[576,128]{1,0:T(8,128)(2,1)S(1)} %maximum_select_fusion.2), channel_id=1, source_target_pairs={{0,4},{1,5},{2,6},{3,7},{4,0},{5,1},{6,2},{7,3},{8,12},{9,13},{10,... | collective-permute-start | bytes 442376 | tf_op jit(solution)/shard_map/ppermute | solution.py:253
  95.0 5.3 %collective-permute-start.17 = (bf16[576,128]{1,0:T(8,128)(2,1)S(1)}, bf16[576,128]{1,0:T(8,128)(2,1)S(1)}, u32[]{:S(2)}, u32[]{:S(2)}) collective-permute-start(bf16[576,128]{1,0:T(8,128)(2,1)S(1)} %maximum_select_fusion.3), channel_id=1, source_target_pairs={{0,2},{1,3},{2,0},{3,1},{4,6},{5,7},{6,4},{7,5},{8,10},{9,11},{10,... | collective-permute-start | bytes 442376 | tf_op jit(solution)/shard_map/ppermute | solution.py:253
  100.2 1.6 %collective-permute-start.16 = (bf16[1152,128]{1,0:T(8,128)(2,1)S(1)}, bf16[1152,128]{1,0:T(8,128)(2,1)S(1)}, u32[]{:S(2)}, u32[]{:S(2)}) collective-permute-start(bf16[1152,128]{1,0:T(8,128)(2,1)S(1)} %maximum_select_fusion), channel_id=1, source_target_pairs={{0,1},{1,0},{2,3},{3,2},{4,5},{5,4},{6,7},{7,6},{8,9},{9,8},{10,11... | collective-permute-start | bytes 884744 | tf_op jit(solution)/shard_map/ppermute | solution.py:253
  100.4 1.9 %collective-permute-start.18 = (bf16[1152,128]{1,0:T(8,128)(2,1)S(1)}, bf16[1152,128]{1,0:T(8,128)(2,1)S(1)}, u32[]{:S(2)}, u32[]{:S(2)}) collective-permute-start(bf16[1152,128]{1,0:T(8,128)(2,1)S(1)} %maximum_select_fusion.1), channel_id=1, source_target_pairs={{0,1},{1,0},{2,3},{3,2},{4,5},{5,4},{6,7},{7,6},{8,9},{9,8},{10,11... | collective-permute-start | bytes 884744 | tf_op jit(solution)/shard_map/ppermute | solution.py:253

commit v4 on v3

--- a/solution.py
+++ b/solution.py
@@ -23,25 +23,28 @@
 
 def fwd_kernel(last, table, *refs):
     if last:
-        own, slow, fast, cot, weight, earlier, keep_in, send_in, mixed, keep, send, xf, basis, cott = refs
+        own, near, far, fast, cot, weight, earlier, keep_in, send_in, mixed, keep, send, xf, basis, cott = refs
     else:
-        own, slow, fast, cot, weight, mixed, keep, send, xf, basis, cott = refs
+        own, near, far, fast, cot, weight, mixed, keep, send, xf, basis, cott = refs
     rows, width, _ = own.shape
     chan = cot.shape[2]
     nk = weight.shape[0]
     ne = table.shape[2] // 3
     odd = table[0, 0, 3 * ne] > 0.5
 
-    def widen(src, r, dst):
+    def widen(src, r, dst, more=None):
         def part(at, to):
-            xf[dst, to] = src[r, at].astype(jnp.float32)
+            piece = src[r, at].astype(jnp.float32)
+            if more is not None:
+                piece = piece + more[r, at].astype(jnp.float32)
+            xf[dst, to] = piece
 
         part(slice(0, width), slice(PAD, PAD + width))
         part(slice(width - PAD, width), slice(0, PAD))
         part(slice(0, PAD), slice(PAD + width, 2 * PAD + width))
 
     for r in range(H):
-        widen(slow, r, jnp.where(odd, H + rows, 0) + r)
+        widen(near, r, jnp.where(odd, H + rows, 0) + r, far)
         widen(fast, r, jnp.where(odd, 0, H + rows) + r)
     for r in range(rows):
         widen(own, r, H + r)
@@ -82,7 +85,7 @@
         send[at + k] = jnp.where(odd, low, high).astype(jnp.bfloat16)
 
 
-def forward(table, own, slow, fast, cot, weight, h, earlier=()):
+def forward(table, own, near, far, fast, cot, weight, h, earlier=()):
     rows, width, chan = cot.shape
     nk = weight.shape[0]
     smem = pl.BlockSpec(memory_space=pltpu.SMEM)
@@ -101,7 +104,7 @@
         lambda *refs: fwd_kernel(last, *refs),
         grid=(1,),
         in_specs=[smem]
-        + [half, edge, side, wide, pl.BlockSpec((nk, HALF, chan), lambda g: (0, h, 0))]
+        + [half, edge, side, side, wide, pl.BlockSpec((nk, HALF, chan), lambda g: (0, h, 0))]
         + ([wide, part(nk), part(nk)] if last else []),
         out_specs=[wide, part(count), part(count)],
         out_shape=[
@@ -114,12 +117,12 @@
             pltpu.VMEM((rows * width, nk * HALF), jnp.bfloat16),
             pltpu.VMEM((chan, rows * width), jnp.bfloat16),
         ],
-        compiler_params=pltpu.CompilerParams(vmem_limit_bytes=48 * 2**20),
+        compiler_params=pltpu.CompilerParams(vmem_limit_bytes=32 * 2**20),
         cost_estimate=pl.CostEstimate(
             flops=0, bytes_accessed=0, transcendentals=0
         ),
         name="forward",
-    )(table, own, slow, fast, cot, weight, *earlier)
+    )(table, own, near, far, fast, cot, weight, *earlier)
 
 
 def bwd_kernel(table, cin, win, own, *rest):
@@ -131,7 +134,7 @@
     odd = table[0, 0, 3 * ne] > 0.5
     nh = chan // HALF
     lines = rows + 2 * H
-    cap = rows * nk * ne + GROUP
+    cap = rows * nk * ne + 2 * GROUP
     for line in range(lines):
         cnt[line] = 0
 
@@ -148,10 +151,11 @@
                 cnt[line] = c + 1
             return carry
 
-        lax.fori_loop(0, nk, bin_one, 0)
+        for k in range(nk):
+            bin_one(k, 0)
     for line in range(lines):
         c = cnt[line]
-        for g in range(GROUP):
+        for g in range(2 * GROUP):
             lst_n[line * cap + c + g] = 0
             lst_o[line * cap + c + g] = PAD
             lst_v[line * cap + c + g] = 0.0
@@ -175,7 +179,8 @@
             s = x if s is None else s + x
         return s
 
-    def line_sum(t, slot):
+    def line_sum(t, slot, dst, row):
+        groups = jnp.maximum((cnt[t] + GROUP - 1) // GROUP, 2)
         for h in range(nh):
             acc[slot, :, h * HALF : (h + 1) * HALF] = terms(t, 0, h)
 
@@ -185,12 +190,15 @@
                 acc[slot, :, cols] = acc[slot, :, cols] + terms(t, g, h)
             return carry
 
-        lax.fori_loop(1, (cnt[t] + GROUP - 1) // GROUP, group, 0)
+        lax.fori_loop(1, groups - 1, group, 0)
+        for h in range(nh):
+            cols = slice(h * HALF, (h + 1) * HALF)
+            total = acc[slot, :, cols] + terms(t, groups - 1, h)
+            dst[row, :, cols] = total.astype(dst.dtype)
 
     def edge(s, carry):
         top = (s < H) != odd
-        line_sum(jnp.where(top, 0, H + rows) + s % H, rows)
-        narrow[s] = acc[rows].astype(narrow.dtype)
+        line_sum(jnp.where(top, 0, H + rows) + s % H, rows, narrow, s)
         return carry
 
     lax.fori_loop(0, 2 * H, edge, 0)
@@ -198,16 +206,13 @@
         pltpu.make_async_copy(narrow.at[0:H], edges[0], out_sems.at[0]),
         pltpu.make_async_copy(narrow.at[H:], edges[1], out_sems.at[1]),
     ]
-    writes.append(pltpu.make_async_copy(acc.at[0:rows], own, out_sems.at[2]))
+    for r in range(rows):
+        writes.append(pltpu.make_async_copy(acc.at[r], own.at[r], out_sems.at[2 + r]))
     for write in writes[:2]:
         write.start()
-
-    def inner(s, carry):
-        line_sum(s + H, s)
-        return carry
-
-    lax.fori_loop(0, rows, inner, 0)
-    writes[2].start()
+    for r in range(rows):
+        line_sum(H + r, r, acc, r)
+        writes[2 + r].start()
     for write in writes:
         write.wait()
 
@@ -219,7 +224,7 @@
     smem = pl.BlockSpec(memory_space=pltpu.SMEM)
     anym = pl.BlockSpec(memory_space=pl.ANY)
     lines = rows + 2 * H
-    cap = rows * nk * ne + GROUP
+    cap = rows * nk * ne + 2 * GROUP
     return pl.pallas_call(
         bwd_kernel,
         in_specs=[smem] + [pl.BlockSpec(memory_space=pltpu.VMEM)] * 2,
@@ -236,7 +241,7 @@
             pltpu.SMEM((lines * cap,), jnp.int32),
             pltpu.SMEM((lines * cap,), jnp.int32),
             pltpu.SMEM((lines * cap,), jnp.float32),
-            pltpu.SemaphoreType.DMA((3,)),
+            pltpu.SemaphoreType.DMA((2 + rows,)),
         ],
         compiler_params=pltpu.CompilerParams(vmem_limit_bytes=56 * 2**20),
         cost_estimate=pl.CostEstimate(flops=0, bytes_accessed=0, transcendentals=0),
@@ -315,10 +320,11 @@
     else:
         head, tail = inputs[:H], inputs[rows - H :]
         to_slow, to_fast = jnp.where(odd, tail, head), jnp.where(odd, head, tail)
+    far = lax.ppermute(to_slow, "lat", far_pairs)
     part = to_slow[:, :, :HALF]
-    slow = [lax.ppermute(part, "lat", slow_pairs)]
+    near = [lax.ppermute(part, "lat", near_pairs)]
     rest, part = lax.optimization_barrier((to_slow, part))
-    slow.append(lax.ppermute(rest[:, :, HALF:], "lat", slow_pairs))
+    near.append(lax.ppermute(rest[:, :, HALF:], "lat", near_pairs))
     fast = lax.ppermute(to_fast, "lat", fast_pairs)
     side = jnp.full((rows, pat_rows.shape[1], 1), odd, jnp.float32)
     table = [
@@ -327,26 +333,28 @@
     ]
     table = jnp.concatenate([*table, side], axis=-1)
     grad, edge_slow, edge_fast = backward(table, cotangent, weight)
-    slow[0], fast, edge_slow, edge_fast = lax.optimization_barrier(
-        (slow[0], fast, edge_slow, edge_fast)
+    near[0], far, fast, edge_slow, edge_fast = lax.optimization_barrier(
+        (near[0], far, fast, edge_slow, edge_fast)
     )
-    partial, *earlier = forward(table, inputs, slow[0], fast, cotangent, weight, 0)
+    partial, *earlier = forward(table, inputs, near[0], far, fast, cotangent, weight, 0)
     partial, edge_slow, edge_fast = lax.optimization_barrier((partial, edge_slow, edge_fast))
     got_far = lax.ppermute(edge_slow, "lat", far_pairs)
     got_near = lax.ppermute(edge_slow, "lat", near_pairs)
     got_fast = lax.ppermute(edge_fast, "lat", fast_pairs)
-    mixed, keep, send = forward(table, inputs, slow[1], fast, cotangent, weight, 1, (partial, *earlier))
+    mixed, keep, send = forward(table, inputs, near[1], far, fast, cotangent, weight, 1, (partial, *earlier))
     scale = 1.0 / math.sqrt(pat_rows.shape[0] * width)
-    got = [got_far, got_near]
+    got = [got_far, got_near, got_fast]
 
     def between(step, values):
         nonlocal grad
         for j in range(2):
             if step == WAITS[j]:
                 values, got[j] = lax.optimization_barrier((values, got[j]))
+        if step == WAITS[0]:
+            values, got[2] = lax.optimization_barrier((values, got[2]))
         if step == ADDED:
             from_slow = got[0].astype(jnp.float32) + got[1].astype(jnp.float32)
-            from_fast = got_fast.astype(jnp.float32)
+            from_fast = got[2].astype(jnp.float32)
             if rows == H:
                 grad = grad + from_slow + from_fast
             else:

time: 104 us -> 103 us (level)
  starting transfers between devices: 31.2 us -> 26 us
  waiting for transfers between devices: 19.6 us -> 23 us
    ppermute x13, starting transfers between devices: 23.1 us -> 13.7 us  [swap(): return lax.ppermute(value, 'lat', [(i, i ^ bit) for i in range(size)])]
    ppermute x13, waiting for transfers between devices: 19.6 us -> 23 us  [swap(): return lax.ppermute(value, 'lat', [(i, i ^ bit) for i in range(size)])]
    ppermute x2 -> x3, starting transfers between devices: 2.22 us -> 5 us  [the longest x1 1.91 us: per_device(): far = lax.ppermute(to_slow, 'lat', far_pairs)]
    ppermute x1, starting transfers between devices: 2.69 us -> 4.02 us  [per_device(): got_fast = lax.ppermute(edge_fast, 'lat', fast_pairs)]
  transfers between devices with their start and end apart: 19 -> 20, of which waited for: 8 -> 12; matrix products, arithmetic and copies ran while one was open for 9% -> 10% of each run, Pallas kernels for 38% -> 39%
where the time goes in v4:
time: 103 us; the launch traced here: 102 us
  Pallas kernels  39.6 us (38%)
  starting transfers between devices  26 us (25%)
  waiting for transfers between devices  23 us (22%)
  other arithmetic  7.99 us (8%)
  local copies, waits for them, and re-layouts  4.9 us (5%)
    ppermute x13, waiting for transfers between devices, swap(): return lax.ppermute(value, 'lat', [(i, i ^ bit) for i in range(size)])  23 us
    pallas_call x2, Pallas kernels, forward(): pl.pallas_call(lambda *refs: fwd_kernel(last, *refs), grid=(1,), in_specs...  22.2 us
    pallas_call x1, Pallas kernels, backward(): pl.pallas_call(bwd_kernel, in_specs=[smem] + [pl.BlockSpec(memory_space=p...  17.5 us
    ppermute x13, starting transfers between devices, swap(): return lax.ppermute(value, 'lat', [(i, i ^ bit) for i in range(size)])  13.7 us
    ppermute x1, starting transfers between devices, per_device(): got_fast = lax.ppermute(edge_fast, 'lat', fast_pairs)  4.02 us
    convert_element_type x1, other arithmetic, between(): grad = grad.astype(jnp.bfloat16)  3.75 us
  transfers between devices with their start and end apart: 20, of which 12 were waited for; matrix products, arithmetic and copies ran while one was open for 10% of the time, Pallas kernels for 39%

profile of v4, /device:TPU:0, one launch (start us, length us, event | category | flops | bytes accessed | tf_op | source)
XLA Modules:
  0.0 102.4 jit_solution(2224813919258518238)
XLA Ops:
  0.6 0.0 copy-start
  0.7 1.9 %collective-permute-start.2 = (bf16[2,1440,256]{2,1,0:T(8,128)(2,1)}, bf16[2,1440,256]{2,1,0:T(8,128)(2,1)}, u32[]{:S(2)}, u32[]{:S(2)}) collective-permute-start(bf16[2,1440,256]{2,1,0:T(8,128)(2,1)} %refs_1_.3), channel_id=1, source_target_pairs={{3,4},{4,3},{7,8},{8,7},{11,12},{12,11},{19,20},{20,19},{23,24},{2... | collective-permute-start | bytes 4423688 | tf_op jit(solution)/shard_map/ppermute | solution.py:323
  2.6 0.5 collective-permute-start.3
  3.0 2.0 %slice.6 = bf16[2,1440,128]{2,1,0:T(8,128)(2,1)} slice(bf16[2,1440,256]{2,1,0:T(8,128)(2,1)} %refs_1_.3), slice={[0:2], [0:1440], [0:128]} | slice | bytes 1474560 | tf_op jit(solution)/shard_map/slice | solution.py:324
  5.1 1.5 %collective-permute-start.1 = (bf16[2,1440,128]{2,1,0:T(8,128)(2,1)}, bf16[2,1440,128]{2,1,0:T(8,128)(2,1)}, u32[]{:S(2)}, u32[]{:S(2)}) collective-permute-start(bf16[2,1440,128]{2,1,0:T(8,128)(2,1)} %slice.6), channel_id=1, source_target_pairs={{1,2},{2,1},{5,6},{6,5},{9,10},{10,9},{13,14},{14,13},{17,18},{18,... | collective-permute-start | bytes 2211848 | tf_op jit(solution)/shard_map/ppermute | solution.py:325
  6.6 0.0 copy-done.1
  6.6 0.9 slice.7
  7.5 1.5 %collective-permute-start = (bf16[2,1440,128]{2,1,0:T(8,128)(2,1)}, bf16[2,1440,128]{2,1,0:T(8,128)(2,1)}, u32[]{:S(2)}, u32[]{:S(2)}) collective-permute-start(bf16[2,1440,128]{2,1,0:T(8,128)(2,1)} %slice.7), channel_id=1, source_target_pairs={{1,2},{2,1},{5,6},{6,5},{9,10},{10,9},{13,14},{14,13},{17,18},{18,... | collective-permute-start | bytes 2211848 | tf_op jit(solution)/shard_map/ppermute | solution.py:327
  9.1 0.1 constant_dynamic-slice_fusion.1
  9.1 0.0 copy-start.2
  9.2 0.2 copy.12
  9.3 0.2 copy.13
  9.5 0.1 constant_dynamic-slice_fusion
  9.6 0.2 copy.14
  9.8 0.1 pad.23.clone
  9.9 0.7 maximum_maximum_fusion.table.refs_0_
  10.6 17.5 %backward.1 = (f32[2,1440,256]{2,1,0:T(8,128)}, bf16[2,1440,256]{2,1,0:T(8,128)(2,1)}, bf16[2,1440,256]{2,1,0:T(8,128)(2,1)}) custom-call(f32[2,9,10]{2,1,0:T(8,128)} %maximum_maximum_fusion.table.refs_0_, bf16[2,1440,256]{2,1,0:T(8,128)(2,1)} %refs_5_.3, bf16[9,256,256]{2,1,0:T(8,128)(2,1)} %refs_6_.3), custom_call_target="tpu_custom_call" | custom-call | tf_op jit(solution)/shard_map/backward/pallas_call | solution.py:228
  28.0 0.0 collective-permute-done.1.refs_2_
  28.0 0.0 collective-permute-done.2.refs_3_
  28.0 0.0 collective-permute-done.3.refs_4_
  28.1 0.0 copy-done.2
  28.1 0.0 copy-done.3
  28.1 10.7 %forward.2 = (f32[2,1440,256]{2,1,0:T(8,128)S(1)}, f32[9,128,128]{2,1,0:T(8,128)S(1)}, bf16[9,128,128]{2,1,0:T(8,128)(2,1)S(1)}) custom-call(f32[2,9,10]{2,1,0:T(8,128)S(1)} %copy-done.5, bf16[2,1440,256]{2,1,0:T(8,128)(2,1)S(1)} %copy-done.1, bf16[2,1440,128]{2,1,0:T(8,128)(2,1)} %collective-permute-done.1.refs_2_, ...), custom_call_target="tpu_custom_call" | custom-call | tf_op jit(solution)/shard_map/forward/pallas_call | solution.py:103
  38.8 1.9 %collective-permute-start.5 = (bf16[2,1440,256]{2,1,0:T(8,128)(2,1)}, bf16[2,1440,256]{2,1,0:T(8,128)(2,1)}, u32[]{:S(2)}, u32[]{:S(2)}) collective-permute-start(bf16[2,1440,256]{2,1,0:T(8,128)(2,1)} %get-tuple-element.46), channel_id=1, source_target_pairs={{3,4},{4,3},{7,8},{8,7},{11,12},{12,11},{19,20},{20,19},{23,24},{2... | collective-permute-start | bytes 4423688 | tf_op jit(solution)/shard_map/ppermute | solution.py:341
  40.6 4.0 %collective-permute-start.6 = (bf16[2,1440,256]{2,1,0:T(8,128)(2,1)}, bf16[2,1440,256]{2,1,0:T(8,128)(2,1)}, u32[]{:S(2)}, u32[]{:S(2)}) collective-permute-start(bf16[2,1440,256]{2,1,0:T(8,128)(2,1)} %get-tuple-element.48), channel_id=1, source_target_pairs={{0,1},{1,0},{2,3},{3,2},{4,5},{5,4},{6,7},{7,6},{8,9},{9,8},{10,11... | collective-permute-start | bytes 4423688 | tf_op jit(solution)/shard_map/ppermute | solution.py:343
  44.7 0.0 collective-permute-done.refs_2_
  44.7 11.5 %forward.3 = (bf16[2,1440,256]{2,1,0:T(8,128)(2,1)}, f32[18,128,128]{2,1,0:T(8,128)S(1)}, bf16[18,128,128]{2,1,0:T(8,128)(2,1)}) custom-call(f32[2,9,10]{2,1,0:T(8,128)S(1)} %copy-done.5, bf16[2,1440,256]{2,1,0:T(8,128)(2,1)S(1)} %copy-done.1, bf16[2,1440,128]{2,1,0:T(8,128)(2,1)} %collective-permute-done.refs_2_, ...), custom_call_target="tpu_custom_call" | custom-call | tf_op jit(solution)/shard_map/forward/pallas_call | solution.py:103
  56.2 1.0 copy-done.4
  57.2 0.0 collective-permute-start.4
  57.2 2.2 %collective-permute-done.4 = bf16[2304,128]{1,0:T(8,128)(2,1)S(1)} collective-permute-done((bf16[2304,128]{1,0:T(8,128)(2,1)}, bf16[2304,128]{1,0:T(8,128)(2,1)S(1)}, u32[]{:S(2)}, u32[]{:S(2)}) %collective-permute-start.4) | collective-permute-done | bytes 589856 | tf_op jit(solution)/shard_map/ppermute | solution.py:258
  59.4 1.4 %bitcast_add_fusion = f32[2304,128]{1,0:T(8,128)S(1)} fusion(f32[18,128,128]{2,1,0:T(8,128)} %copy-done.4, bf16[2304,128]{1,0:T(8,128)(2,1)S(1)} %collective-permute-done.4), kind=kLoop, calls=%fused_computation.2 | loop fusion | flops 589824 | bytes 2949120 | tf_op jit(solution)/shard_map/add | solution.py:266
  60.8 0.0 collective-permute-done.5
  60.8 0.0 collective-permute-done.6
  60.8 0.1 fusion
  60.9 1.8 %collective-permute-start.10 = (bf16[576,128]{1,0:T(8,128)(2,1)S(1)}, bf16[576,128]{1,0:T(8,128)(2,1)S(1)}, u32[]{:S(2)}, u32[]{:S(2)}) collective-permute-start(bf16[576,128]{1,0:T(8,128)(2,1)S(1)} %dynamic-slice_convert_fusion), channel_id=1, source_target_pairs={{0,2},{1,3},{2,0},{3,1},{4,6},{5,7},{6,4},{7,5},{8,10},{9,11},{10,... | collective-permute-start | bytes 442376 | tf_op jit(solution)/shard_map/ppermute | solution.py:258
  62.7 1.0 collective-permute-start.13
  63.7 1.3 %collective-permute-start.7 = (bf16[576,128]{1,0:T(8,128)(2,1)S(1)}, bf16[576,128]{1,0:T(8,128)(2,1)S(1)}, u32[]{:S(2)}, u32[]{:S(2)}) collective-permute-start(bf16[576,128]{1,0:T(8,128)(2,1)S(1)} %dynamic-slice_convert_fusion.1), channel_id=1, source_target_pairs={{0,4},{1,5},{2,6},{3,7},{4,0},{5,1},{6,2},{7,3},{8,12},{9,13},{10,... | collective-permute-start | bytes 442376 | tf_op jit(solution)/shard_map/ppermute | solution.py:258
  65.0 2.3 %collective-permute-done.10 = bf16[576,128]{1,0:T(8,128)(2,1)S(1)} collective-permute-done((bf16[576,128]{1,0:T(8,128)(2,1)S(1)}, bf16[576,128]{1,0:T(8,128)(2,1)S(1)}, u32[]{:S(2)}, u32[]{:S(2)}) %collective-permute-start.10) | collective-permute-done | bytes 147488 | tf_op jit(solution)/shard_map/ppermute | solution.py:258
  67.4 1.6 %collective-permute-start.11 = (bf16[288,128]{1,0:T(8,128)(2,1)S(1)}, bf16[288,128]{1,0:T(8,128)(2,1)S(1)}, u32[]{:S(2)}, u32[]{:S(2)}) collective-permute-start(bf16[288,128]{1,0:T(8,128)(2,1)S(1)} %dynamic-slice_convert_fusion.2), channel_id=1, source_target_pairs={{0,4},{1,5},{2,6},{3,7},{4,0},{5,1},{6,2},{7,3},{8,12},{9,13},{10,... | collective-permute-start | bytes 221192 | tf_op jit(solution)/shard_map/ppermute | solution.py:258
  69.0 0.9 collective-permute-done.7
  69.9 1.3 %collective-permute-start.8 = (bf16[288,128]{1,0:T(8,128)(2,1)S(1)}, bf16[288,128]{1,0:T(8,128)(2,1)S(1)}, u32[]{:S(2)}, u32[]{:S(2)}) collective-permute-start(bf16[288,128]{1,0:T(8,128)(2,1)S(1)} %dynamic-slice_convert_fusion.3), channel_id=1, source_target_pairs={{0,8},{1,9},{2,10},{3,11},{4,12},{5,13},{6,14},{7,15},{8,0},{9,1},... | collective-permute-start | bytes 221192 | tf_op jit(solution)/shard_map/ppermute | solution.py:258
  71.2 0.9 collective-permute-done.11
  72.1 2.2 %collective-permute-start.12 = (bf16[288,128]{1,0:T(8,128)(2,1)S(1)}, bf16[288,128]{1,0:T(8,128)(2,1)S(1)}, u32[]{:S(2)}, u32[]{:S(2)}) collective-permute-start(bf16[288,128]{1,0:T(8,128)(2,1)S(1)} %add_convert_fusion.2), channel_id=1, source_target_pairs={{0,8},{1,9},{2,10},{3,11},{4,12},{5,13},{6,14},{7,15},{8,0},{9,1},... | collective-permute-start | bytes 221192 | tf_op jit(solution)/shard_map/ppermute | solution.py:258
  74.3 4.8 %collective-permute-done.8 = bf16[288,128]{1,0:T(8,128)(2,1)S(1)} collective-permute-done((bf16[288,128]{1,0:T(8,128)(2,1)S(1)}, bf16[288,128]{1,0:T(8,128)(2,1)S(1)}, u32[]{:S(2)}, u32[]{:S(2)}) %collective-permute-start.8) | collective-permute-done | bytes 73760 | tf_op jit(solution)/shard_map/ppermute | solution.py:258
  79.2 0.6 collective-permute-start.9
  79.8 0.5 collective-permute-done.12
  80.3 5.4 %collective-permute-done.9 = bf16[288,128]{1,0:T(8,128)(2,1)S(1)} collective-permute-done((bf16[288,128]{1,0:T(8,128)(2,1)S(1)}, bf16[288,128]{1,0:T(8,128)(2,1)S(1)}, u32[]{:S(2)}, u32[]{:S(2)}) %collective-permute-start.9) | collective-permute-done | bytes 73760 | tf_op jit(solution)/shard_map/ppermute | solution.py:258
  85.7 0.0 collective-permute-done.13
  85.7 2.0 %collective-permute-start.15 = (bf16[288,128]{1,0:T(8,128)(2,1)S(1)}, bf16[288,128]{1,0:T(8,128)(2,1)S(1)}, u32[]{:S(2)}, u32[]{:S(2)}) collective-permute-start(bf16[288,128]{1,0:T(8,128)(2,1)S(1)} %add_convert_fusion.1), channel_id=1, source_target_pairs={{0,4},{1,5},{2,6},{3,7},{4,0},{5,1},{6,2},{7,3},{8,12},{9,13},{10,... | collective-permute-start | bytes 221192 | tf_op jit(solution)/shard_map/ppermute | solution.py:258
  87.7 1.3 %collective-permute-start.14 = (bf16[288,128]{1,0:T(8,128)(2,1)S(1)}, bf16[288,128]{1,0:T(8,128)(2,1)S(1)}, u32[]{:S(2)}, u32[]{:S(2)}) collective-permute-start(bf16[288,128]{1,0:T(8,128)(2,1)S(1)} %add_convert_fusion.3), channel_id=1, source_target_pairs={{0,8},{1,9},{2,10},{3,11},{4,12},{5,13},{6,14},{7,15},{8,0},{9,1},... | collective-permute-start | bytes 221192 | tf_op jit(solution)/shard_map/ppermute | solution.py:258
  89.0 3.7 %add_convert_fusion = bf16[2,1440,256]{2,1,0:T(8,128)(2,1)} fusion(bf16[2,1440,256]{2,1,0:T(8,128)(2,1)} %collective-permute-done.6, f32[2,1440,256]{2,1,0:T(8,128)S(1)} %copy-done.6, bf16[2,1440,256]{2,1,0:T(8,128)(2,1)S(1)} %collective-permute-done.13, bf16[2,1440,256]{2,1,0:T(8,128)(2,1)} %collective-permute-done.5), kind=kLoop, calls=%fused_computation | loop fusion | flops 5160960 | bytes 8847360 | tf_op jit(solution)/shard_map/convert_element_type | solution.py:363
  92.7 0.0 collective-permute-done.15
  92.8 0.5 collective-permute-done.14
  93.3 0.5 collective-permute-start.16
  93.8 0.7 collective-permute-start.18
  94.6 4.0 %collective-permute-done.16 = bf16[576,128]{1,0:T(8,128)(2,1)S(1)} collective-permute-done((bf16[576,128]{1,0:T(8,128)(2,1)S(1)}, bf16[576,128]{1,0:T(8,128)(2,1)S(1)}, u32[]{:S(2)}, u32[]{:S(2)}) %collective-permute-start.16) | collective-permute-done | bytes 147488 | tf_op jit(solution)/shard_map/ppermute | solution.py:258
  98.5 0.1 maximum_select_fusion
  98.6 0.1 collective-permute-start.17
  98.7 0.3 collective-permute-done.18
  99.0 0.1 maximum_select_fusion.1
  99.1 0.3 collective-permute-start.19
  99.4 0.9 collective-permute-done.17
  100.3 0.4 collective-permute-done.19
  100.8 1.6 %convert_multiply_fusion = f32[9,256,256]{2,1,0:T(8,128)} fusion(bf16[9,128,128]{2,1,0:T(8,128)(2,1)S(1)} %bitcast.11, bf16[9,128,128]{2,1,0:T(8,128)(2,1)S(1)} %bitcast.10, bf16[9,128,128]{2,1,0:T(8,128)(2,1)S(1)} %bitcast.9, bf16[9,128,128]{2,1,0:T(8,128)(2,1)S(1)} %bitcast.8), kind=kLoop, calls=%fused_computation.1 | loop fusion | flops 5308416 | bytes 3538944 | tf_op jit(solution)/shard_map/mul | solution.py:369
  (28 shorter events, 0.4 us)
Async XLA Ops:
  0.6 8.9 %copy-start = (f32[32,9,3]{0,2,1:T(4,128)S(1)}, f32[32,9,3]{0,2,1:T(4,128)}, u32[]{:S(2)}) copy-start(f32[32,9,3]{0,2,1:T(4,128)} %param.11) | copy-start | bytes 10372
  0.6 6.0 %copy-start.1 = (bf16[2,1440,256]{2,1,0:T(8,128)(2,1)S(1)}, bf16[2,1440,256]{2,1,0:T(8,128)(2,1)}, u32[]{:S(2)}) copy-start(bf16[2,1440,256]{2,1,0:T(8,128)(2,1)} %refs_1_.3) | copy-start | bytes 4423684
  0.7 8.4 %copy-start.7 = (s32[32,9,3]{0,2,1:T(4,128)S(1)}, s32[32,9,3]{0,2,1:T(4,128)}, u32[]{:S(2)}) copy-start(s32[32,9,3]{0,2,1:T(4,128)} %param.10) | copy-start | bytes 10372
  0.7 8.4 %copy-start.8 = (s32[32,9,3]{0,2,1:T(4,128)S(1)}, s32[32,9,3]{0,2,1:T(4,128)}, u32[]{:S(2)}) copy-start(s32[32,9,3]{0,2,1:T(4,128)} %param.9) | copy-start | bytes 10372
  0.7 27.4 %collective-permute-start.2 = (bf16[2,1440,256]{2,1,0:T(8,128)(2,1)}, bf16[2,1440,256]{2,1,0:T(8,128)(2,1)}, u32[]{:S(2)}, u32[]{:S(2)}) collective-permute-start(bf16[2,1440,256]{2,1,0:T(8,128)(2,1)} %refs_1_.3), channel_id=1, source_target_pairs={{3,4},{4,3},{7,8},{8,7},{11,12},{12,11},{19,20},{20,19},{23,24},{2... | collective-permute-start | bytes 4423688 | tf_op jit(solution)/shard_map/ppermute | solution.py:323
  2.6 25.5 %collective-permute-start.3 = (bf16[2,1440,256]{2,1,0:T(8,128)(2,1)}, bf16[2,1440,256]{2,1,0:T(8,128)(2,1)}, u32[]{:S(2)}, u32[]{:S(2)}) collective-permute-start(bf16[2,1440,256]{2,1,0:T(8,128)(2,1)} %refs_1_.3), channel_id=1, source_target_pairs={{0,1},{1,0},{2,3},{3,2},{4,5},{5,4},{6,7},{7,6},{8,9},{9,8},{10,11... | collective-permute-start | bytes 4423688 | tf_op jit(solution)/shard_map/ppermute | solution.py:328
  5.1 23.0 %collective-permute-start.1 = (bf16[2,1440,128]{2,1,0:T(8,128)(2,1)}, bf16[2,1440,128]{2,1,0:T(8,128)(2,1)}, u32[]{:S(2)}, u32[]{:S(2)}) collective-permute-start(bf16[2,1440,128]{2,1,0:T(8,128)(2,1)} %slice.6), channel_id=1, source_target_pairs={{1,2},{2,1},{5,6},{6,5},{9,10},{10,9},{13,14},{14,13},{17,18},{18,... | collective-permute-start | bytes 2211848 | tf_op jit(solution)/shard_map/ppermute | solution.py:325
  7.5 37.1 %collective-permute-start = (bf16[2,1440,128]{2,1,0:T(8,128)(2,1)}, bf16[2,1440,128]{2,1,0:T(8,128)(2,1)}, u32[]{:S(2)}, u32[]{:S(2)}) collective-permute-start(bf16[2,1440,128]{2,1,0:T(8,128)(2,1)} %slice.7), channel_id=1, source_target_pairs={{1,2},{2,1},{5,6},{6,5},{9,10},{10,9},{13,14},{14,13},{17,18},{18,... | collective-permute-start | bytes 2211848 | tf_op jit(solution)/shard_map/ppermute | solution.py:327
  9.1 18.9 %copy-start.2 = (bf16[2,1440,256]{2,1,0:T(8,128)(2,1)S(1)}, bf16[2,1440,256]{2,1,0:T(8,128)(2,1)}, u32[]{:S(2)}) copy-start(bf16[2,1440,256]{2,1,0:T(8,128)(2,1)} %refs_5_.3) | copy-start | bytes 4423684
  9.8 18.3 %copy-start.3 = (bf16[9,256,256]{2,1,0:T(8,128)(2,1)S(1)}, bf16[9,256,256]{2,1,0:T(8,128)(2,1)}, u32[]{:S(2)}) copy-start(bf16[9,256,256]{2,1,0:T(8,128)(2,1)} %refs_6_.3) | copy-start | bytes 3538948
  10.6 17.5 %copy-start.5 = (f32[2,9,10]{2,1,0:T(8,128)S(1)}, f32[2,9,10]{2,1,0:T(8,128)}, u32[]{:S(2)}) copy-start(f32[2,9,10]{2,1,0:T(8,128)} %maximum_maximum_fusion.table.refs_0_) | copy-start | bytes 2164
  38.8 22.0 %collective-permute-start.5 = (bf16[2,1440,256]{2,1,0:T(8,128)(2,1)}, bf16[2,1440,256]{2,1,0:T(8,128)(2,1)}, u32[]{:S(2)}, u32[]{:S(2)}) collective-permute-start(bf16[2,1440,256]{2,1,0:T(8,128)(2,1)} %get-tuple-element.46), channel_id=1, source_target_pairs={{3,4},{4,3},{7,8},{8,7},{11,12},{12,11},{19,20},{20,19},{23,24},{2... | collective-permute-start | bytes 4423688 | tf_op jit(solution)/shard_map/ppermute | solution.py:341
  40.6 20.2 %collective-permute-start.6 = (bf16[2,1440,256]{2,1,0:T(8,128)(2,1)}, bf16[2,1440,256]{2,1,0:T(8,128)(2,1)}, u32[]{:S(2)}, u32[]{:S(2)}) collective-permute-start(bf16[2,1440,256]{2,1,0:T(8,128)(2,1)} %get-tuple-element.48), channel_id=1, source_target_pairs={{0,1},{1,0},{2,3},{3,2},{4,5},{5,4},{6,7},{7,6},{8,9},{9,8},{10,11... | collective-permute-start | bytes 4423688 | tf_op jit(solution)/shard_map/ppermute | solution.py:343
  56.2 1.0 copy-start.4
  57.2 2.2 %collective-permute-start.4 = (bf16[2304,128]{1,0:T(8,128)(2,1)}, bf16[2304,128]{1,0:T(8,128)(2,1)S(1)}, u32[]{:S(2)}, u32[]{:S(2)}) collective-permute-start(bf16[2304,128]{1,0:T(8,128)(2,1)} %bitcast.1), channel_id=1, source_target_pairs={{0,1},{1,0},{2,3},{3,2},{4,5},{5,4},{6,7},{7,6},{8,9},{9,8},{10,11... | collective-permute-start | bytes 1769480 | tf_op jit(solution)/shard_map/ppermute | solution.py:258
  60.9 6.4 %collective-permute-start.10 = (bf16[576,128]{1,0:T(8,128)(2,1)S(1)}, bf16[576,128]{1,0:T(8,128)(2,1)S(1)}, u32[]{:S(2)}, u32[]{:S(2)}) collective-permute-start(bf16[576,128]{1,0:T(8,128)(2,1)S(1)} %dynamic-slice_convert_fusion), channel_id=1, source_target_pairs={{0,2},{1,3},{2,0},{3,1},{4,6},{5,7},{6,4},{7,5},{8,10},{9,11},{10,... | collective-permute-start | bytes 442376 | tf_op jit(solution)/shard_map/ppermute | solution.py:258
  62.7 23.0 %collective-permute-start.13 = (bf16[2,1440,256]{2,1,0:T(8,128)(2,1)}, bf16[2,1440,256]{2,1,0:T(8,128)(2,1)S(1)}, u32[]{:S(2)}, u32[]{:S(2)}) collective-permute-start(bf16[2,1440,256]{2,1,0:T(8,128)(2,1)} %get-tuple-element.46), channel_id=1, source_target_pairs={{1,2},{2,1},{5,6},{6,5},{9,10},{10,9},{13,14},{14,13},{17,18},{18,... | collective-permute-start | bytes 4423688 | tf_op jit(solution)/shard_map/ppermute | solution.py:342
  63.7 25.3 %copy-start.6 = (f32[2,1440,256]{2,1,0:T(8,128)S(1)}, f32[2,1440,256]{2,1,0:T(8,128)}, u32[]{:S(2)}) copy-start(f32[2,1440,256]{2,1,0:T(8,128)} %get-tuple-element.52) | copy-start | bytes 8847364
  63.7 6.1 %collective-permute-start.7 = (bf16[576,128]{1,0:T(8,128)(2,1)S(1)}, bf16[576,128]{1,0:T(8,128)(2,1)S(1)}, u32[]{:S(2)}, u32[]{:S(2)}) collective-permute-start(bf16[576,128]{1,0:T(8,128)(2,1)S(1)} %dynamic-slice_convert_fusion.1), channel_id=1, source_target_pairs={{0,4},{1,5},{2,6},{3,7},{4,0},{5,1},{6,2},{7,3},{8,12},{9,13},{10,... | collective-permute-start | bytes 442376 | tf_op jit(solution)/shard_map/ppermute | solution.py:258
  67.4 4.7 %collective-permute-start.11 = (bf16[288,128]{1,0:T(8,128)(2,1)S(1)}, bf16[288,128]{1,0:T(8,128)(2,1)S(1)}, u32[]{:S(2)}, u32[]{:S(2)}) collective-permute-start(bf16[288,128]{1,0:T(8,128)(2,1)S(1)} %dynamic-slice_convert_fusion.2), channel_id=1, source_target_pairs={{0,4},{1,5},{2,6},{3,7},{4,0},{5,1},{6,2},{7,3},{8,12},{9,13},{10,... | collective-permute-start | bytes 221192 | tf_op jit(solution)/shard_map/ppermute | solution.py:258
  69.9 9.2 %collective-permute-start.8 = (bf16[288,128]{1,0:T(8,128)(2,1)S(1)}, bf16[288,128]{1,0:T(8,128)(2,1)S(1)}, u32[]{:S(2)}, u32[]{:S(2)}) collective-permute-start(bf16[288,128]{1,0:T(8,128)(2,1)S(1)} %dynamic-slice_convert_fusion.3), channel_id=1, source_target_pairs={{0,8},{1,9},{2,10},{3,11},{4,12},{5,13},{6,14},{7,15},{8,0},{9,1},... | collective-permute-start | bytes 221192 | tf_op jit(solution)/shard_map/ppermute | solution.py:258
  72.1 8.2 %collective-permute-start.12 = (bf16[288,128]{1,0:T(8,128)(2,1)S(1)}, bf16[288,128]{1,0:T(8,128)(2,1)S(1)}, u32[]{:S(2)}, u32[]{:S(2)}) collective-permute-start(bf16[288,128]{1,0:T(8,128)(2,1)S(1)} %add_convert_fusion.2), channel_id=1, source_target_pairs={{0,8},{1,9},{2,10},{3,11},{4,12},{5,13},{6,14},{7,15},{8,0},{9,1},... | collective-permute-start | bytes 221192 | tf_op jit(solution)/shard_map/ppermute | solution.py:258
  79.2 6.5 %collective-permute-start.9 = (bf16[288,128]{1,0:T(8,128)(2,1)S(1)}, bf16[288,128]{1,0:T(8,128)(2,1)S(1)}, u32[]{:S(2)}, u32[]{:S(2)}) collective-permute-start(bf16[288,128]{1,0:T(8,128)(2,1)S(1)} %add_convert_fusion.4), channel_id=1, source_target_pairs={{0,2},{1,3},{2,0},{3,1},{4,6},{5,7},{6,4},{7,5},{8,10},{9,11},{10,... | collective-permute-start | bytes 221192 | tf_op jit(solution)/shard_map/ppermute | solution.py:258
  85.7 7.0 %collective-permute-start.15 = (bf16[288,128]{1,0:T(8,128)(2,1)S(1)}, bf16[288,128]{1,0:T(8,128)(2,1)S(1)}, u32[]{:S(2)}, u32[]{:S(2)}) collective-permute-start(bf16[288,128]{1,0:T(8,128)(2,1)S(1)} %add_convert_fusion.1), channel_id=1, source_target_pairs={{0,4},{1,5},{2,6},{3,7},{4,0},{5,1},{6,2},{7,3},{8,12},{9,13},{10,... | collective-permute-start | bytes 221192 | tf_op jit(solution)/shard_map/ppermute | solution.py:258
  87.7 5.6 %collective-permute-start.14 = (bf16[288,128]{1,0:T(8,128)(2,1)S(1)}, bf16[288,128]{1,0:T(8,128)(2,1)S(1)}, u32[]{:S(2)}, u32[]{:S(2)}) collective-permute-start(bf16[288,128]{1,0:T(8,128)(2,1)S(1)} %add_convert_fusion.3), channel_id=1, source_target_pairs={{0,8},{1,9},{2,10},{3,11},{4,12},{5,13},{6,14},{7,15},{8,0},{9,1},... | collective-permute-start | bytes 221192 | tf_op jit(solution)/shard_map/ppermute | solution.py:258
  93.3 5.2 %collective-permute-start.16 = (bf16[576,128]{1,0:T(8,128)(2,1)S(1)}, bf16[576,128]{1,0:T(8,128)(2,1)S(1)}, u32[]{:S(2)}, u32[]{:S(2)}) collective-permute-start(bf16[576,128]{1,0:T(8,128)(2,1)S(1)} %maximum_select_fusion.2), channel_id=1, source_target_pairs={{0,4},{1,5},{2,6},{3,7},{4,0},{5,1},{6,2},{7,3},{8,12},{9,13},{10,... | collective-permute-start | bytes 442376 | tf_op jit(solution)/shard_map/ppermute | solution.py:258
  93.8 5.1 %collective-permute-start.18 = (bf16[576,128]{1,0:T(8,128)(2,1)S(1)}, bf16[576,128]{1,0:T(8,128)(2,1)S(1)}, u32[]{:S(2)}, u32[]{:S(2)}) collective-permute-start(bf16[576,128]{1,0:T(8,128)(2,1)S(1)} %maximum_select_fusion.3), channel_id=1, source_target_pairs={{0,2},{1,3},{2,0},{3,1},{4,6},{5,7},{6,4},{7,5},{8,10},{9,11},{10,... | collective-permute-start | bytes 442376 | tf_op jit(solution)/shard_map/ppermute | solution.py:258
  98.6 1.6 %collective-permute-start.17 = (bf16[1152,128]{1,0:T(8,128)(2,1)S(1)}, bf16[1152,128]{1,0:T(8,128)(2,1)S(1)}, u32[]{:S(2)}, u32[]{:S(2)}) collective-permute-start(bf16[1152,128]{1,0:T(8,128)(2,1)S(1)} %maximum_select_fusion), channel_id=1, source_target_pairs={{0,1},{1,0},{2,3},{3,2},{4,5},{5,4},{6,7},{7,6},{8,9},{9,8},{10,11... | collective-permute-start | bytes 884744 | tf_op jit(solution)/shard_map/ppermute | solution.py:258
  99.1 1.6 %collective-permute-start.19 = (bf16[1152,128]{1,0:T(8,128)(2,1)S(1)}, bf16[1152,128]{1,0:T(8,128)(2,1)S(1)}, u32[]{:S(2)}, u32[]{:S(2)}) collective-permute-start(bf16[1152,128]{1,0:T(8,128)(2,1)S(1)} %maximum_select_fusion.1), channel_id=1, source_target_pairs={{0,1},{1,0},{2,3},{3,2},{4,5},{5,4},{6,7},{7,6},{8,9},{9,8},{10,11... | collective-permute-start | bytes 884744 | tf_op jit(solution)/shard_map/ppermute | solution.py:258

commit v5 on v4

--- a/solution.py
+++ b/solution.py
@@ -348,8 +348,11 @@
     def between(step, values):
         nonlocal grad
         for j in range(2):
-            if step == WAITS[j]:
+            if step == WAITS[j] and j == 0:
                 values, got[j] = lax.optimization_barrier((values, got[j]))
+            elif step == WAITS[j]:
+                values = list(values)
+                values[1], got[j] = lax.optimization_barrier((values[1], got[j]))
         if step == WAITS[0]:
             values, got[2] = lax.optimization_barrier((values, got[2]))
         if step == ADDED:

time: 103 us -> 103 us (level)
  starting transfers between devices: 26 us -> 22.8 us
  waiting for transfers between devices: 23 us -> 26 us
    ppermute x13, starting transfers between devices: 13.7 us -> 10.5 us  [swap(): return lax.ppermute(value, 'lat', [(i, i ^ bit) for i in range(size)])]
    ppermute x13, waiting for transfers between devices: 23 us -> 25.9 us  [swap(): return lax.ppermute(value, 'lat', [(i, i ^ bit) for i in range(size)])]
  transfers between devices with their start and end apart: 20 -> 20, of which waited for: 12 -> 10; matrix products, arithmetic and copies ran while one was open for 10% -> 10% of each run, Pallas kernels for 39% -> 39%
where the time goes in v5:
time: 103 us
  Pallas kernels  40.1 us (39%)
  waiting for transfers between devices  26 us (25%)
  starting transfers between devices  22.8 us (22%)
  other arithmetic  7.99 us (8%)
  local copies, waits for them, and re-layouts  4.9 us (5%)
    ppermute x13, waiting for transfers between devices, swap(): return lax.ppermute(value, 'lat', [(i, i ^ bit) for i in range(size)])  25.9 us
    pallas_call x2, Pallas kernels, forward(): pl.pallas_call(lambda *refs: fwd_kernel(last, *refs), grid=(1,), in_specs...  22.1 us
    pallas_call x1, Pallas kernels, backward(): pl.pallas_call(bwd_kernel, in_specs=[smem] + [pl.BlockSpec(memory_space=p...  18 us
    ppermute x13, starting transfers between devices, swap(): return lax.ppermute(value, 'lat', [(i, i ^ bit) for i in range(size)])  10.5 us
    ppermute x1, starting transfers between devices, per_device(): got_fast = lax.ppermute(edge_fast, 'lat', fast_pairs)  3.92 us
    convert_element_type x1, other arithmetic, between(): grad = grad.astype(jnp.bfloat16)  3.75 us
  transfers between devices with their start and end apart: 20, of which 10 were waited for; matrix products, arithmetic and copies ran while one was open for 10% of the time, Pallas kernels for 39%

profile of v5, /device:TPU:0, one launch (start us, length us, event | category | flops | bytes accessed | tf_op | source)
XLA Modules:
  0.0 102.6 jit_solution(4198616378674266090)
XLA Ops:
  0.6 0.0 copy-start
  0.6 0.0 copy-start.1
  0.7 0.0 copy-start.7
  0.7 0.0 copy-start.8
  0.7 1.9 %collective-permute-start.2 = (bf16[2,1440,256]{2,1,0:T(8,128)(2,1)}, bf16[2,1440,256]{2,1,0:T(8,128)(2,1)}, u32[]{:S(2)}, u32[]{:S(2)}) collective-permute-start(bf16[2,1440,256]{2,1,0:T(8,128)(2,1)} %refs_1_.3), channel_id=1, source_target_pairs={{3,4},{4,3},{7,8},{8,7},{11,12},{12,11},{19,20},{20,19},{23,24},{2... | collective-permute-start | bytes 4423688 | tf_op jit(solution)/shard_map/ppermute | solution.py:323
  2.6 0.5 collective-permute-start.3
  3.0 2.0 %slice.6 = bf16[2,1440,128]{2,1,0:T(8,128)(2,1)} slice(bf16[2,1440,256]{2,1,0:T(8,128)(2,1)} %refs_1_.3), slice={[0:2], [0:1440], [0:128]} | slice | bytes 1474560 | tf_op jit(solution)/shard_map/slice | solution.py:324
  5.1 1.5 %collective-permute-start.1 = (bf16[2,1440,128]{2,1,0:T(8,128)(2,1)}, bf16[2,1440,128]{2,1,0:T(8,128)(2,1)}, u32[]{:S(2)}, u32[]{:S(2)}) collective-permute-start(bf16[2,1440,128]{2,1,0:T(8,128)(2,1)} %slice.6), channel_id=1, source_target_pairs={{1,2},{2,1},{5,6},{6,5},{9,10},{10,9},{13,14},{14,13},{17,18},{18,... | collective-permute-start | bytes 2211848 | tf_op jit(solution)/shard_map/ppermute | solution.py:325
  6.6 0.9 slice.7
  7.5 1.5 %collective-permute-start = (bf16[2,1440,128]{2,1,0:T(8,128)(2,1)}, bf16[2,1440,128]{2,1,0:T(8,128)(2,1)}, u32[]{:S(2)}, u32[]{:S(2)}) collective-permute-start(bf16[2,1440,128]{2,1,0:T(8,128)(2,1)} %slice.7), channel_id=1, source_target_pairs={{1,2},{2,1},{5,6},{6,5},{9,10},{10,9},{13,14},{14,13},{17,18},{18,... | collective-permute-start | bytes 2211848 | tf_op jit(solution)/shard_map/ppermute | solution.py:327
  9.1 0.1 constant_dynamic-slice_fusion.1
  9.1 0.0 copy-start.2
  9.2 0.2 copy.12
  9.3 0.2 copy.13
  9.5 0.1 constant_dynamic-slice_fusion
  9.6 0.2 copy.14
  9.8 0.1 pad.23.clone
  9.9 0.7 maximum_maximum_fusion.table.refs_0_
  10.6 18.0 %backward.1 = (f32[2,1440,256]{2,1,0:T(8,128)}, bf16[2,1440,256]{2,1,0:T(8,128)(2,1)}, bf16[2,1440,256]{2,1,0:T(8,128)(2,1)}) custom-call(f32[2,9,10]{2,1,0:T(8,128)} %maximum_maximum_fusion.table.refs_0_, bf16[2,1440,256]{2,1,0:T(8,128)(2,1)} %refs_5_.3, bf16[9,256,256]{2,1,0:T(8,128)(2,1)} %refs_6_.3), custom_call_target="tpu_custom_call" | custom-call | tf_op jit(solution)/shard_map/backward/pallas_call | solution.py:228
  28.6 0.0 collective-permute-done.1.refs_2_
  28.6 0.0 collective-permute-done.2.refs_3_
  28.6 0.0 collective-permute-done.3.refs_4_
  28.6 10.6 %forward.2 = (f32[2,1440,256]{2,1,0:T(8,128)S(1)}, f32[9,128,128]{2,1,0:T(8,128)S(1)}, bf16[9,128,128]{2,1,0:T(8,128)(2,1)S(1)}) custom-call(f32[2,9,10]{2,1,0:T(8,128)S(1)} %copy-done.5, bf16[2,1440,256]{2,1,0:T(8,128)(2,1)S(1)} %copy-done.1, bf16[2,1440,128]{2,1,0:T(8,128)(2,1)} %collective-permute-done.1.refs_2_, ...), custom_call_target="tpu_custom_call" | custom-call | tf_op jit(solution)/shard_map/forward/pallas_call | solution.py:103
  39.3 1.9 %collective-permute-start.5 = (bf16[2,1440,256]{2,1,0:T(8,128)(2,1)}, bf16[2,1440,256]{2,1,0:T(8,128)(2,1)}, u32[]{:S(2)}, u32[]{:S(2)}) collective-permute-start(bf16[2,1440,256]{2,1,0:T(8,128)(2,1)} %get-tuple-element.45), channel_id=1, source_target_pairs={{3,4},{4,3},{7,8},{8,7},{11,12},{12,11},{19,20},{20,19},{23,24},{2... | collective-permute-start | bytes 4423688 | tf_op jit(solution)/shard_map/ppermute | solution.py:341
  41.1 3.9 %collective-permute-start.6 = (bf16[2,1440,256]{2,1,0:T(8,128)(2,1)}, bf16[2,1440,256]{2,1,0:T(8,128)(2,1)}, u32[]{:S(2)}, u32[]{:S(2)}) collective-permute-start(bf16[2,1440,256]{2,1,0:T(8,128)(2,1)} %get-tuple-element.47), channel_id=1, source_target_pairs={{0,1},{1,0},{2,3},{3,2},{4,5},{5,4},{6,7},{7,6},{8,9},{9,8},{10,11... | collective-permute-start | bytes 4423688 | tf_op jit(solution)/shard_map/ppermute | solution.py:343
  45.1 0.0 collective-permute-done.refs_2_
  45.1 11.5 %forward.3 = (bf16[2,1440,256]{2,1,0:T(8,128)(2,1)}, f32[18,128,128]{2,1,0:T(8,128)S(1)}, bf16[18,128,128]{2,1,0:T(8,128)(2,1)}) custom-call(f32[2,9,10]{2,1,0:T(8,128)S(1)} %copy-done.5, bf16[2,1440,256]{2,1,0:T(8,128)(2,1)S(1)} %copy-done.1, bf16[2,1440,128]{2,1,0:T(8,128)(2,1)} %collective-permute-done.refs_2_, ...), custom_call_target="tpu_custom_call" | custom-call | tf_op jit(solution)/shard_map/forward/pallas_call | solution.py:103
  56.5 1.0 copy-done.4
  57.5 0.0 collective-permute-start.4
  57.5 2.2 %collective-permute-done.4 = bf16[2304,128]{1,0:T(8,128)(2,1)S(1)} collective-permute-done((bf16[2304,128]{1,0:T(8,128)(2,1)}, bf16[2304,128]{1,0:T(8,128)(2,1)S(1)}, u32[]{:S(2)}, u32[]{:S(2)}) %collective-permute-start.4) | collective-permute-done | bytes 589856 | tf_op jit(solution)/shard_map/ppermute | solution.py:258
  59.7 1.4 %bitcast_add_fusion = f32[2304,128]{1,0:T(8,128)S(1)} fusion(f32[18,128,128]{2,1,0:T(8,128)} %copy-done.4, bf16[2304,128]{1,0:T(8,128)(2,1)S(1)} %collective-permute-done.4), kind=kLoop, calls=%fused_computation.2 | loop fusion | flops 589824 | bytes 2949120 | tf_op jit(solution)/shard_map/add | solution.py:266
  61.1 0.0 collective-permute-done.5
  61.2 0.0 collective-permute-done.6
  61.2 0.1 fusion
  61.3 0.9 collective-permute-start.11
  62.2 1.0 collective-permute-start.14
  63.2 1.6 %collective-permute-start.7 = (bf16[576,128]{1,0:T(8,128)(2,1)S(1)}, bf16[576,128]{1,0:T(8,128)(2,1)S(1)}, u32[]{:S(2)}, u32[]{:S(2)}) collective-permute-start(bf16[576,128]{1,0:T(8,128)(2,1)S(1)} %dynamic-slice_convert_fusion.1), channel_id=1, source_target_pairs={{0,4},{1,5},{2,6},{3,7},{4,0},{5,1},{6,2},{7,3},{8,12},{9,13},{10,... | collective-permute-start | bytes 442376 | tf_op jit(solution)/shard_map/ppermute | solution.py:258
  64.8 3.1 %collective-permute-done.11 = bf16[576,128]{1,0:T(8,128)(2,1)S(1)} collective-permute-done((bf16[576,128]{1,0:T(8,128)(2,1)S(1)}, bf16[576,128]{1,0:T(8,128)(2,1)S(1)}, u32[]{:S(2)}, u32[]{:S(2)}) %collective-permute-start.11) | collective-permute-done | bytes 147488 | tf_op jit(solution)/shard_map/ppermute | solution.py:258
  68.0 1.5 %collective-permute-start.12 = (bf16[288,128]{1,0:T(8,128)(2,1)S(1)}, bf16[288,128]{1,0:T(8,128)(2,1)S(1)}, u32[]{:S(2)}, u32[]{:S(2)}) collective-permute-start(bf16[288,128]{1,0:T(8,128)(2,1)S(1)} %dynamic-slice_convert_fusion.2), channel_id=1, source_target_pairs={{0,4},{1,5},{2,6},{3,7},{4,0},{5,1},{6,2},{7,3},{8,12},{9,13},{10,... | collective-permute-start | bytes 221192 | tf_op jit(solution)/shard_map/ppermute | solution.py:258
  69.5 0.0 collective-permute-done.7
  69.5 1.5 %collective-permute-start.8 = (bf16[288,128]{1,0:T(8,128)(2,1)S(1)}, bf16[288,128]{1,0:T(8,128)(2,1)S(1)}, u32[]{:S(2)}, u32[]{:S(2)}) collective-permute-start(bf16[288,128]{1,0:T(8,128)(2,1)S(1)} %dynamic-slice_convert_fusion.3), channel_id=1, source_target_pairs={{0,8},{1,9},{2,10},{3,11},{4,12},{5,13},{6,14},{7,15},{8,0},{9,1},... | collective-permute-start | bytes 221192 | tf_op jit(solution)/shard_map/ppermute | solution.py:258
  71.0 1.5 %collective-permute-done.12 = bf16[288,128]{1,0:T(8,128)(2,1)S(1)} collective-permute-done((bf16[288,128]{1,0:T(8,128)(2,1)S(1)}, bf16[288,128]{1,0:T(8,128)(2,1)S(1)}, u32[]{:S(2)}, u32[]{:S(2)}) %collective-permute-start.12) | collective-permute-done | bytes 73760 | tf_op jit(solution)/shard_map/ppermute | solution.py:258
  72.5 1.5 %collective-permute-start.13 = (bf16[288,128]{1,0:T(8,128)(2,1)S(1)}, bf16[288,128]{1,0:T(8,128)(2,1)S(1)}, u32[]{:S(2)}, u32[]{:S(2)}) collective-permute-start(bf16[288,128]{1,0:T(8,128)(2,1)S(1)} %add_convert_fusion.2), channel_id=1, source_target_pairs={{0,8},{1,9},{2,10},{3,11},{4,12},{5,13},{6,14},{7,15},{8,0},{9,1},... | collective-permute-start | bytes 221192 | tf_op jit(solution)/shard_map/ppermute | solution.py:258
  74.0 4.8 %collective-permute-done.8 = bf16[288,128]{1,0:T(8,128)(2,1)S(1)} collective-permute-done((bf16[288,128]{1,0:T(8,128)(2,1)S(1)}, bf16[288,128]{1,0:T(8,128)(2,1)S(1)}, u32[]{:S(2)}, u32[]{:S(2)}) %collective-permute-start.8) | collective-permute-done | bytes 73760 | tf_op jit(solution)/shard_map/ppermute | solution.py:258
  78.8 0.5 collective-permute-start.9
  79.3 0.8 collective-permute-done.13
  80.1 0.0 collective-permute-done.14
  80.1 0.7 collective-permute-start.15
  80.8 5.7 %collective-permute-done.9 = bf16[288,128]{1,0:T(8,128)(2,1)S(1)} collective-permute-done((bf16[288,128]{1,0:T(8,128)(2,1)S(1)}, bf16[288,128]{1,0:T(8,128)(2,1)S(1)}, u32[]{:S(2)}, u32[]{:S(2)}) %collective-permute-start.9) | collective-permute-done | bytes 73760 | tf_op jit(solution)/shard_map/ppermute | solution.py:258
  86.6 1.3 %collective-permute-start.10 = (bf16[288,128]{1,0:T(8,128)(2,1)S(1)}, bf16[288,128]{1,0:T(8,128)(2,1)S(1)}, u32[]{:S(2)}, u32[]{:S(2)}) collective-permute-start(bf16[288,128]{1,0:T(8,128)(2,1)S(1)} %add_convert_fusion.3), channel_id=1, source_target_pairs={{0,8},{1,9},{2,10},{3,11},{4,12},{5,13},{6,14},{7,15},{8,0},{9,1},... | collective-permute-start | bytes 221192 | tf_op jit(solution)/shard_map/ppermute | solution.py:258
  87.9 3.7 %add_convert_fusion = bf16[2,1440,256]{2,1,0:T(8,128)(2,1)} fusion(bf16[2,1440,256]{2,1,0:T(8,128)(2,1)} %collective-permute-done.6, f32[2,1440,256]{2,1,0:T(8,128)S(1)} %copy-done.6, bf16[2,1440,256]{2,1,0:T(8,128)(2,1)S(1)} %collective-permute-done.14, bf16[2,1440,256]{2,1,0:T(8,128)(2,1)} %collective-permute-done.5), kind=kLoop, calls=%fused_computation | loop fusion | flops 5160960 | bytes 8847360 | tf_op jit(solution)/shard_map/convert_element_type | solution.py:366
  91.6 0.0 collective-permute-done.15
  91.7 1.5 %collective-permute-done.10 = bf16[288,128]{1,0:T(8,128)(2,1)S(1)} collective-permute-done((bf16[288,128]{1,0:T(8,128)(2,1)S(1)}, bf16[288,128]{1,0:T(8,128)(2,1)S(1)}, u32[]{:S(2)}, u32[]{:S(2)}) %collective-permute-start.10) | collective-permute-done | bytes 73760 | tf_op jit(solution)/shard_map/ppermute | solution.py:258
  93.2 0.1 collective-permute-start.16
  93.3 0.5 collective-permute-start.18
  93.8 4.9 %collective-permute-done.16 = bf16[576,128]{1,0:T(8,128)(2,1)S(1)} collective-permute-done((bf16[576,128]{1,0:T(8,128)(2,1)S(1)}, bf16[576,128]{1,0:T(8,128)(2,1)S(1)}, u32[]{:S(2)}, u32[]{:S(2)}) %collective-permute-start.16) | collective-permute-done | bytes 147488 | tf_op jit(solution)/shard_map/ppermute | solution.py:258
  98.8 0.1 maximum_select_fusion
  98.9 0.1 collective-permute-start.17
  98.9 0.0 collective-permute-done.18
  99.0 0.1 maximum_select_fusion.1
  99.0 0.5 collective-permute-start.19
  99.6 0.9 collective-permute-done.17
  100.5 0.4 collective-permute-done.19
  101.0 1.6 %convert_multiply_fusion = f32[9,256,256]{2,1,0:T(8,128)} fusion(bf16[9,128,128]{2,1,0:T(8,128)(2,1)S(1)} %bitcast.11, bf16[9,128,128]{2,1,0:T(8,128)(2,1)S(1)} %bitcast.10, bf16[9,128,128]{2,1,0:T(8,128)(2,1)S(1)} %bitcast.9, bf16[9,128,128]{2,1,0:T(8,128)(2,1)S(1)} %bitcast.8), kind=kLoop, calls=%fused_computation.1 | loop fusion | flops 5308416 | bytes 3538944 | tf_op jit(solution)/shard_map/mul | solution.py:372
  (28 shorter events, 0.4 us)
Async XLA Ops:
  0.6 8.9 %copy-start = (f32[32,9,3]{0,2,1:T(4,128)S(1)}, f32[32,9,3]{0,2,1:T(4,128)}, u32[]{:S(2)}) copy-start(f32[32,9,3]{0,2,1:T(4,128)} %param.11) | copy-start | bytes 10372
  0.6 6.0 %copy-start.1 = (bf16[2,1440,256]{2,1,0:T(8,128)(2,1)S(1)}, bf16[2,1440,256]{2,1,0:T(8,128)(2,1)}, u32[]{:S(2)}) copy-start(bf16[2,1440,256]{2,1,0:T(8,128)(2,1)} %refs_1_.3) | copy-start | bytes 4423684
  0.7 8.4 %copy-start.7 = (s32[32,9,3]{0,2,1:T(4,128)S(1)}, s32[32,9,3]{0,2,1:T(4,128)}, u32[]{:S(2)}) copy-start(s32[32,9,3]{0,2,1:T(4,128)} %param.10) | copy-start | bytes 10372
  0.7 8.4 %copy-start.8 = (s32[32,9,3]{0,2,1:T(4,128)S(1)}, s32[32,9,3]{0,2,1:T(4,128)}, u32[]{:S(2)}) copy-start(s32[32,9,3]{0,2,1:T(4,128)} %param.9) | copy-start | bytes 10372
  0.7 27.9 %collective-permute-start.2 = (bf16[2,1440,256]{2,1,0:T(8,128)(2,1)}, bf16[2,1440,256]{2,1,0:T(8,128)(2,1)}, u32[]{:S(2)}, u32[]{:S(2)}) collective-permute-start(bf16[2,1440,256]{2,1,0:T(8,128)(2,1)} %refs_1_.3), channel_id=1, source_target_pairs={{3,4},{4,3},{7,8},{8,7},{11,12},{12,11},{19,20},{20,19},{23,24},{2... | collective-permute-start | bytes 4423688 | tf_op jit(solution)/shard_map/ppermute | solution.py:323
  2.6 26.0 %collective-permute-start.3 = (bf16[2,1440,256]{2,1,0:T(8,128)(2,1)}, bf16[2,1440,256]{2,1,0:T(8,128)(2,1)}, u32[]{:S(2)}, u32[]{:S(2)}) collective-permute-start(bf16[2,1440,256]{2,1,0:T(8,128)(2,1)} %refs_1_.3), channel_id=1, source_target_pairs={{0,1},{1,0},{2,3},{3,2},{4,5},{5,4},{6,7},{7,6},{8,9},{9,8},{10,11... | collective-permute-start | bytes 4423688 | tf_op jit(solution)/shard_map/ppermute | solution.py:328
  5.1 23.5 %collective-permute-start.1 = (bf16[2,1440,128]{2,1,0:T(8,128)(2,1)}, bf16[2,1440,128]{2,1,0:T(8,128)(2,1)}, u32[]{:S(2)}, u32[]{:S(2)}) collective-permute-start(bf16[2,1440,128]{2,1,0:T(8,128)(2,1)} %slice.6), channel_id=1, source_target_pairs={{1,2},{2,1},{5,6},{6,5},{9,10},{10,9},{13,14},{14,13},{17,18},{18,... | collective-permute-start | bytes 2211848 | tf_op jit(solution)/shard_map/ppermute | solution.py:325
  7.5 37.5 %collective-permute-start = (bf16[2,1440,128]{2,1,0:T(8,128)(2,1)}, bf16[2,1440,128]{2,1,0:T(8,128)(2,1)}, u32[]{:S(2)}, u32[]{:S(2)}) collective-permute-start(bf16[2,1440,128]{2,1,0:T(8,128)(2,1)} %slice.7), channel_id=1, source_target_pairs={{1,2},{2,1},{5,6},{6,5},{9,10},{10,9},{13,14},{14,13},{17,18},{18,... | collective-permute-start | bytes 2211848 | tf_op jit(solution)/shard_map/ppermute | solution.py:327
  9.1 19.5 %copy-start.2 = (bf16[2,1440,256]{2,1,0:T(8,128)(2,1)S(1)}, bf16[2,1440,256]{2,1,0:T(8,128)(2,1)}, u32[]{:S(2)}) copy-start(bf16[2,1440,256]{2,1,0:T(8,128)(2,1)} %refs_5_.3) | copy-start | bytes 4423684
  9.8 18.8 %copy-start.3 = (bf16[9,256,256]{2,1,0:T(8,128)(2,1)S(1)}, bf16[9,256,256]{2,1,0:T(8,128)(2,1)}, u32[]{:S(2)}) copy-start(bf16[9,256,256]{2,1,0:T(8,128)(2,1)} %refs_6_.3) | copy-start | bytes 3538948
  10.6 18.1 %copy-start.5 = (f32[2,9,10]{2,1,0:T(8,128)S(1)}, f32[2,9,10]{2,1,0:T(8,128)}, u32[]{:S(2)}) copy-start(f32[2,9,10]{2,1,0:T(8,128)} %maximum_maximum_fusion.table.refs_0_) | copy-start | bytes 2164
  39.3 21.9 %collective-permute-start.5 = (bf16[2,1440,256]{2,1,0:T(8,128)(2,1)}, bf16[2,1440,256]{2,1,0:T(8,128)(2,1)}, u32[]{:S(2)}, u32[]{:S(2)}) collective-permute-start(bf16[2,1440,256]{2,1,0:T(8,128)(2,1)} %get-tuple-element.45), channel_id=1, source_target_pairs={{3,4},{4,3},{7,8},{8,7},{11,12},{12,11},{19,20},{20,19},{23,24},{2... | collective-permute-start | bytes 4423688 | tf_op jit(solution)/shard_map/ppermute | solution.py:341
  41.1 20.0 %collective-permute-start.6 = (bf16[2,1440,256]{2,1,0:T(8,128)(2,1)}, bf16[2,1440,256]{2,1,0:T(8,128)(2,1)}, u32[]{:S(2)}, u32[]{:S(2)}) collective-permute-start(bf16[2,1440,256]{2,1,0:T(8,128)(2,1)} %get-tuple-element.47), channel_id=1, source_target_pairs={{0,1},{1,0},{2,3},{3,2},{4,5},{5,4},{6,7},{7,6},{8,9},{9,8},{10,11... | collective-permute-start | bytes 4423688 | tf_op jit(solution)/shard_map/ppermute | solution.py:343
  56.5 1.0 copy-start.4
  57.5 2.2 %collective-permute-start.4 = (bf16[2304,128]{1,0:T(8,128)(2,1)}, bf16[2304,128]{1,0:T(8,128)(2,1)S(1)}, u32[]{:S(2)}, u32[]{:S(2)}) collective-permute-start(bf16[2304,128]{1,0:T(8,128)(2,1)} %bitcast.1), channel_id=1, source_target_pairs={{0,1},{1,0},{2,3},{3,2},{4,5},{5,4},{6,7},{7,6},{8,9},{9,8},{10,11... | collective-permute-start | bytes 1769480 | tf_op jit(solution)/shard_map/ppermute | solution.py:258
  61.3 6.7 %collective-permute-start.11 = (bf16[576,128]{1,0:T(8,128)(2,1)S(1)}, bf16[576,128]{1,0:T(8,128)(2,1)S(1)}, u32[]{:S(2)}, u32[]{:S(2)}) collective-permute-start(bf16[576,128]{1,0:T(8,128)(2,1)S(1)} %dynamic-slice_convert_fusion), channel_id=1, source_target_pairs={{0,2},{1,3},{2,0},{3,1},{4,6},{5,7},{6,4},{7,5},{8,10},{9,11},{10,... | collective-permute-start | bytes 442376 | tf_op jit(solution)/shard_map/ppermute | solution.py:258
  62.2 17.9 %collective-permute-start.14 = (bf16[2,1440,256]{2,1,0:T(8,128)(2,1)}, bf16[2,1440,256]{2,1,0:T(8,128)(2,1)S(1)}, u32[]{:S(2)}, u32[]{:S(2)}) collective-permute-start(bf16[2,1440,256]{2,1,0:T(8,128)(2,1)} %get-tuple-element.45), channel_id=1, source_target_pairs={{1,2},{2,1},{5,6},{6,5},{9,10},{10,9},{13,14},{14,13},{17,18},{18,... | collective-permute-start | bytes 4423688 | tf_op jit(solution)/shard_map/ppermute | solution.py:342
  63.2 24.7 %copy-start.6 = (f32[2,1440,256]{2,1,0:T(8,128)S(1)}, f32[2,1440,256]{2,1,0:T(8,128)}, u32[]{:S(2)}) copy-start(f32[2,1440,256]{2,1,0:T(8,128)} %get-tuple-element.50) | copy-start | bytes 8847364
  63.2 6.3 %collective-permute-start.7 = (bf16[576,128]{1,0:T(8,128)(2,1)S(1)}, bf16[576,128]{1,0:T(8,128)(2,1)S(1)}, u32[]{:S(2)}, u32[]{:S(2)}) collective-permute-start(bf16[576,128]{1,0:T(8,128)(2,1)S(1)} %dynamic-slice_convert_fusion.1), channel_id=1, source_target_pairs={{0,4},{1,5},{2,6},{3,7},{4,0},{5,1},{6,2},{7,3},{8,12},{9,13},{10,... | collective-permute-start | bytes 442376 | tf_op jit(solution)/shard_map/ppermute | solution.py:258
  68.0 4.5 %collective-permute-start.12 = (bf16[288,128]{1,0:T(8,128)(2,1)S(1)}, bf16[288,128]{1,0:T(8,128)(2,1)S(1)}, u32[]{:S(2)}, u32[]{:S(2)}) collective-permute-start(bf16[288,128]{1,0:T(8,128)(2,1)S(1)} %dynamic-slice_convert_fusion.2), channel_id=1, source_target_pairs={{0,4},{1,5},{2,6},{3,7},{4,0},{5,1},{6,2},{7,3},{8,12},{9,13},{10,... | collective-permute-start | bytes 221192 | tf_op jit(solution)/shard_map/ppermute | solution.py:258
  69.5 9.3 %collective-permute-start.8 = (bf16[288,128]{1,0:T(8,128)(2,1)S(1)}, bf16[288,128]{1,0:T(8,128)(2,1)S(1)}, u32[]{:S(2)}, u32[]{:S(2)}) collective-permute-start(bf16[288,128]{1,0:T(8,128)(2,1)S(1)} %dynamic-slice_convert_fusion.3), channel_id=1, source_target_pairs={{0,8},{1,9},{2,10},{3,11},{4,12},{5,13},{6,14},{7,15},{8,0},{9,1},... | collective-permute-start | bytes 221192 | tf_op jit(solution)/shard_map/ppermute | solution.py:258
  72.5 7.6 %collective-permute-start.13 = (bf16[288,128]{1,0:T(8,128)(2,1)S(1)}, bf16[288,128]{1,0:T(8,128)(2,1)S(1)}, u32[]{:S(2)}, u32[]{:S(2)}) collective-permute-start(bf16[288,128]{1,0:T(8,128)(2,1)S(1)} %add_convert_fusion.2), channel_id=1, source_target_pairs={{0,8},{1,9},{2,10},{3,11},{4,12},{5,13},{6,14},{7,15},{8,0},{9,1},... | collective-permute-start | bytes 221192 | tf_op jit(solution)/shard_map/ppermute | solution.py:258
  78.8 7.7 %collective-permute-start.9 = (bf16[288,128]{1,0:T(8,128)(2,1)S(1)}, bf16[288,128]{1,0:T(8,128)(2,1)S(1)}, u32[]{:S(2)}, u32[]{:S(2)}) collective-permute-start(bf16[288,128]{1,0:T(8,128)(2,1)S(1)} %add_convert_fusion.4), channel_id=1, source_target_pairs={{0,2},{1,3},{2,0},{3,1},{4,6},{5,7},{6,4},{7,5},{8,10},{9,11},{10,... | collective-permute-start | bytes 221192 | tf_op jit(solution)/shard_map/ppermute | solution.py:258
  80.1 11.5 %collective-permute-start.15 = (bf16[288,128]{1,0:T(8,128)(2,1)S(1)}, bf16[288,128]{1,0:T(8,128)(2,1)S(1)}, u32[]{:S(2)}, u32[]{:S(2)}) collective-permute-start(bf16[288,128]{1,0:T(8,128)(2,1)S(1)} %add_convert_fusion.1), channel_id=1, source_target_pairs={{0,4},{1,5},{2,6},{3,7},{4,0},{5,1},{6,2},{7,3},{8,12},{9,13},{10,... | collective-permute-start | bytes 221192 | tf_op jit(solution)/shard_map/ppermute | solution.py:258
  86.6 6.6 %collective-permute-start.10 = (bf16[288,128]{1,0:T(8,128)(2,1)S(1)}, bf16[288,128]{1,0:T(8,128)(2,1)S(1)}, u32[]{:S(2)}, u32[]{:S(2)}) collective-permute-start(bf16[288,128]{1,0:T(8,128)(2,1)S(1)} %add_convert_fusion.3), channel_id=1, source_target_pairs={{0,8},{1,9},{2,10},{3,11},{4,12},{5,13},{6,14},{7,15},{8,0},{9,1},... | collective-permute-start | bytes 221192 | tf_op jit(solution)/shard_map/ppermute | solution.py:258
  93.2 5.5 %collective-permute-start.16 = (bf16[576,128]{1,0:T(8,128)(2,1)S(1)}, bf16[576,128]{1,0:T(8,128)(2,1)S(1)}, u32[]{:S(2)}, u32[]{:S(2)}) collective-permute-start(bf16[576,128]{1,0:T(8,128)(2,1)S(1)} %maximum_select_fusion.2), channel_id=1, source_target_pairs={{0,4},{1,5},{2,6},{3,7},{4,0},{5,1},{6,2},{7,3},{8,12},{9,13},{10,... | collective-permute-start | bytes 442376 | tf_op jit(solution)/shard_map/ppermute | solution.py:258
  93.3 5.6 %collective-permute-start.18 = (bf16[576,128]{1,0:T(8,128)(2,1)S(1)}, bf16[576,128]{1,0:T(8,128)(2,1)S(1)}, u32[]{:S(2)}, u32[]{:S(2)}) collective-permute-start(bf16[576,128]{1,0:T(8,128)(2,1)S(1)} %maximum_select_fusion.3), channel_id=1, source_target_pairs={{0,2},{1,3},{2,0},{3,1},{4,6},{5,7},{6,4},{7,5},{8,10},{9,11},{10,... | collective-permute-start | bytes 442376 | tf_op jit(solution)/shard_map/ppermute | solution.py:258
  98.9 1.6 %collective-permute-start.17 = (bf16[1152,128]{1,0:T(8,128)(2,1)S(1)}, bf16[1152,128]{1,0:T(8,128)(2,1)S(1)}, u32[]{:S(2)}, u32[]{:S(2)}) collective-permute-start(bf16[1152,128]{1,0:T(8,128)(2,1)S(1)} %maximum_select_fusion), channel_id=1, source_target_pairs={{0,1},{1,0},{2,3},{3,2},{4,5},{5,4},{6,7},{7,6},{8,9},{9,8},{10,11... | collective-permute-start | bytes 884744 | tf_op jit(solution)/shard_map/ppermute | solution.py:258
  99.0 1.9 %collective-permute-start.19 = (bf16[1152,128]{1,0:T(8,128)(2,1)S(1)}, bf16[1152,128]{1,0:T(8,128)(2,1)S(1)}, u32[]{:S(2)}, u32[]{:S(2)}) collective-permute-start(bf16[1152,128]{1,0:T(8,128)(2,1)S(1)} %maximum_select_fusion.1), channel_id=1, source_target_pairs={{0,1},{1,0},{2,3},{3,2},{4,5},{5,4},{6,7},{7,6},{8,9},{9,8},{10,11... | collective-permute-start | bytes 884744 | tf_op jit(solution)/shard_map/ppermute | solution.py:258

commit v6 on v5

--- a/solution.py
+++ b/solution.py
@@ -61,7 +61,7 @@
             basis[i * width : (i + 1) * width, cols] = t.astype(jnp.bfloat16)
             return carry
 
-        lax.fori_loop(0, nk, per_k, 0)
+        lax.fori_loop(0, nk, per_k, 0, unroll=3)
     wflat = weight[...].reshape(nk * HALF, chan)
     parts = 3 * rows
     tile = rows * width // parts

time: 103 us -> 102 us (level)
  waiting for transfers between devices: 26 us -> 19.1 us
  starting transfers between devices: 22.8 us -> 28 us
    ppermute x13, waiting for transfers between devices: 25.9 us -> 19.1 us  [swap(): return lax.ppermute(value, 'lat', [(i, i ^ bit) for i in range(size)])]
    ppermute x13, starting transfers between devices: 10.5 us -> 16 us  [swap(): return lax.ppermute(value, 'lat', [(i, i ^ bit) for i in range(size)])]
  transfers between devices with their start and end apart: 20 -> 20, of which waited for: 10 -> 11; matrix products, arithmetic and copies ran while one was open for 10% -> 10% of each run, Pallas kernels for 39% -> 40%
where the time goes in v6:
time: 102 us; the launch traced here: 101 us
  Pallas kernels  40.1 us (39%)
  starting transfers between devices  28 us (27%)
  waiting for transfers between devices  19.1 us (19%)
  other arithmetic  7.99 us (8%)
  local copies, waits for them, and re-layouts  4.9 us (5%)
    pallas_call x2, Pallas kernels, forward(): pl.pallas_call(lambda *refs: fwd_kernel(last, *refs), grid=(1,), in_specs...  21.9 us
    ppermute x13, waiting for transfers between devices, swap(): return lax.ppermute(value, 'lat', [(i, i ^ bit) for i in range(size)])  19.1 us
    pallas_call x1, Pallas kernels, backward(): pl.pallas_call(bwd_kernel, in_specs=[smem] + [pl.BlockSpec(memory_space=p...  18.3 us
    ppermute x13, starting transfers between devices, swap(): return lax.ppermute(value, 'lat', [(i, i ^ bit) for i in range(size)])  16 us
    ppermute x1, starting transfers between devices, per_device(): got_fast = lax.ppermute(edge_fast, 'lat', fast_pairs)  3.77 us
    convert_element_type x1, other arithmetic, between(): grad = grad.astype(jnp.bfloat16)  3.75 us
  transfers between devices with their start and end apart: 20, of which 11 were waited for; matrix products, arithmetic and copies ran while one was open for 10% of the time, Pallas kernels for 40%

profile of v6, /device:TPU:0, one launch (start us, length us, event | category | flops | bytes accessed | tf_op | source)
XLA Modules:
  0.0 101.1 jit_solution(11444127544367367767)
XLA Ops:
  0.6 0.0 copy-start
  0.6 0.0 copy-start.1
  0.7 1.9 %collective-permute-start.2 = (bf16[2,1440,256]{2,1,0:T(8,128)(2,1)}, bf16[2,1440,256]{2,1,0:T(8,128)(2,1)}, u32[]{:S(2)}, u32[]{:S(2)}) collective-permute-start(bf16[2,1440,256]{2,1,0:T(8,128)(2,1)} %refs_1_.3), channel_id=1, source_target_pairs={{3,4},{4,3},{7,8},{8,7},{11,12},{12,11},{19,20},{20,19},{23,24},{2... | collective-permute-start | bytes 4423688 | tf_op jit(solution)/shard_map/ppermute | solution.py:323
  2.6 0.5 collective-permute-start.3
  3.0 2.0 %slice.6 = bf16[2,1440,128]{2,1,0:T(8,128)(2,1)} slice(bf16[2,1440,256]{2,1,0:T(8,128)(2,1)} %refs_1_.3), slice={[0:2], [0:1440], [0:128]} | slice | bytes 1474560 | tf_op jit(solution)/shard_map/slice | solution.py:324
  5.1 1.5 %collective-permute-start.1 = (bf16[2,1440,128]{2,1,0:T(8,128)(2,1)}, bf16[2,1440,128]{2,1,0:T(8,128)(2,1)}, u32[]{:S(2)}, u32[]{:S(2)}) collective-permute-start(bf16[2,1440,128]{2,1,0:T(8,128)(2,1)} %slice.6), channel_id=1, source_target_pairs={{1,2},{2,1},{5,6},{6,5},{9,10},{10,9},{13,14},{14,13},{17,18},{18,... | collective-permute-start | bytes 2211848 | tf_op jit(solution)/shard_map/ppermute | solution.py:325
  6.6 0.0 copy-done.1
  6.6 0.9 slice.7
  7.5 1.5 %collective-permute-start = (bf16[2,1440,128]{2,1,0:T(8,128)(2,1)}, bf16[2,1440,128]{2,1,0:T(8,128)(2,1)}, u32[]{:S(2)}, u32[]{:S(2)}) collective-permute-start(bf16[2,1440,128]{2,1,0:T(8,128)(2,1)} %slice.7), channel_id=1, source_target_pairs={{1,2},{2,1},{5,6},{6,5},{9,10},{10,9},{13,14},{14,13},{17,18},{18,... | collective-permute-start | bytes 2211848 | tf_op jit(solution)/shard_map/ppermute | solution.py:327
  9.1 0.0 copy-done.7
  9.1 0.1 constant_dynamic-slice_fusion.1
  9.1 0.0 copy-start.2
  9.2 0.2 copy.12
  9.3 0.2 copy.13
  9.5 0.1 constant_dynamic-slice_fusion
  9.6 0.2 copy.14
  9.8 0.1 pad.23.clone
  9.9 0.7 maximum_maximum_fusion.table.refs_0_
  10.6 18.3 %backward.1 = (f32[2,1440,256]{2,1,0:T(8,128)}, bf16[2,1440,256]{2,1,0:T(8,128)(2,1)}, bf16[2,1440,256]{2,1,0:T(8,128)(2,1)}) custom-call(f32[2,9,10]{2,1,0:T(8,128)} %maximum_maximum_fusion.table.refs_0_, bf16[2,1440,256]{2,1,0:T(8,128)(2,1)} %refs_5_.3, bf16[9,256,256]{2,1,0:T(8,128)(2,1)} %refs_6_.3), custom_call_target="tpu_custom_call" | custom-call | tf_op jit(solution)/shard_map/backward/pallas_call | solution.py:228
  28.8 0.0 collective-permute-done.1.refs_2_
  28.8 0.0 collective-permute-done.2.refs_3_
  28.8 0.0 collective-permute-done.3.refs_4_
  28.9 10.5 %forward.2 = (f32[2,1440,256]{2,1,0:T(8,128)S(1)}, f32[9,128,128]{2,1,0:T(8,128)S(1)}, bf16[9,128,128]{2,1,0:T(8,128)(2,1)S(1)}) custom-call(f32[2,9,10]{2,1,0:T(8,128)S(1)} %copy-done.5, bf16[2,1440,256]{2,1,0:T(8,128)(2,1)S(1)} %copy-done.1, bf16[2,1440,128]{2,1,0:T(8,128)(2,1)} %collective-permute-done.1.refs_2_, ...), custom_call_target="tpu_custom_call" | custom-call | tf_op jit(solution)/shard_map/forward/pallas_call | solution.py:103
  39.4 1.9 %collective-permute-start.5 = (bf16[2,1440,256]{2,1,0:T(8,128)(2,1)}, bf16[2,1440,256]{2,1,0:T(8,128)(2,1)}, u32[]{:S(2)}, u32[]{:S(2)}) collective-permute-start(bf16[2,1440,256]{2,1,0:T(8,128)(2,1)} %get-tuple-element.45), channel_id=1, source_target_pairs={{3,4},{4,3},{7,8},{8,7},{11,12},{12,11},{19,20},{20,19},{23,24},{2... | collective-permute-start | bytes 4423688 | tf_op jit(solution)/shard_map/ppermute | solution.py:341
  41.3 3.8 %collective-permute-start.6 = (bf16[2,1440,256]{2,1,0:T(8,128)(2,1)}, bf16[2,1440,256]{2,1,0:T(8,128)(2,1)}, u32[]{:S(2)}, u32[]{:S(2)}) collective-permute-start(bf16[2,1440,256]{2,1,0:T(8,128)(2,1)} %get-tuple-element.47), channel_id=1, source_target_pairs={{0,1},{1,0},{2,3},{3,2},{4,5},{5,4},{6,7},{7,6},{8,9},{9,8},{10,11... | collective-permute-start | bytes 4423688 | tf_op jit(solution)/shard_map/ppermute | solution.py:343
  45.1 0.0 collective-permute-done.refs_2_
  45.1 11.4 %forward.3 = (bf16[2,1440,256]{2,1,0:T(8,128)(2,1)}, f32[18,128,128]{2,1,0:T(8,128)S(1)}, bf16[18,128,128]{2,1,0:T(8,128)(2,1)}) custom-call(f32[2,9,10]{2,1,0:T(8,128)S(1)} %copy-done.5, bf16[2,1440,256]{2,1,0:T(8,128)(2,1)S(1)} %copy-done.1, bf16[2,1440,128]{2,1,0:T(8,128)(2,1)} %collective-permute-done.refs_2_, ...), custom_call_target="tpu_custom_call" | custom-call | tf_op jit(solution)/shard_map/forward/pallas_call | solution.py:103
  56.4 1.0 copy-done.4
  57.4 0.0 collective-permute-start.4
  57.4 2.2 %collective-permute-done.4 = bf16[2304,128]{1,0:T(8,128)(2,1)S(1)} collective-permute-done((bf16[2304,128]{1,0:T(8,128)(2,1)}, bf16[2304,128]{1,0:T(8,128)(2,1)S(1)}, u32[]{:S(2)}, u32[]{:S(2)}) %collective-permute-start.4) | collective-permute-done | bytes 589856 | tf_op jit(solution)/shard_map/ppermute | solution.py:258
  59.6 1.4 %bitcast_add_fusion = f32[2304,128]{1,0:T(8,128)S(1)} fusion(f32[18,128,128]{2,1,0:T(8,128)} %copy-done.4, bf16[2304,128]{1,0:T(8,128)(2,1)S(1)} %collective-permute-done.4), kind=kLoop, calls=%fused_computation.2 | loop fusion | flops 589824 | bytes 2949120 | tf_op jit(solution)/shard_map/add | solution.py:266
  61.0 0.0 collective-permute-done.5
  61.1 0.0 collective-permute-done.6
  61.1 0.1 fusion
  61.2 1.0 %collective-permute-start.11 = (bf16[576,128]{1,0:T(8,128)(2,1)S(1)}, bf16[576,128]{1,0:T(8,128)(2,1)S(1)}, u32[]{:S(2)}, u32[]{:S(2)}) collective-permute-start(bf16[576,128]{1,0:T(8,128)(2,1)S(1)} %dynamic-slice_convert_fusion), channel_id=1, source_target_pairs={{0,2},{1,3},{2,0},{3,1},{4,6},{5,7},{6,4},{7,5},{8,10},{9,11},{10,... | collective-permute-start | bytes 442376 | tf_op jit(solution)/shard_map/ppermute | solution.py:258
  62.2 1.0 collective-permute-start.14
  63.2 1.0 collective-permute-start.7
  64.2 3.0 %collective-permute-done.11 = bf16[576,128]{1,0:T(8,128)(2,1)S(1)} collective-permute-done((bf16[576,128]{1,0:T(8,128)(2,1)S(1)}, bf16[576,128]{1,0:T(8,128)(2,1)S(1)}, u32[]{:S(2)}, u32[]{:S(2)}) %collective-permute-start.11) | collective-permute-done | bytes 147488 | tf_op jit(solution)/shard_map/ppermute | solution.py:258
  67.2 0.8 collective-permute-start.12
  68.0 0.6 collective-permute-done.7
  68.6 2.6 %collective-permute-start.8 = (bf16[288,128]{1,0:T(8,128)(2,1)S(1)}, bf16[288,128]{1,0:T(8,128)(2,1)S(1)}, u32[]{:S(2)}, u32[]{:S(2)}) collective-permute-start(bf16[288,128]{1,0:T(8,128)(2,1)S(1)} %dynamic-slice_convert_fusion.3), channel_id=1, source_target_pairs={{0,8},{1,9},{2,10},{3,11},{4,12},{5,13},{6,14},{7,15},{8,0},{9,1},... | collective-permute-start | bytes 221192 | tf_op jit(solution)/shard_map/ppermute | solution.py:258
  71.2 0.4 collective-permute-done.12
  71.7 2.0 %collective-permute-start.13 = (bf16[288,128]{1,0:T(8,128)(2,1)S(1)}, bf16[288,128]{1,0:T(8,128)(2,1)S(1)}, u32[]{:S(2)}, u32[]{:S(2)}) collective-permute-start(bf16[288,128]{1,0:T(8,128)(2,1)S(1)} %add_convert_fusion.2), channel_id=1, source_target_pairs={{0,8},{1,9},{2,10},{3,11},{4,12},{5,13},{6,14},{7,15},{8,0},{9,1},... | collective-permute-start | bytes 221192 | tf_op jit(solution)/shard_map/ppermute | solution.py:258
  73.7 2.3 %collective-permute-done.8 = bf16[288,128]{1,0:T(8,128)(2,1)S(1)} collective-permute-done((bf16[288,128]{1,0:T(8,128)(2,1)S(1)}, bf16[288,128]{1,0:T(8,128)(2,1)S(1)}, u32[]{:S(2)}, u32[]{:S(2)}) %collective-permute-start.8) | collective-permute-done | bytes 73760 | tf_op jit(solution)/shard_map/ppermute | solution.py:258
  76.1 4.4 %collective-permute-start.9 = (bf16[288,128]{1,0:T(8,128)(2,1)S(1)}, bf16[288,128]{1,0:T(8,128)(2,1)S(1)}, u32[]{:S(2)}, u32[]{:S(2)}) collective-permute-start(bf16[288,128]{1,0:T(8,128)(2,1)S(1)} %add_convert_fusion.4), channel_id=1, source_target_pairs={{0,2},{1,3},{2,0},{3,1},{4,6},{5,7},{6,4},{7,5},{8,10},{9,11},{10,... | collective-permute-start | bytes 221192 | tf_op jit(solution)/shard_map/ppermute | solution.py:258
  80.5 0.0 collective-permute-done.13
  80.5 0.0 collective-permute-done.14
  80.5 0.1 collective-permute-start.15
  80.6 4.9 %collective-permute-done.9 = bf16[288,128]{1,0:T(8,128)(2,1)S(1)} collective-permute-done((bf16[288,128]{1,0:T(8,128)(2,1)S(1)}, bf16[288,128]{1,0:T(8,128)(2,1)S(1)}, u32[]{:S(2)}, u32[]{:S(2)}) %collective-permute-start.9) | collective-permute-done | bytes 73760 | tf_op jit(solution)/shard_map/ppermute | solution.py:258
  85.5 2.0 %collective-permute-start.10 = (bf16[288,128]{1,0:T(8,128)(2,1)S(1)}, bf16[288,128]{1,0:T(8,128)(2,1)S(1)}, u32[]{:S(2)}, u32[]{:S(2)}) collective-permute-start(bf16[288,128]{1,0:T(8,128)(2,1)S(1)} %add_convert_fusion.3), channel_id=1, source_target_pairs={{0,8},{1,9},{2,10},{3,11},{4,12},{5,13},{6,14},{7,15},{8,0},{9,1},... | collective-permute-start | bytes 221192 | tf_op jit(solution)/shard_map/ppermute | solution.py:258
  87.6 3.7 %add_convert_fusion = bf16[2,1440,256]{2,1,0:T(8,128)(2,1)} fusion(bf16[2,1440,256]{2,1,0:T(8,128)(2,1)} %collective-permute-done.6, f32[2,1440,256]{2,1,0:T(8,128)S(1)} %copy-done.6, bf16[2,1440,256]{2,1,0:T(8,128)(2,1)S(1)} %collective-permute-done.14, bf16[2,1440,256]{2,1,0:T(8,128)(2,1)} %collective-permute-done.5), kind=kLoop, calls=%fused_computation | loop fusion | flops 5160960 | bytes 8847360 | tf_op jit(solution)/shard_map/convert_element_type | solution.py:366
  91.3 0.0 collective-permute-done.15
  91.4 0.6 collective-permute-done.10
  92.0 0.3 collective-permute-start.16
  92.3 1.2 %collective-permute-start.18 = (bf16[576,128]{1,0:T(8,128)(2,1)S(1)}, bf16[576,128]{1,0:T(8,128)(2,1)S(1)}, u32[]{:S(2)}, u32[]{:S(2)}) collective-permute-start(bf16[576,128]{1,0:T(8,128)(2,1)S(1)} %maximum_select_fusion.3), channel_id=1, source_target_pairs={{0,2},{1,3},{2,0},{3,1},{4,6},{5,7},{6,4},{7,5},{8,10},{9,11},{10,... | collective-permute-start | bytes 442376 | tf_op jit(solution)/shard_map/ppermute | solution.py:258
  93.5 3.7 %collective-permute-done.16 = bf16[576,128]{1,0:T(8,128)(2,1)S(1)} collective-permute-done((bf16[576,128]{1,0:T(8,128)(2,1)S(1)}, bf16[576,128]{1,0:T(8,128)(2,1)S(1)}, u32[]{:S(2)}, u32[]{:S(2)}) %collective-permute-start.16) | collective-permute-done | bytes 147488 | tf_op jit(solution)/shard_map/ppermute | solution.py:258
  97.2 0.1 maximum_select_fusion
  97.3 0.1 collective-permute-start.17
  97.4 0.1 collective-permute-done.18
  97.5 0.1 maximum_select_fusion.1
  97.6 0.5 collective-permute-start.19
  98.1 0.9 collective-permute-done.17
  99.0 0.4 collective-permute-done.19
  99.4 1.6 %convert_multiply_fusion = f32[9,256,256]{2,1,0:T(8,128)} fusion(bf16[9,128,128]{2,1,0:T(8,128)(2,1)S(1)} %bitcast.11, bf16[9,128,128]{2,1,0:T(8,128)(2,1)S(1)} %bitcast.10, bf16[9,128,128]{2,1,0:T(8,128)(2,1)S(1)} %bitcast.9, bf16[9,128,128]{2,1,0:T(8,128)(2,1)S(1)} %bitcast.8), kind=kLoop, calls=%fused_computation.1 | loop fusion | flops 5308416 | bytes 3538944 | tf_op jit(solution)/shard_map/mul | solution.py:372
  (28 shorter events, 0.4 us)
Async XLA Ops:
  0.6 8.9 %copy-start = (f32[32,9,3]{0,2,1:T(4,128)S(1)}, f32[32,9,3]{0,2,1:T(4,128)}, u32[]{:S(2)}) copy-start(f32[32,9,3]{0,2,1:T(4,128)} %param.11) | copy-start | bytes 10372
  0.6 6.0 %copy-start.1 = (bf16[2,1440,256]{2,1,0:T(8,128)(2,1)S(1)}, bf16[2,1440,256]{2,1,0:T(8,128)(2,1)}, u32[]{:S(2)}) copy-start(bf16[2,1440,256]{2,1,0:T(8,128)(2,1)} %refs_1_.3) | copy-start | bytes 4423684
  0.7 8.4 %copy-start.7 = (s32[32,9,3]{0,2,1:T(4,128)S(1)}, s32[32,9,3]{0,2,1:T(4,128)}, u32[]{:S(2)}) copy-start(s32[32,9,3]{0,2,1:T(4,128)} %param.10) | copy-start | bytes 10372
  0.7 8.4 %copy-start.8 = (s32[32,9,3]{0,2,1:T(4,128)S(1)}, s32[32,9,3]{0,2,1:T(4,128)}, u32[]{:S(2)}) copy-start(s32[32,9,3]{0,2,1:T(4,128)} %param.9) | copy-start | bytes 10372
  0.7 28.2 %collective-permute-start.2 = (bf16[2,1440,256]{2,1,0:T(8,128)(2,1)}, bf16[2,1440,256]{2,1,0:T(8,128)(2,1)}, u32[]{:S(2)}, u32[]{:S(2)}) collective-permute-start(bf16[2,1440,256]{2,1,0:T(8,128)(2,1)} %refs_1_.3), channel_id=1, source_target_pairs={{3,4},{4,3},{7,8},{8,7},{11,12},{12,11},{19,20},{20,19},{23,24},{2... | collective-permute-start | bytes 4423688 | tf_op jit(solution)/shard_map/ppermute | solution.py:323
  2.6 26.3 %collective-permute-start.3 = (bf16[2,1440,256]{2,1,0:T(8,128)(2,1)}, bf16[2,1440,256]{2,1,0:T(8,128)(2,1)}, u32[]{:S(2)}, u32[]{:S(2)}) collective-permute-start(bf16[2,1440,256]{2,1,0:T(8,128)(2,1)} %refs_1_.3), channel_id=1, source_target_pairs={{0,1},{1,0},{2,3},{3,2},{4,5},{5,4},{6,7},{7,6},{8,9},{9,8},{10,11... | collective-permute-start | bytes 4423688 | tf_op jit(solution)/shard_map/ppermute | solution.py:328
  5.1 23.8 %collective-permute-start.1 = (bf16[2,1440,128]{2,1,0:T(8,128)(2,1)}, bf16[2,1440,128]{2,1,0:T(8,128)(2,1)}, u32[]{:S(2)}, u32[]{:S(2)}) collective-permute-start(bf16[2,1440,128]{2,1,0:T(8,128)(2,1)} %slice.6), channel_id=1, source_target_pairs={{1,2},{2,1},{5,6},{6,5},{9,10},{10,9},{13,14},{14,13},{17,18},{18,... | collective-permute-start | bytes 2211848 | tf_op jit(solution)/shard_map/ppermute | solution.py:325
  7.5 37.5 %collective-permute-start = (bf16[2,1440,128]{2,1,0:T(8,128)(2,1)}, bf16[2,1440,128]{2,1,0:T(8,128)(2,1)}, u32[]{:S(2)}, u32[]{:S(2)}) collective-permute-start(bf16[2,1440,128]{2,1,0:T(8,128)(2,1)} %slice.7), channel_id=1, source_target_pairs={{1,2},{2,1},{5,6},{6,5},{9,10},{10,9},{13,14},{14,13},{17,18},{18,... | collective-permute-start | bytes 2211848 | tf_op jit(solution)/shard_map/ppermute | solution.py:327
  9.1 19.7 %copy-start.2 = (bf16[2,1440,256]{2,1,0:T(8,128)(2,1)S(1)}, bf16[2,1440,256]{2,1,0:T(8,128)(2,1)}, u32[]{:S(2)}) copy-start(bf16[2,1440,256]{2,1,0:T(8,128)(2,1)} %refs_5_.3) | copy-start | bytes 4423684
  9.8 19.1 %copy-start.3 = (bf16[9,256,256]{2,1,0:T(8,128)(2,1)S(1)}, bf16[9,256,256]{2,1,0:T(8,128)(2,1)}, u32[]{:S(2)}) copy-start(bf16[9,256,256]{2,1,0:T(8,128)(2,1)} %refs_6_.3) | copy-start | bytes 3538948
  10.6 18.3 %copy-start.5 = (f32[2,9,10]{2,1,0:T(8,128)S(1)}, f32[2,9,10]{2,1,0:T(8,128)}, u32[]{:S(2)}) copy-start(f32[2,9,10]{2,1,0:T(8,128)} %maximum_maximum_fusion.table.refs_0_) | copy-start | bytes 2164
  39.4 21.6 %collective-permute-start.5 = (bf16[2,1440,256]{2,1,0:T(8,128)(2,1)}, bf16[2,1440,256]{2,1,0:T(8,128)(2,1)}, u32[]{:S(2)}, u32[]{:S(2)}) collective-permute-start(bf16[2,1440,256]{2,1,0:T(8,128)(2,1)} %get-tuple-element.45), channel_id=1, source_target_pairs={{3,4},{4,3},{7,8},{8,7},{11,12},{12,11},{19,20},{20,19},{23,24},{2... | collective-permute-start | bytes 4423688 | tf_op jit(solution)/shard_map/ppermute | solution.py:341
  41.3 19.8 %collective-permute-start.6 = (bf16[2,1440,256]{2,1,0:T(8,128)(2,1)}, bf16[2,1440,256]{2,1,0:T(8,128)(2,1)}, u32[]{:S(2)}, u32[]{:S(2)}) collective-permute-start(bf16[2,1440,256]{2,1,0:T(8,128)(2,1)} %get-tuple-element.47), channel_id=1, source_target_pairs={{0,1},{1,0},{2,3},{3,2},{4,5},{5,4},{6,7},{7,6},{8,9},{9,8},{10,11... | collective-permute-start | bytes 4423688 | tf_op jit(solution)/shard_map/ppermute | solution.py:343
  56.4 1.0 copy-start.4
  57.4 2.2 %collective-permute-start.4 = (bf16[2304,128]{1,0:T(8,128)(2,1)}, bf16[2304,128]{1,0:T(8,128)(2,1)S(1)}, u32[]{:S(2)}, u32[]{:S(2)}) collective-permute-start(bf16[2304,128]{1,0:T(8,128)(2,1)} %bitcast.1), channel_id=1, source_target_pairs={{0,1},{1,0},{2,3},{3,2},{4,5},{5,4},{6,7},{7,6},{8,9},{9,8},{10,11... | collective-permute-start | bytes 1769480 | tf_op jit(solution)/shard_map/ppermute | solution.py:258
  61.2 6.0 %collective-permute-start.11 = (bf16[576,128]{1,0:T(8,128)(2,1)S(1)}, bf16[576,128]{1,0:T(8,128)(2,1)S(1)}, u32[]{:S(2)}, u32[]{:S(2)}) collective-permute-start(bf16[576,128]{1,0:T(8,128)(2,1)S(1)} %dynamic-slice_convert_fusion), channel_id=1, source_target_pairs={{0,2},{1,3},{2,0},{3,1},{4,6},{5,7},{6,4},{7,5},{8,10},{9,11},{10,... | collective-permute-start | bytes 442376 | tf_op jit(solution)/shard_map/ppermute | solution.py:258
  62.2 18.3 %collective-permute-start.14 = (bf16[2,1440,256]{2,1,0:T(8,128)(2,1)}, bf16[2,1440,256]{2,1,0:T(8,128)(2,1)S(1)}, u32[]{:S(2)}, u32[]{:S(2)}) collective-permute-start(bf16[2,1440,256]{2,1,0:T(8,128)(2,1)} %get-tuple-element.45), channel_id=1, source_target_pairs={{1,2},{2,1},{5,6},{6,5},{9,10},{10,9},{13,14},{14,13},{17,18},{18,... | collective-permute-start | bytes 4423688 | tf_op jit(solution)/shard_map/ppermute | solution.py:342
  63.2 24.4 %copy-start.6 = (f32[2,1440,256]{2,1,0:T(8,128)S(1)}, f32[2,1440,256]{2,1,0:T(8,128)}, u32[]{:S(2)}) copy-start(f32[2,1440,256]{2,1,0:T(8,128)} %get-tuple-element.50) | copy-start | bytes 8847364
  63.2 5.4 %collective-permute-start.7 = (bf16[576,128]{1,0:T(8,128)(2,1)S(1)}, bf16[576,128]{1,0:T(8,128)(2,1)S(1)}, u32[]{:S(2)}, u32[]{:S(2)}) collective-permute-start(bf16[576,128]{1,0:T(8,128)(2,1)S(1)} %dynamic-slice_convert_fusion.1), channel_id=1, source_target_pairs={{0,4},{1,5},{2,6},{3,7},{4,0},{5,1},{6,2},{7,3},{8,12},{9,13},{10,... | collective-permute-start | bytes 442376 | tf_op jit(solution)/shard_map/ppermute | solution.py:258
  67.2 4.4 %collective-permute-start.12 = (bf16[288,128]{1,0:T(8,128)(2,1)S(1)}, bf16[288,128]{1,0:T(8,128)(2,1)S(1)}, u32[]{:S(2)}, u32[]{:S(2)}) collective-permute-start(bf16[288,128]{1,0:T(8,128)(2,1)S(1)} %dynamic-slice_convert_fusion.2), channel_id=1, source_target_pairs={{0,4},{1,5},{2,6},{3,7},{4,0},{5,1},{6,2},{7,3},{8,12},{9,13},{10,... | collective-permute-start | bytes 221192 | tf_op jit(solution)/shard_map/ppermute | solution.py:258
  68.6 7.4 %collective-permute-start.8 = (bf16[288,128]{1,0:T(8,128)(2,1)S(1)}, bf16[288,128]{1,0:T(8,128)(2,1)S(1)}, u32[]{:S(2)}, u32[]{:S(2)}) collective-permute-start(bf16[288,128]{1,0:T(8,128)(2,1)S(1)} %dynamic-slice_convert_fusion.3), channel_id=1, source_target_pairs={{0,8},{1,9},{2,10},{3,11},{4,12},{5,13},{6,14},{7,15},{8,0},{9,1},... | collective-permute-start | bytes 221192 | tf_op jit(solution)/shard_map/ppermute | solution.py:258
  71.7 8.8 %collective-permute-start.13 = (bf16[288,128]{1,0:T(8,128)(2,1)S(1)}, bf16[288,128]{1,0:T(8,128)(2,1)S(1)}, u32[]{:S(2)}, u32[]{:S(2)}) collective-permute-start(bf16[288,128]{1,0:T(8,128)(2,1)S(1)} %add_convert_fusion.2), channel_id=1, source_target_pairs={{0,8},{1,9},{2,10},{3,11},{4,12},{5,13},{6,14},{7,15},{8,0},{9,1},... | collective-permute-start | bytes 221192 | tf_op jit(solution)/shard_map/ppermute | solution.py:258
  76.1 9.4 %collective-permute-start.9 = (bf16[288,128]{1,0:T(8,128)(2,1)S(1)}, bf16[288,128]{1,0:T(8,128)(2,1)S(1)}, u32[]{:S(2)}, u32[]{:S(2)}) collective-permute-start(bf16[288,128]{1,0:T(8,128)(2,1)S(1)} %add_convert_fusion.4), channel_id=1, source_target_pairs={{0,2},{1,3},{2,0},{3,1},{4,6},{5,7},{6,4},{7,5},{8,10},{9,11},{10,... | collective-permute-start | bytes 221192 | tf_op jit(solution)/shard_map/ppermute | solution.py:258
  80.5 10.8 %collective-permute-start.15 = (bf16[288,128]{1,0:T(8,128)(2,1)S(1)}, bf16[288,128]{1,0:T(8,128)(2,1)S(1)}, u32[]{:S(2)}, u32[]{:S(2)}) collective-permute-start(bf16[288,128]{1,0:T(8,128)(2,1)S(1)} %add_convert_fusion.1), channel_id=1, source_target_pairs={{0,4},{1,5},{2,6},{3,7},{4,0},{5,1},{6,2},{7,3},{8,12},{9,13},{10,... | collective-permute-start | bytes 221192 | tf_op jit(solution)/shard_map/ppermute | solution.py:258
  85.5 6.4 %collective-permute-start.10 = (bf16[288,128]{1,0:T(8,128)(2,1)S(1)}, bf16[288,128]{1,0:T(8,128)(2,1)S(1)}, u32[]{:S(2)}, u32[]{:S(2)}) collective-permute-start(bf16[288,128]{1,0:T(8,128)(2,1)S(1)} %add_convert_fusion.3), channel_id=1, source_target_pairs={{0,8},{1,9},{2,10},{3,11},{4,12},{5,13},{6,14},{7,15},{8,0},{9,1},... | collective-permute-start | bytes 221192 | tf_op jit(solution)/shard_map/ppermute | solution.py:258
  92.0 5.2 %collective-permute-start.16 = (bf16[576,128]{1,0:T(8,128)(2,1)S(1)}, bf16[576,128]{1,0:T(8,128)(2,1)S(1)}, u32[]{:S(2)}, u32[]{:S(2)}) collective-permute-start(bf16[576,128]{1,0:T(8,128)(2,1)S(1)} %maximum_select_fusion.2), channel_id=1, source_target_pairs={{0,4},{1,5},{2,6},{3,7},{4,0},{5,1},{6,2},{7,3},{8,12},{9,13},{10,... | collective-permute-start | bytes 442376 | tf_op jit(solution)/shard_map/ppermute | solution.py:258
  92.3 5.2 %collective-permute-start.18 = (bf16[576,128]{1,0:T(8,128)(2,1)S(1)}, bf16[576,128]{1,0:T(8,128)(2,1)S(1)}, u32[]{:S(2)}, u32[]{:S(2)}) collective-permute-start(bf16[576,128]{1,0:T(8,128)(2,1)S(1)} %maximum_select_fusion.3), channel_id=1, source_target_pairs={{0,2},{1,3},{2,0},{3,1},{4,6},{5,7},{6,4},{7,5},{8,10},{9,11},{10,... | collective-permute-start | bytes 442376 | tf_op jit(solution)/shard_map/ppermute | solution.py:258
  97.3 1.6 %collective-permute-start.17 = (bf16[1152,128]{1,0:T(8,128)(2,1)S(1)}, bf16[1152,128]{1,0:T(8,128)(2,1)S(1)}, u32[]{:S(2)}, u32[]{:S(2)}) collective-permute-start(bf16[1152,128]{1,0:T(8,128)(2,1)S(1)} %maximum_select_fusion), channel_id=1, source_target_pairs={{0,1},{1,0},{2,3},{3,2},{4,5},{5,4},{6,7},{7,6},{8,9},{9,8},{10,11... | collective-permute-start | bytes 884744 | tf_op jit(solution)/shard_map/ppermute | solution.py:258
  97.6 1.8 %collective-permute-start.19 = (bf16[1152,128]{1,0:T(8,128)(2,1)S(1)}, bf16[1152,128]{1,0:T(8,128)(2,1)S(1)}, u32[]{:S(2)}, u32[]{:S(2)}) collective-permute-start(bf16[1152,128]{1,0:T(8,128)(2,1)S(1)} %maximum_select_fusion.1), channel_id=1, source_target_pairs={{0,1},{1,0},{2,3},{3,2},{4,5},{5,4},{6,7},{7,6},{8,9},{9,8},{10,11... | collective-permute-start | bytes 884744 | tf_op jit(solution)/shard_map/ppermute | solution.py:258

commit v7 on v5

--- a/solution.py
+++ b/solution.py
@@ -270,7 +270,7 @@
     orders = [rest[1:] + rest[:1], rest]
     for step in range(len(rest) - 1):
         values = between(step, values)
-        for j in range(2):
+        for j in (1, 0):
             bit = orders[j][step]
             side = (index // bit) % 2
             count = values[j].shape[0] // 2
@@ -285,7 +285,7 @@
         values[j] = (sent.astype(jnp.float32) + got.astype(jnp.float32)).astype(jnp.bfloat16)
     for step in reversed(range(len(rest) - 1)):
         values = between(2 * len(rest) - 2 - step, values)
-        for j in range(2):
+        for j in (1, 0):
             bit = orders[j][step]
             side = (index // bit) % 2
             got = swap(values[j], bit, size)

time: 103 us -> 102 us (level)
  waiting for transfers between devices: 26 us -> 24.3 us
  starting transfers between devices: 22.8 us -> 24.4 us
    ppermute x13, waiting for transfers between devices: 25.9 us -> 24.3 us  [swap(): return lax.ppermute(value, 'lat', [(i, i ^ bit) for i in range(size)])]
    ppermute x13, starting transfers between devices: 10.5 us -> 12.1 us  [swap(): return lax.ppermute(value, 'lat', [(i, i ^ bit) for i in range(size)])]
where the time goes in v7:
time: 102 us; the launch traced here: 103 us
  Pallas kernels  40 us (39%)
  starting transfers between devices  24.4 us (24%)
  waiting for transfers between devices  24.3 us (24%)
  other arithmetic  7.99 us (8%)
  local copies, waits for them, and re-layouts  4.9 us (5%)
    ppermute x13, waiting for transfers between devices, swap(): return lax.ppermute(value, 'lat', [(i, i ^ bit) for i in range(size)])  24.3 us
    pallas_call x2, Pallas kernels, forward(): pl.pallas_call(lambda *refs: fwd_kernel(last, *refs), grid=(1,), in_specs...  22.1 us
    pallas_call x1, Pallas kernels, backward(): pl.pallas_call(bwd_kernel, in_specs=[smem] + [pl.BlockSpec(memory_space=p...  17.9 us
    ppermute x13, starting transfers between devices, swap(): return lax.ppermute(value, 'lat', [(i, i ^ bit) for i in range(size)])  12.1 us
    ppermute x1, starting transfers between devices, per_device(): got_fast = lax.ppermute(edge_fast, 'lat', fast_pairs)  4.05 us
    convert_element_type x1, other arithmetic, between(): grad = grad.astype(jnp.bfloat16)  3.75 us
  transfers between devices with their start and end apart: 20, of which 10 were waited for; matrix products, arithmetic and copies ran while one was open for 10% of the time, Pallas kernels for 39%

profile of v7, /device:TPU:0, one launch (start us, length us, event | category | flops | bytes accessed | tf_op | source)
XLA Modules:
  0.0 102.5 jit_solution(4198616378674266090)
XLA Ops:
  0.6 0.0 copy-start
  0.6 0.0 copy-start.1
  0.7 0.0 copy-start.7
  0.7 1.9 %collective-permute-start.2 = (bf16[2,1440,256]{2,1,0:T(8,128)(2,1)}, bf16[2,1440,256]{2,1,0:T(8,128)(2,1)}, u32[]{:S(2)}, u32[]{:S(2)}) collective-permute-start(bf16[2,1440,256]{2,1,0:T(8,128)(2,1)} %refs_1_.3), channel_id=1, source_target_pairs={{3,4},{4,3},{7,8},{8,7},{11,12},{12,11},{19,20},{20,19},{23,24},{2... | collective-permute-start | bytes 4423688 | tf_op jit(solution)/shard_map/ppermute | solution.py:323
  2.6 0.5 collective-permute-start.3
  3.0 2.0 %slice.6 = bf16[2,1440,128]{2,1,0:T(8,128)(2,1)} slice(bf16[2,1440,256]{2,1,0:T(8,128)(2,1)} %refs_1_.3), slice={[0:2], [0:1440], [0:128]} | slice | bytes 1474560 | tf_op jit(solution)/shard_map/slice | solution.py:324
  5.1 1.5 %collective-permute-start.1 = (bf16[2,1440,128]{2,1,0:T(8,128)(2,1)}, bf16[2,1440,128]{2,1,0:T(8,128)(2,1)}, u32[]{:S(2)}, u32[]{:S(2)}) collective-permute-start(bf16[2,1440,128]{2,1,0:T(8,128)(2,1)} %slice.6), channel_id=1, source_target_pairs={{1,2},{2,1},{5,6},{6,5},{9,10},{10,9},{13,14},{14,13},{17,18},{18,... | collective-permute-start | bytes 2211848 | tf_op jit(solution)/shard_map/ppermute | solution.py:325
  6.6 0.9 slice.7
  7.5 1.5 %collective-permute-start = (bf16[2,1440,128]{2,1,0:T(8,128)(2,1)}, bf16[2,1440,128]{2,1,0:T(8,128)(2,1)}, u32[]{:S(2)}, u32[]{:S(2)}) collective-permute-start(bf16[2,1440,128]{2,1,0:T(8,128)(2,1)} %slice.7), channel_id=1, source_target_pairs={{1,2},{2,1},{5,6},{6,5},{9,10},{10,9},{13,14},{14,13},{17,18},{18,... | collective-permute-start | bytes 2211848 | tf_op jit(solution)/shard_map/ppermute | solution.py:327
  9.1 0.1 constant_dynamic-slice_fusion.1
  9.1 0.0 copy-start.2
  9.2 0.2 copy.12
  9.3 0.2 copy.13
  9.5 0.1 constant_dynamic-slice_fusion
  9.6 0.2 copy.14
  9.8 0.1 pad.23.clone
  9.9 0.7 maximum_maximum_fusion.table.refs_0_
  10.6 17.9 %backward.1 = (f32[2,1440,256]{2,1,0:T(8,128)}, bf16[2,1440,256]{2,1,0:T(8,128)(2,1)}, bf16[2,1440,256]{2,1,0:T(8,128)(2,1)}) custom-call(f32[2,9,10]{2,1,0:T(8,128)} %maximum_maximum_fusion.table.refs_0_, bf16[2,1440,256]{2,1,0:T(8,128)(2,1)} %refs_5_.3, bf16[9,256,256]{2,1,0:T(8,128)(2,1)} %refs_6_.3), custom_call_target="tpu_custom_call" | custom-call | tf_op jit(solution)/shard_map/backward/pallas_call | solution.py:228
  28.5 0.0 collective-permute-done.1.refs_2_
  28.5 0.0 collective-permute-done.2.refs_3_
  28.5 0.0 collective-permute-done.3.refs_4_
  28.6 10.6 %forward.2 = (f32[2,1440,256]{2,1,0:T(8,128)S(1)}, f32[9,128,128]{2,1,0:T(8,128)S(1)}, bf16[9,128,128]{2,1,0:T(8,128)(2,1)S(1)}) custom-call(f32[2,9,10]{2,1,0:T(8,128)S(1)} %copy-done.5, bf16[2,1440,256]{2,1,0:T(8,128)(2,1)S(1)} %copy-done.1, bf16[2,1440,128]{2,1,0:T(8,128)(2,1)} %collective-permute-done.1.refs_2_, ...), custom_call_target="tpu_custom_call" | custom-call | tf_op jit(solution)/shard_map/forward/pallas_call | solution.py:103
  39.2 1.9 %collective-permute-start.5 = (bf16[2,1440,256]{2,1,0:T(8,128)(2,1)}, bf16[2,1440,256]{2,1,0:T(8,128)(2,1)}, u32[]{:S(2)}, u32[]{:S(2)}) collective-permute-start(bf16[2,1440,256]{2,1,0:T(8,128)(2,1)} %get-tuple-element.45), channel_id=1, source_target_pairs={{3,4},{4,3},{7,8},{8,7},{11,12},{12,11},{19,20},{20,19},{23,24},{2... | collective-permute-start | bytes 4423688 | tf_op jit(solution)/shard_map/ppermute | solution.py:341
  41.1 4.0 %collective-permute-start.6 = (bf16[2,1440,256]{2,1,0:T(8,128)(2,1)}, bf16[2,1440,256]{2,1,0:T(8,128)(2,1)}, u32[]{:S(2)}, u32[]{:S(2)}) collective-permute-start(bf16[2,1440,256]{2,1,0:T(8,128)(2,1)} %get-tuple-element.47), channel_id=1, source_target_pairs={{0,1},{1,0},{2,3},{3,2},{4,5},{5,4},{6,7},{7,6},{8,9},{9,8},{10,11... | collective-permute-start | bytes 4423688 | tf_op jit(solution)/shard_map/ppermute | solution.py:343
  45.1 0.0 collective-permute-done.refs_2_
  45.1 11.5 %forward.3 = (bf16[2,1440,256]{2,1,0:T(8,128)(2,1)}, f32[18,128,128]{2,1,0:T(8,128)S(1)}, bf16[18,128,128]{2,1,0:T(8,128)(2,1)}) custom-call(f32[2,9,10]{2,1,0:T(8,128)S(1)} %copy-done.5, bf16[2,1440,256]{2,1,0:T(8,128)(2,1)S(1)} %copy-done.1, bf16[2,1440,128]{2,1,0:T(8,128)(2,1)} %collective-permute-done.refs_2_, ...), custom_call_target="tpu_custom_call" | custom-call | tf_op jit(solution)/shard_map/forward/pallas_call | solution.py:103
  56.6 1.0 copy-done.4
  57.6 0.1 collective-permute-start.4
  57.7 2.1 %collective-permute-done.4 = bf16[2304,128]{1,0:T(8,128)(2,1)S(1)} collective-permute-done((bf16[2304,128]{1,0:T(8,128)(2,1)}, bf16[2304,128]{1,0:T(8,128)(2,1)S(1)}, u32[]{:S(2)}, u32[]{:S(2)}) %collective-permute-start.4) | collective-permute-done | bytes 589856 | tf_op jit(solution)/shard_map/ppermute | solution.py:258
  59.8 1.4 %bitcast_add_fusion = f32[2304,128]{1,0:T(8,128)S(1)} fusion(f32[18,128,128]{2,1,0:T(8,128)} %copy-done.4, bf16[2304,128]{1,0:T(8,128)(2,1)S(1)} %collective-permute-done.4), kind=kLoop, calls=%fused_computation.2 | loop fusion | flops 589824 | bytes 2949120 | tf_op jit(solution)/shard_map/add | solution.py:266
  61.2 0.0 collective-permute-done.5
  61.2 0.0 collective-permute-done.6
  61.2 0.1 fusion
  61.3 1.4 %collective-permute-start.11 = (bf16[576,128]{1,0:T(8,128)(2,1)S(1)}, bf16[576,128]{1,0:T(8,128)(2,1)S(1)}, u32[]{:S(2)}, u32[]{:S(2)}) collective-permute-start(bf16[576,128]{1,0:T(8,128)(2,1)S(1)} %dynamic-slice_convert_fusion), channel_id=1, source_target_pairs={{0,2},{1,3},{2,0},{3,1},{4,6},{5,7},{6,4},{7,5},{8,10},{9,11},{10,... | collective-permute-start | bytes 442376 | tf_op jit(solution)/shard_map/ppermute | solution.py:258
  62.7 1.0 collective-permute-start.14
  63.7 0.7 collective-permute-start.7
  64.4 3.2 %collective-permute-done.11 = bf16[576,128]{1,0:T(8,128)(2,1)S(1)} collective-permute-done((bf16[576,128]{1,0:T(8,128)(2,1)S(1)}, bf16[576,128]{1,0:T(8,128)(2,1)S(1)}, u32[]{:S(2)}, u32[]{:S(2)}) %collective-permute-start.11) | collective-permute-done | bytes 147488 | tf_op jit(solution)/shard_map/ppermute | solution.py:258
  67.6 1.5 %collective-permute-start.12 = (bf16[288,128]{1,0:T(8,128)(2,1)S(1)}, bf16[288,128]{1,0:T(8,128)(2,1)S(1)}, u32[]{:S(2)}, u32[]{:S(2)}) collective-permute-start(bf16[288,128]{1,0:T(8,128)(2,1)S(1)} %dynamic-slice_convert_fusion.2), channel_id=1, source_target_pairs={{0,4},{1,5},{2,6},{3,7},{4,0},{5,1},{6,2},{7,3},{8,12},{9,13},{10,... | collective-permute-start | bytes 221192 | tf_op jit(solution)/shard_map/ppermute | solution.py:258
  69.1 0.4 collective-permute-done.7
  69.6 1.5 %collective-permute-start.8 = (bf16[288,128]{1,0:T(8,128)(2,1)S(1)}, bf16[288,128]{1,0:T(8,128)(2,1)S(1)}, u32[]{:S(2)}, u32[]{:S(2)}) collective-permute-start(bf16[288,128]{1,0:T(8,128)(2,1)S(1)} %dynamic-slice_convert_fusion.3), channel_id=1, source_target_pairs={{0,8},{1,9},{2,10},{3,11},{4,12},{5,13},{6,14},{7,15},{8,0},{9,1},... | collective-permute-start | bytes 221192 | tf_op jit(solution)/shard_map/ppermute | solution.py:258
  71.1 1.0 collective-permute-done.12
  72.1 1.9 %collective-permute-start.13 = (bf16[288,128]{1,0:T(8,128)(2,1)S(1)}, bf16[288,128]{1,0:T(8,128)(2,1)S(1)}, u32[]{:S(2)}, u32[]{:S(2)}) collective-permute-start(bf16[288,128]{1,0:T(8,128)(2,1)S(1)} %add_convert_fusion.2), channel_id=1, source_target_pairs={{0,8},{1,9},{2,10},{3,11},{4,12},{5,13},{6,14},{7,15},{8,0},{9,1},... | collective-permute-start | bytes 221192 | tf_op jit(solution)/shard_map/ppermute | solution.py:258
  74.0 4.4 %collective-permute-done.8 = bf16[288,128]{1,0:T(8,128)(2,1)S(1)} collective-permute-done((bf16[288,128]{1,0:T(8,128)(2,1)S(1)}, bf16[288,128]{1,0:T(8,128)(2,1)S(1)}, u32[]{:S(2)}, u32[]{:S(2)}) %collective-permute-start.8) | collective-permute-done | bytes 73760 | tf_op jit(solution)/shard_map/ppermute | solution.py:258
  78.5 1.5 %collective-permute-start.9 = (bf16[288,128]{1,0:T(8,128)(2,1)S(1)}, bf16[288,128]{1,0:T(8,128)(2,1)S(1)}, u32[]{:S(2)}, u32[]{:S(2)}) collective-permute-start(bf16[288,128]{1,0:T(8,128)(2,1)S(1)} %add_convert_fusion.4), channel_id=1, source_target_pairs={{0,2},{1,3},{2,0},{3,1},{4,6},{5,7},{6,4},{7,5},{8,10},{9,11},{10,... | collective-permute-start | bytes 221192 | tf_op jit(solution)/shard_map/ppermute | solution.py:258
  80.0 0.0 collective-permute-done.13
  80.1 0.0 collective-permute-done.14
  80.1 0.4 collective-permute-start.15
  80.5 5.4 %collective-permute-done.9 = bf16[288,128]{1,0:T(8,128)(2,1)S(1)} collective-permute-done((bf16[288,128]{1,0:T(8,128)(2,1)S(1)}, bf16[288,128]{1,0:T(8,128)(2,1)S(1)}, u32[]{:S(2)}, u32[]{:S(2)}) %collective-permute-start.9) | collective-permute-done | bytes 73760 | tf_op jit(solution)/shard_map/ppermute | solution.py:258
  85.9 1.7 %collective-permute-start.10 = (bf16[288,128]{1,0:T(8,128)(2,1)S(1)}, bf16[288,128]{1,0:T(8,128)(2,1)S(1)}, u32[]{:S(2)}, u32[]{:S(2)}) collective-permute-start(bf16[288,128]{1,0:T(8,128)(2,1)S(1)} %add_convert_fusion.3), channel_id=1, source_target_pairs={{0,8},{1,9},{2,10},{3,11},{4,12},{5,13},{6,14},{7,15},{8,0},{9,1},... | collective-permute-start | bytes 221192 | tf_op jit(solution)/shard_map/ppermute | solution.py:258
  87.7 0.0 copy-done.6
  87.7 3.7 %add_convert_fusion = bf16[2,1440,256]{2,1,0:T(8,128)(2,1)} fusion(bf16[2,1440,256]{2,1,0:T(8,128)(2,1)} %collective-permute-done.6, f32[2,1440,256]{2,1,0:T(8,128)S(1)} %copy-done.6, bf16[2,1440,256]{2,1,0:T(8,128)(2,1)S(1)} %collective-permute-done.14, bf16[2,1440,256]{2,1,0:T(8,128)(2,1)} %collective-permute-done.5), kind=kLoop, calls=%fused_computation | loop fusion | flops 5160960 | bytes 8847360 | tf_op jit(solution)/shard_map/convert_element_type | solution.py:366
  91.4 0.0 collective-permute-done.15
  91.5 1.4 %collective-permute-done.10 = bf16[288,128]{1,0:T(8,128)(2,1)S(1)} collective-permute-done((bf16[288,128]{1,0:T(8,128)(2,1)S(1)}, bf16[288,128]{1,0:T(8,128)(2,1)S(1)}, u32[]{:S(2)}, u32[]{:S(2)}) %collective-permute-start.10) | collective-permute-done | bytes 73760 | tf_op jit(solution)/shard_map/ppermute | solution.py:258
  92.9 0.1 collective-permute-start.16
  92.9 0.6 collective-permute-start.18
  93.6 5.1 %collective-permute-done.16 = bf16[576,128]{1,0:T(8,128)(2,1)S(1)} collective-permute-done((bf16[576,128]{1,0:T(8,128)(2,1)S(1)}, bf16[576,128]{1,0:T(8,128)(2,1)S(1)}, u32[]{:S(2)}, u32[]{:S(2)}) %collective-permute-start.16) | collective-permute-done | bytes 147488 | tf_op jit(solution)/shard_map/ppermute | solution.py:258
  98.6 0.1 maximum_select_fusion
  98.7 0.1 collective-permute-start.17
  98.8 0.0 collective-permute-done.18
  98.8 0.1 maximum_select_fusion.1
  98.9 0.5 collective-permute-start.19
  99.5 0.9 collective-permute-done.17
  100.4 0.4 collective-permute-done.19
  100.9 1.6 %convert_multiply_fusion = f32[9,256,256]{2,1,0:T(8,128)} fusion(bf16[9,128,128]{2,1,0:T(8,128)(2,1)S(1)} %bitcast.11, bf16[9,128,128]{2,1,0:T(8,128)(2,1)S(1)} %bitcast.10, bf16[9,128,128]{2,1,0:T(8,128)(2,1)S(1)} %bitcast.9, bf16[9,128,128]{2,1,0:T(8,128)(2,1)S(1)} %bitcast.8), kind=kLoop, calls=%fused_computation.1 | loop fusion | flops 5308416 | bytes 3538944 | tf_op jit(solution)/shard_map/mul | solution.py:372
  (28 shorter events, 0.4 us)
Async XLA Ops:
  0.6 8.9 %copy-start = (f32[32,9,3]{0,2,1:T(4,128)S(1)}, f32[32,9,3]{0,2,1:T(4,128)}, u32[]{:S(2)}) copy-start(f32[32,9,3]{0,2,1:T(4,128)} %param.11) | copy-start | bytes 10372
  0.6 6.0 %copy-start.1 = (bf16[2,1440,256]{2,1,0:T(8,128)(2,1)S(1)}, bf16[2,1440,256]{2,1,0:T(8,128)(2,1)}, u32[]{:S(2)}) copy-start(bf16[2,1440,256]{2,1,0:T(8,128)(2,1)} %refs_1_.3) | copy-start | bytes 4423684
  0.7 8.4 %copy-start.7 = (s32[32,9,3]{0,2,1:T(4,128)S(1)}, s32[32,9,3]{0,2,1:T(4,128)}, u32[]{:S(2)}) copy-start(s32[32,9,3]{0,2,1:T(4,128)} %param.10) | copy-start | bytes 10372
  0.7 8.4 %copy-start.8 = (s32[32,9,3]{0,2,1:T(4,128)S(1)}, s32[32,9,3]{0,2,1:T(4,128)}, u32[]{:S(2)}) copy-start(s32[32,9,3]{0,2,1:T(4,128)} %param.9) | copy-start | bytes 10372
  0.7 27.9 %collective-permute-start.2 = (bf16[2,1440,256]{2,1,0:T(8,128)(2,1)}, bf16[2,1440,256]{2,1,0:T(8,128)(2,1)}, u32[]{:S(2)}, u32[]{:S(2)}) collective-permute-start(bf16[2,1440,256]{2,1,0:T(8,128)(2,1)} %refs_1_.3), channel_id=1, source_target_pairs={{3,4},{4,3},{7,8},{8,7},{11,12},{12,11},{19,20},{20,19},{23,24},{2... | collective-permute-start | bytes 4423688 | tf_op jit(solution)/shard_map/ppermute | solution.py:323
  2.6 26.0 %collective-permute-start.3 = (bf16[2,1440,256]{2,1,0:T(8,128)(2,1)}, bf16[2,1440,256]{2,1,0:T(8,128)(2,1)}, u32[]{:S(2)}, u32[]{:S(2)}) collective-permute-start(bf16[2,1440,256]{2,1,0:T(8,128)(2,1)} %refs_1_.3), channel_id=1, source_target_pairs={{0,1},{1,0},{2,3},{3,2},{4,5},{5,4},{6,7},{7,6},{8,9},{9,8},{10,11... | collective-permute-start | bytes 4423688 | tf_op jit(solution)/shard_map/ppermute | solution.py:328
  5.1 23.5 %collective-permute-start.1 = (bf16[2,1440,128]{2,1,0:T(8,128)(2,1)}, bf16[2,1440,128]{2,1,0:T(8,128)(2,1)}, u32[]{:S(2)}, u32[]{:S(2)}) collective-permute-start(bf16[2,1440,128]{2,1,0:T(8,128)(2,1)} %slice.6), channel_id=1, source_target_pairs={{1,2},{2,1},{5,6},{6,5},{9,10},{10,9},{13,14},{14,13},{17,18},{18,... | collective-permute-start | bytes 2211848 | tf_op jit(solution)/shard_map/ppermute | solution.py:325
  7.5 37.6 %collective-permute-start = (bf16[2,1440,128]{2,1,0:T(8,128)(2,1)}, bf16[2,1440,128]{2,1,0:T(8,128)(2,1)}, u32[]{:S(2)}, u32[]{:S(2)}) collective-permute-start(bf16[2,1440,128]{2,1,0:T(8,128)(2,1)} %slice.7), channel_id=1, source_target_pairs={{1,2},{2,1},{5,6},{6,5},{9,10},{10,9},{13,14},{14,13},{17,18},{18,... | collective-permute-start | bytes 2211848 | tf_op jit(solution)/shard_map/ppermute | solution.py:327
  9.1 19.4 %copy-start.2 = (bf16[2,1440,256]{2,1,0:T(8,128)(2,1)S(1)}, bf16[2,1440,256]{2,1,0:T(8,128)(2,1)}, u32[]{:S(2)}) copy-start(bf16[2,1440,256]{2,1,0:T(8,128)(2,1)} %refs_5_.3) | copy-start | bytes 4423684
  9.8 18.8 %copy-start.3 = (bf16[9,256,256]{2,1,0:T(8,128)(2,1)S(1)}, bf16[9,256,256]{2,1,0:T(8,128)(2,1)}, u32[]{:S(2)}) copy-start(bf16[9,256,256]{2,1,0:T(8,128)(2,1)} %refs_6_.3) | copy-start | bytes 3538948
  10.6 18.0 %copy-start.5 = (f32[2,9,10]{2,1,0:T(8,128)S(1)}, f32[2,9,10]{2,1,0:T(8,128)}, u32[]{:S(2)}) copy-start(f32[2,9,10]{2,1,0:T(8,128)} %maximum_maximum_fusion.table.refs_0_) | copy-start | bytes 2164
  39.2 22.0 %collective-permute-start.5 = (bf16[2,1440,256]{2,1,0:T(8,128)(2,1)}, bf16[2,1440,256]{2,1,0:T(8,128)(2,1)}, u32[]{:S(2)}, u32[]{:S(2)}) collective-permute-start(bf16[2,1440,256]{2,1,0:T(8,128)(2,1)} %get-tuple-element.45), channel_id=1, source_target_pairs={{3,4},{4,3},{7,8},{8,7},{11,12},{12,11},{19,20},{20,19},{23,24},{2... | collective-permute-start | bytes 4423688 | tf_op jit(solution)/shard_map/ppermute | solution.py:341
  41.1 20.1 %collective-permute-start.6 = (bf16[2,1440,256]{2,1,0:T(8,128)(2,1)}, bf16[2,1440,256]{2,1,0:T(8,128)(2,1)}, u32[]{:S(2)}, u32[]{:S(2)}) collective-permute-start(bf16[2,1440,256]{2,1,0:T(8,128)(2,1)} %get-tuple-element.47), channel_id=1, source_target_pairs={{0,1},{1,0},{2,3},{3,2},{4,5},{5,4},{6,7},{7,6},{8,9},{9,8},{10,11... | collective-permute-start | bytes 4423688 | tf_op jit(solution)/shard_map/ppermute | solution.py:343
  56.6 1.0 copy-start.4
  57.6 2.2 %collective-permute-start.4 = (bf16[2304,128]{1,0:T(8,128)(2,1)}, bf16[2304,128]{1,0:T(8,128)(2,1)S(1)}, u32[]{:S(2)}, u32[]{:S(2)}) collective-permute-start(bf16[2304,128]{1,0:T(8,128)(2,1)} %bitcast.1), channel_id=1, source_target_pairs={{0,1},{1,0},{2,3},{3,2},{4,5},{5,4},{6,7},{7,6},{8,9},{9,8},{10,11... | collective-permute-start | bytes 1769480 | tf_op jit(solution)/shard_map/ppermute | solution.py:258
  61.3 6.2 %collective-permute-start.11 = (bf16[576,128]{1,0:T(8,128)(2,1)S(1)}, bf16[576,128]{1,0:T(8,128)(2,1)S(1)}, u32[]{:S(2)}, u32[]{:S(2)}) collective-permute-start(bf16[576,128]{1,0:T(8,128)(2,1)S(1)} %dynamic-slice_convert_fusion), channel_id=1, source_target_pairs={{0,2},{1,3},{2,0},{3,1},{4,6},{5,7},{6,4},{7,5},{8,10},{9,11},{10,... | collective-permute-start | bytes 442376 | tf_op jit(solution)/shard_map/ppermute | solution.py:258
  62.7 17.4 %collective-permute-start.14 = (bf16[2,1440,256]{2,1,0:T(8,128)(2,1)}, bf16[2,1440,256]{2,1,0:T(8,128)(2,1)S(1)}, u32[]{:S(2)}, u32[]{:S(2)}) collective-permute-start(bf16[2,1440,256]{2,1,0:T(8,128)(2,1)} %get-tuple-element.45), channel_id=1, source_target_pairs={{1,2},{2,1},{5,6},{6,5},{9,10},{10,9},{13,14},{14,13},{17,18},{18,... | collective-permute-start | bytes 4423688 | tf_op jit(solution)/shard_map/ppermute | solution.py:342
  63.7 24.0 %copy-start.6 = (f32[2,1440,256]{2,1,0:T(8,128)S(1)}, f32[2,1440,256]{2,1,0:T(8,128)}, u32[]{:S(2)}) copy-start(f32[2,1440,256]{2,1,0:T(8,128)} %get-tuple-element.50) | copy-start | bytes 8847364
  63.7 5.8 %collective-permute-start.7 = (bf16[576,128]{1,0:T(8,128)(2,1)S(1)}, bf16[576,128]{1,0:T(8,128)(2,1)S(1)}, u32[]{:S(2)}, u32[]{:S(2)}) collective-permute-start(bf16[576,128]{1,0:T(8,128)(2,1)S(1)} %dynamic-slice_convert_fusion.1), channel_id=1, source_target_pairs={{0,4},{1,5},{2,6},{3,7},{4,0},{5,1},{6,2},{7,3},{8,12},{9,13},{10,... | collective-permute-start | bytes 442376 | tf_op jit(solution)/shard_map/ppermute | solution.py:258
  67.6 4.5 %collective-permute-start.12 = (bf16[288,128]{1,0:T(8,128)(2,1)S(1)}, bf16[288,128]{1,0:T(8,128)(2,1)S(1)}, u32[]{:S(2)}, u32[]{:S(2)}) collective-permute-start(bf16[288,128]{1,0:T(8,128)(2,1)S(1)} %dynamic-slice_convert_fusion.2), channel_id=1, source_target_pairs={{0,4},{1,5},{2,6},{3,7},{4,0},{5,1},{6,2},{7,3},{8,12},{9,13},{10,... | collective-permute-start | bytes 221192 | tf_op jit(solution)/shard_map/ppermute | solution.py:258
  69.6 8.9 %collective-permute-start.8 = (bf16[288,128]{1,0:T(8,128)(2,1)S(1)}, bf16[288,128]{1,0:T(8,128)(2,1)S(1)}, u32[]{:S(2)}, u32[]{:S(2)}) collective-permute-start(bf16[288,128]{1,0:T(8,128)(2,1)S(1)} %dynamic-slice_convert_fusion.3), channel_id=1, source_target_pairs={{0,8},{1,9},{2,10},{3,11},{4,12},{5,13},{6,14},{7,15},{8,0},{9,1},... | collective-permute-start | bytes 221192 | tf_op jit(solution)/shard_map/ppermute | solution.py:258
  72.1 7.9 %collective-permute-start.13 = (bf16[288,128]{1,0:T(8,128)(2,1)S(1)}, bf16[288,128]{1,0:T(8,128)(2,1)S(1)}, u32[]{:S(2)}, u32[]{:S(2)}) collective-permute-start(bf16[288,128]{1,0:T(8,128)(2,1)S(1)} %add_convert_fusion.2), channel_id=1, source_target_pairs={{0,8},{1,9},{2,10},{3,11},{4,12},{5,13},{6,14},{7,15},{8,0},{9,1},... | collective-permute-start | bytes 221192 | tf_op jit(solution)/shard_map/ppermute | solution.py:258
  78.5 7.4 %collective-permute-start.9 = (bf16[288,128]{1,0:T(8,128)(2,1)S(1)}, bf16[288,128]{1,0:T(8,128)(2,1)S(1)}, u32[]{:S(2)}, u32[]{:S(2)}) collective-permute-start(bf16[288,128]{1,0:T(8,128)(2,1)S(1)} %add_convert_fusion.4), channel_id=1, source_target_pairs={{0,2},{1,3},{2,0},{3,1},{4,6},{5,7},{6,4},{7,5},{8,10},{9,11},{10,... | collective-permute-start | bytes 221192 | tf_op jit(solution)/shard_map/ppermute | solution.py:258
  80.1 11.3 %collective-permute-start.15 = (bf16[288,128]{1,0:T(8,128)(2,1)S(1)}, bf16[288,128]{1,0:T(8,128)(2,1)S(1)}, u32[]{:S(2)}, u32[]{:S(2)}) collective-permute-start(bf16[288,128]{1,0:T(8,128)(2,1)S(1)} %add_convert_fusion.1), channel_id=1, source_target_pairs={{0,4},{1,5},{2,6},{3,7},{4,0},{5,1},{6,2},{7,3},{8,12},{9,13},{10,... | collective-permute-start | bytes 221192 | tf_op jit(solution)/shard_map/ppermute | solution.py:258
  85.9 6.9 %collective-permute-start.10 = (bf16[288,128]{1,0:T(8,128)(2,1)S(1)}, bf16[288,128]{1,0:T(8,128)(2,1)S(1)}, u32[]{:S(2)}, u32[]{:S(2)}) collective-permute-start(bf16[288,128]{1,0:T(8,128)(2,1)S(1)} %add_convert_fusion.3), channel_id=1, source_target_pairs={{0,8},{1,9},{2,10},{3,11},{4,12},{5,13},{6,14},{7,15},{8,0},{9,1},... | collective-permute-start | bytes 221192 | tf_op jit(solution)/shard_map/ppermute | solution.py:258
  92.9 5.8 %collective-permute-start.16 = (bf16[576,128]{1,0:T(8,128)(2,1)S(1)}, bf16[576,128]{1,0:T(8,128)(2,1)S(1)}, u32[]{:S(2)}, u32[]{:S(2)}) collective-permute-start(bf16[576,128]{1,0:T(8,128)(2,1)S(1)} %maximum_select_fusion.2), channel_id=1, source_target_pairs={{0,4},{1,5},{2,6},{3,7},{4,0},{5,1},{6,2},{7,3},{8,12},{9,13},{10,... | collective-permute-start | bytes 442376 | tf_op jit(solution)/shard_map/ppermute | solution.py:258
  92.9 5.9 %collective-permute-start.18 = (bf16[576,128]{1,0:T(8,128)(2,1)S(1)}, bf16[576,128]{1,0:T(8,128)(2,1)S(1)}, u32[]{:S(2)}, u32[]{:S(2)}) collective-permute-start(bf16[576,128]{1,0:T(8,128)(2,1)S(1)} %maximum_select_fusion.3), channel_id=1, source_target_pairs={{0,2},{1,3},{2,0},{3,1},{4,6},{5,7},{6,4},{7,5},{8,10},{9,11},{10,... | collective-permute-start | bytes 442376 | tf_op jit(solution)/shard_map/ppermute | solution.py:258
  98.7 1.6 %collective-permute-start.17 = (bf16[1152,128]{1,0:T(8,128)(2,1)S(1)}, bf16[1152,128]{1,0:T(8,128)(2,1)S(1)}, u32[]{:S(2)}, u32[]{:S(2)}) collective-permute-start(bf16[1152,128]{1,0:T(8,128)(2,1)S(1)} %maximum_select_fusion), channel_id=1, source_target_pairs={{0,1},{1,0},{2,3},{3,2},{4,5},{5,4},{6,7},{7,6},{8,9},{9,8},{10,11... | collective-permute-start | bytes 884744 | tf_op jit(solution)/shard_map/ppermute | solution.py:258
  98.9 1.9 %collective-permute-start.19 = (bf16[1152,128]{1,0:T(8,128)(2,1)S(1)}, bf16[1152,128]{1,0:T(8,128)(2,1)S(1)}, u32[]{:S(2)}, u32[]{:S(2)}) collective-permute-start(bf16[1152,128]{1,0:T(8,128)(2,1)S(1)} %maximum_select_fusion.1), channel_id=1, source_target_pairs={{0,1},{1,0},{2,3},{3,2},{4,5},{5,4},{6,7},{7,6},{8,9},{9,8},{10,11... | collective-permute-start | bytes 884744 | tf_op jit(solution)/shard_map/ppermute | solution.py:258
